TPU v7x, 32 devices: a whole 2x2x4 slice. The times are simulated.
32 devices in a mesh: grp: 4 (over z), wide: 8 (over y, x, core).
Axes of the slice: x: 2, y: 2, z: 4, core: 2. Of those that a mesh axis runs over, the one named last changes fastest.
Arguments:
- coeff_in: float32 [2336, 512], P(('grp', 'wide')), may hold values from -6 to 6
- coupling: float32 [2048, 64, 64], P(('grp', 'wide')), may hold values from -0.5 to 0.5
- source: int32 [2048], P(('grp', 'wide')), may hold values from 0 to 291, as said below
- target: int32 [2048], P(('grp', 'wide')), may hold values from 0 to 72, as said below
- counts: int32 [256], P(('grp', 'wide')), may hold values from 1 to 8, as said below
- transfer: float32 [2304, 64, 64], P(('grp', 'wide')), may hold values from -0.75 to 0.75
- basis: float32 [2048, 64, 128], P(('grp', 'wide')), may hold values from -0.75 to 0.75
Outputs:
- product: float32 [8, 262144], P(None, ('grp', 'wide'))
Inputs may be any that keep to these rules, and one draw needn't show every extreme that they name: source names a cluster of the same level as the block's target: member v // 73 of the block's group, local number v % 73. target is the local number of a cluster at the owner. `counts`: in every draw, for each index of grp one index of wide receives 8 live blocks from every device.
All inputs are finite; a program needn't handle non-finite values.
Results may differ from a plain program's by a relative error of at most 0.00007.
Values sent between devices are 32-bit elements; how exact they have to be, the bound alone decides.
No kernel may reach another device: no remote copies, remote signals or barrier semaphores. Data moves between devices by JAX's collectives and lax.ppermute only.
A program may use at most 64 MiB of HBM per device.

v0:
```python
import jax
import jax.numpy as jnp
from jax import lax
from jax.sharding import PartitionSpec as P

BRANCH = 8


def on_device(coeff_in, coupling, source, target, counts, transfer, basis):
    nwide = lax.axis_size("wide")
    nblocks = coupling.shape[0]
    slots = nblocks // nwide
    ncl = coeff_in.shape[0]
    rank = coupling.shape[1]
    width = coeff_in.shape[1]
    table = lax.all_gather(coeff_in, "grp", axis=0, tiled=True)
    picked = table[source].reshape(nblocks, rank, width // rank)
    partial_value = jnp.einsum(
        "bij,bjr->bir", coupling, picked, precision=lax.Precision.HIGHEST
    ).reshape(nblocks, width)
    position = jnp.arange(nblocks, dtype=jnp.int32)
    peer = position // slots
    live = position % slots < counts[peer]
    partial_value = jnp.where(live[:, None], partial_value, jnp.zeros_like(partial_value))
    owner_row = peer * ncl + target
    summed = jax.ops.segment_sum(partial_value, owner_row, num_segments=nwide * ncl)
    arrived = lax.all_to_all(summed, "wide", split_axis=0, concat_axis=0, tiled=True)
    coeff = jnp.sum(arrived.reshape(nwide, ncl, width), axis=0)
    coeff = coeff.reshape(ncl, rank, width // rank)
    branch = BRANCH
    top = coeff[0]
    middle = coeff[1 : 1 + branch] + jnp.einsum(
        "cij,jr->cir", transfer[:branch], top, precision=lax.Precision.HIGHEST
    )
    parent = jnp.repeat(middle, branch, axis=0)
    leaves = coeff[1 + branch :] + jnp.einsum(
        "cij,cjr->cir", transfer[branch:], parent, precision=lax.Precision.HIGHEST
    )
    result = jnp.einsum("ckr,ckp->rcp", leaves, basis, precision=lax.Precision.HIGHEST)
    return result.reshape(result.shape[0], result.shape[1] * result.shape[2])


def solution(mesh):
    placed = (
        P(("grp", "wide"), None),
        P(("grp", "wide"), None, None),
        P(("grp", "wide")),
        P(("grp", "wide")),
        P(("grp", "wide")),
        P(("grp", "wide"), None, None),
        P(("grp", "wide"), None, None),
    )
    return jax.shard_map(
        on_device, mesh=mesh, in_specs=placed, out_specs=P(None, ("grp", "wide")), check_vma=False
    )
```

profile of v0, /device:TPU:0, one launch (start us, length us, event | category | flops | bytes accessed | tf_op | source)
XLA Modules:
  0.0 71.7 jit_solution(9447556839759781216)
XLA Ops:
  0.0 0.0 copy-start
  0.0 0.8 %compare_select_fusion = s32[64]{0:T(128)S(1)} fusion(s32[64]{0:T(128)} %param.9), kind=kLoop, calls=%fused_computation.13 | loop fusion | flops 192 | bytes 512 | tf_op jit(solution)/shard_map/select_n | solution.py:17
  0.8 0.7 fusion.7
  1.5 1.6 %fusion.9 = (s32[1]{0:T(128)}, s32[1]{0:T(128)}, s32[1]{0:T(128)}, s32[1]{0:T(128)}, s32[1]{0:T(128)}, /*index=5*/s32[1]{0:T(128)}, s32[1]{0:T(128)}, s32[1]{0:T(128)}) fusion(s32[8]{0:T(128)} %param.11), kind=kLoop, calls=%fused_computation.36 | loop fusion | bytes 64 | tf_op jit(solution)/shard_map/gather | solution.py:23
  3.1 19.8 %all-gather = f32[4,73,512]{2,1,0:T(8,128)S(1)} all-gather(f32[1,73,512]{2,1,0:T(8,128)} %bitcast.53), channel_id=1, replica_groups=mesh['grp'=4,'wide'=8] {'grp'}, dimensions={0}, use_global_device_ids=true | all-gather | bytes 747520 | tf_op jit(solution)/shard_map/all_gather | solution.py:16
  22.9 0.1 reshape.135
  23.0 0.7 gather_fusion
  23.7 0.1 copy.30
  23.8 0.2 copy.31
  24.0 4.9 %convolution_bitcast_fusion.2 = f32[64,64,8]{1,2,0:T(8,128)S(1)} fusion(f32[64,64,8]{1,2,0:T(8,128)S(1)} %copy.31, f32[64,64,64]{2,1,0:T(8,128)} %param.8), kind=kOutput, calls=%fused_computation.5 | convolution fusion | flops 25165824 | bytes 1310720 | tf_op jit(solution)/shard_map/bij,bjr->bir/dot_general | solution.py:18
  28.9 0.2 copy.32
  29.1 5.0 %fusion.5 = pred[64]{0:T(512)(128)(4,1)S(1)} fusion(s32[]{:T(128)} %bitcast.2, s32[]{:T(128)} %bitcast.3, s32[]{:T(128)} %bitcast.4, s32[]{:T(128)} %bitcast.5, s32[]{:T(128)} %bitcast.6, s32[]{:T(128)} %bitcast.8, s32[]{:T(128)} %bitcast.7, s32[]{:T(128)} %bitcast.1), kind=kLoop, calls=%fused_computation.32 | loop fusion | flops 2048 | bytes 96 | tf_op jit(solution)/shard_map/lt | solution.py:23
  34.1 0.1 copy.33
  34.2 1.2 %scatter_custom_fusion = f32[584,512]{1,0:T(8,128)S(1)} fusion(s32[64]{0:T(128)S(1)} %fusion.7, f32[64,512]{1,0:T(8,128)S(1)} %copy.33, f32[]{:T(128)} %constant.34.clone.1), kind=kCustom, calls=%fused_computation.8 | custom fusion | flops 32768 | bytes 1196036 | tf_op jit(solution)/shard_map/scatter-add | solution.py:26
  35.5 1.2 %all_to_all.6 = f32[8,73,512]{2,1,0:T(8,128)} reshape(f32[584,512]{1,0:T(8,128)S(1)} %scatter_custom_fusion) | data formatting | bytes 2392064 | tf_op jit(solution)/shard_map/all_to_all | solution.py:27
  36.7 3.7 %all-to-all-start = ((f32[8,73,512]{2,1,0:T(8,128)}), f32[8,73,512]{2,1,0:T(8,128)S(1)}, u32[]{:S(2)}, u32[]{:S(2)}) async-start(f32[8,73,512]{2,1,0:T(8,128)} %all_to_all.6), calls=%async_computation | async-start | bytes 2621440 | tf_op jit(solution)/shard_map/all_to_all | solution.py:27
  40.4 3.5 %slice.28 = f32[64,64,64]{0,2,1:T(8,128)} slice(f32[72,64,64]{0,2,1:T(8,128)} %param.12), slice={[8:72], [0:64], [0:64]} | slice | bytes 2097152 | tf_op jit(solution)/shard_map/slice | solution.py:37
  43.9 2.9 %copy.42 = f32[8,64,64]{2,1,0:T(8,128)} copy(f32[8,64,64]{0,2,1:T(8,128)} %bitcast.49) | data formatting | bytes 262144
  46.8 3.8 %copy.43 = f32[64,64,64]{2,1,0:T(8,128)} copy(f32[64,64,64]{0,2,1:T(8,128)} %slice.28) | data formatting | bytes 2097152
  50.6 8.0 %all-to-all-done = f32[8,73,512]{2,1,0:T(8,128)S(1)} async-done(((f32[8,73,512]{2,1,0:T(8,128)}), f32[8,73,512]{2,1,0:T(8,128)S(1)}, u32[]{:S(2)}, u32[]{:S(2)}) %all-to-all-start) | async-done | bytes 1196064 | tf_op jit(solution)/shard_map/all_to_all | solution.py:27
  58.6 0.8 %reduce_sum.9 = f32[73,512]{1,0:T(8,128)} reduce(f32[8,73,512]{2,1,0:T(8,128)S(1)} %all-to-all-done, f32[]{:T(128)} %constant.34.clone.1), dimensions={0}, to_apply=%region_1.2 | reduce | flops 261632 | bytes 1345540 | tf_op jit(solution)/shard_map/reduce_sum | solution.py:28
  59.4 0.7 %slice_reduce_fusion = f32[512]{0:T(512)S(1)} fusion(f32[73,512]{1,0:T(8,128)} %reduce_sum.9), kind=kLoop, calls=%fused_computation.15 | loop fusion | bytes 4096 | tf_op jit(solution)/shard_map/slice | solution.py:31
  60.1 0.8 %slice.41 = f32[8,512]{1,0:T(8,128)S(1)} slice(f32[73,512]{1,0:T(8,128)} %reduce_sum.9), slice={[1:9], [0:512]} | slice | bytes 32768 | tf_op jit(solution)/shard_map/slice | solution.py:32
  60.9 0.9 %slice.40 = f32[64,512]{1,0:T(8,128)S(1)} slice(f32[73,512]{1,0:T(8,128)} %reduce_sum.9), slice={[9:73], [0:512]} | slice | bytes 262144 | tf_op jit(solution)/shard_map/slice | solution.py:36
  61.8 0.1 squeeze.3
  61.9 0.1 copy.34
  62.0 0.2 copy.39
  62.2 0.2 slice.25
  62.4 0.1 copy.37
  62.5 1.7 %fusion.1 = f32[8,64,8]{1,2,0:T(8,128)S(1)} fusion(f32[8,64,8]{1,2,0:T(8,128)S(1)} %copy.37, f32[8,64,64]{2,1,0:T(8,128)} %copy.42, f32[64,8]{1,0:T(8,128)S(1)} %squeeze.3), kind=kOutput, calls=%fused_computation.7 | convolution fusion | flops 3149824 | bytes 165888 | tf_op jit(solution)/shard_map/cij,jr->cir/dot_general | solution.py:32
  64.2 4.9 %fusion = f32[64,64,8]{1,2,0:T(8,128)S(1)} fusion(f32[64,64,8]{1,2,0:T(8,128)S(1)} %copy.39, f32[64,64,8]{1,2,0:T(8,128)S(1)} %bitcast.52, f32[64,64,64]{2,1,0:T(8,128)} %copy.43), kind=kOutput, calls=%fused_computation.4 | convolution fusion | flops 25198592 | bytes 1441792 | tf_op jit(solution)/shard_map/cij,cjr->cir/dot_general | solution.py:36
  69.2 0.0 copy-done
  69.2 2.6 %convolution_bitcast_fusion = f32[8,8192]{1,0:T(8,128)} fusion(f32[64,64,8]{1,2,0:T(8,128)S(1)} %fusion, f32[64,64,128]{2,1,0:T(8,128)S(1)} %copy-done), kind=kOutput, calls=%fused_computation.2 | convolution fusion | flops 50331648 | bytes 2490368 | tf_op jit(solution)/shard_map/ckr,ckp->rcp/dot_general | solution.py:39
  (3 shorter events, 0.1 us)
Async XLA Ops:
  0.0 69.2 %copy-start = (f32[64,64,128]{2,1,0:T(8,128)S(1)}, f32[64,64,128]{2,1,0:T(8,128)}, u32[]{:S(2)}) copy-start(f32[64,64,128]{2,1,0:T(8,128)} %param.13) | copy-start | bytes 6291460
  36.7 21.9 %all-to-all-start = ((f32[8,73,512]{2,1,0:T(8,128)}), f32[8,73,512]{2,1,0:T(8,128)S(1)}, u32[]{:S(2)}, u32[]{:S(2)}) async-start(f32[8,73,512]{2,1,0:T(8,128)} %all_to_all.6), calls=%async_computation | async-start | bytes 2621440 | tf_op jit(solution)/shard_map/all_to_all | solution.py:27
where the time goes:
time: 72.4 us; the launch traced here: 71.7 us
  blocking collectives  19.8 us (27%)
  local copies, waits for them, and re-layouts  17.5 us (24%)
  matrix products  14.1 us (19%)
  other arithmetic  8.46 us (12%)
  waiting for transfers between devices  8.04 us (11%)
  starting transfers between devices  3.72 us (5%)
    all_gather x1, blocking collectives, on_device(): table = lax.all_gather(coeff_in, 'grp', axis=0, tiled=True)  19.8 us
    all_to_all x1, waiting for transfers between devices, on_device(): lax.all_to_all(summed, 'wide', split_axis=0, concat_axis=0, tiled=True)  8.04 us
    unnamed x5, local copies, waits for them, and re-layouts  6.78 us
    lt x1, other arithmetic, on_device(): live = position % slots < counts[peer]  4.95 us
    dot_general x1, matrix products, on_device(): jnp.einsum('cij,cjr->cir', transfer[branch:], parent, precision=lax.Preci...  4.94 us
    dot_general x1, matrix products, on_device(): jnp.einsum('bij,bjr->bir', coupling, picked, precision=lax.Precision.HIGH...  4.94 us
    all_to_all x1, starting transfers between devices, on_device(): lax.all_to_all(summed, 'wide', split_axis=0, concat_axis=0, tiled=True)  3.72 us
    slice x1, local copies, waits for them, and re-layouts, on_device(): transfer[branch:]  3.49 us
  transfers between devices with their start and end apart: 1, of which 1 were waited for; matrix products, arithmetic and copies ran while one was open for 14% of the time, Pallas kernels for 0%

commit v1 on v0

v1 whole, which is shorter than its diff:
```python
import functools

import jax
import jax.numpy as jnp
from jax import lax
from jax.experimental import pallas as pl
from jax.experimental.pallas import tpu as pltpu
from jax.sharding import PartitionSpec as P

BRANCH = 8
RANK = 64
RHS = 8
SLOTS = 8
HALF = 4
BF = jnp.bfloat16
F32 = jnp.float32


def split(x):
    high = x.astype(BF)
    low = (x - high.astype(F32)).astype(BF)
    return high, low


def mm(a, b):
    return jnp.dot(a, b, preferred_element_type=F32)


def product3(x, high_ref_value, low_ref_value):
    rows = x.shape[0]
    high, low = split(x)
    both = mm(jnp.concatenate([high, low], axis=0), high_ref_value)
    return both[:rows] + both[rows:] + mm(high, low_ref_value)


def iota(shape, dim):
    return lax.broadcasted_iota(jnp.int32, shape, dim)


def prepare(target, counts, coupling, transfer, basis, ct_h, ct_l, t_h, t_l, b_h, b_l, code):
    nwide = code.shape[0]

    def per_peer(p, carry):
        for s in range(HALF):
            pair = jnp.concatenate([coupling[SLOTS * p + s], coupling[SLOTS * p + HALF + s]], axis=0)
            high, low = split(pair.T)
            ct_h[p, RANK * s : RANK * (s + 1), :] = high
            ct_l[p, RANK * s : RANK * (s + 1), :] = low
        row, lane = iota((8, 128), 0), iota((8, 128), 1)
        value = jnp.zeros((8, 128), jnp.int32)
        for slot in range(SLOTS):
            here = (row == slot // HALF) & ((lane % 32) // RHS == slot % HALF)
            at = jnp.where(slot < counts[p], target[SLOTS * p + slot] * RHS, -RHS)
            value = jnp.where(here, at + lane % RHS, value)
        code[p] = value.astype(F32)
        return carry

    lax.fori_loop(0, nwide, per_peer, 0)
    for g in range(1 + BRANCH):
        block = transfer[BRANCH * g : BRANCH * (g + 1)].reshape(BRANCH * RANK, RANK)
        high, low = split(block.T)
        t_h[RANK * g : RANK * (g + 1), :] = high
        t_l[RANK * g : RANK * (g + 1), :] = low

    def per_group(g, carry):
        rows = pl.ds(pl.multiple_of(g * 256, 256), 256)
        high, low = split(basis[rows, :])
        b_h[rows, :] = high
        b_l[rows, :] = low
        return carry

    lax.fori_loop(0, basis.shape[0] // 256, per_group, 0)


def couple(ntab, idx, *refs):
    tables, (ct_h, ct_l, code, out, held, sems) = refs[:ntab], refs[ntab:]
    nwide = out.shape[0]
    copies = [pltpu.make_async_copy(tables[k], held.at[k], sems.at[k]) for k in range(ntab)]
    for copy in copies:
        copy.start()
    width = RANK * RHS
    gather = jnp.where(iota((width, 256), 0) // RHS == iota((width, 256), 1) % RANK, 1.0, 0.0).astype(BF)
    mine = iota((RHS, width), 0) == iota((RHS, width), 1) % RHS
    diagonal = (iota((64, 256), 0) // RHS) % HALF == iota((64, 256), 1) // RANK
    left = iota((32, 128), 1) < RANK
    for copy in copies:
        copy.wait()
    for p in range(nwide):
        picked = []
        for slot in range(SLOTS):
            at = idx[SLOTS * p + slot]
            row = held[at // 128, pl.ds(at % 128, 1), :]
            picked.append(jnp.where(mine, jnp.broadcast_to(row, (RHS, width)), 0.0))
        high, low = split(jnp.concatenate(picked, axis=0))
        x = mm(jnp.concatenate([high, low], axis=0), gather)
        x = jnp.where(diagonal, x[:64] + x[64:], 0.0)
        z = product3(x, ct_h[p], ct_l[p])
        out[p, :32, :] = jnp.where(left, z[:32], z[32:])
        out[p, 32:, :] = code[p]


def downward(arrived, t_h, t_l, b_h, b_l, out, full):
    nwide = arrived.shape[0]
    ncl = full.shape[0] // RHS
    value = jnp.concatenate([arrived[p, :32, :] for p in range(nwide)], axis=0)
    high, low = split(value)
    weights = jnp.concatenate([high, low], axis=1)
    lane = iota((1, 128), 1)
    codes = []
    for h in range(2):
        parts = []
        for q in range(nwide // 4):
            part = arrived[4 * q, 32 + h : 33 + h, :]
            for e in range(1, 4):
                part = jnp.where(lane // 32 == e, arrived[4 * q + e, 32 + h : 33 + h, :], part)
            parts.append(part)
        codes.append(jnp.concatenate(parts, axis=1).astype(jnp.int32))
    total = full.shape[0]
    step = 80
    for at in range(0, total, step):
        rows = min(step, total - at)
        sums = []
        for h in range(2):
            place = iota((rows, 32 * nwide), 0) + at
            hot = jnp.where(place == codes[h], 1.0, 0.0).astype(BF)
            r = mm(hot, weights)
            sums.append(r[:, :128] + r[:, 128:])
        s = jnp.where(iota((rows, 128), 1) < RANK, sums[0], sums[1])
        full[at : at + rows, :] = s + pltpu.roll(s, RANK, 1)

    first = iota((RHS, 128), 1) < RANK

    def pairs(cluster, count):
        parts = []
        for i in range(0, count, 2):
            a = full[RHS * (cluster + i) : RHS * (cluster + i + 1), :]
            b = full[RHS * (cluster + i + 1) : RHS * (cluster + i + 2), :]
            parts.append(jnp.where(first, a, b))
        return jnp.concatenate(parts, axis=1)

    diagonal = iota((32, 256), 0) // RHS == iota((32, 256), 1) // RANK

    def spread(x):
        return jnp.where(diagonal, jnp.concatenate([x] * 4, axis=0), 0.0)

    top = full[:RHS, :RANK]
    middle = pairs(1, BRANCH) + product3(top, t_h[:RANK, :], t_l[:RANK, :])
    for g in range(2):
        at = slice(RANK + 256 * g, RANK + 256 * (g + 1))
        down = product3(spread(middle[:, 256 * g : 256 * (g + 1)]), t_h[at, :], t_l[at, :])
        for c4 in range(4):
            c = 4 * g + c4
            leaves = pairs(1 + BRANCH + BRANCH * c, BRANCH) + down[RHS * c4 : RHS * (c4 + 1), :]
            for half in range(2):
                j = BRANCH * c + 4 * half
                rows = slice(RANK * j, RANK * (j + 4))
                far = product3(spread(leaves[:, 256 * half : 256 * (half + 1)]), b_h[rows, :], b_l[rows, :])
                for l4 in range(4):
                    out[:, 128 * (j + l4) : 128 * (j + l4 + 1)] = far[RHS * l4 : RHS * (l4 + 1), :]


VMEM = pl.BlockSpec(memory_space=pltpu.VMEM)
SMEM = pl.BlockSpec(memory_space=pltpu.SMEM)
ANY = pl.BlockSpec(memory_space=pl.ANY)


def on_device(coeff_in, coupling, source, target, counts, transfer, basis):
    nwide, ngrp = lax.axis_size("wide"), lax.axis_size("grp")
    nblocks = coupling.shape[0]
    ncl, width = coeff_in.shape
    nleaf, rank, points = basis.shape
    tables = [coeff_in]
    for k in range(1, ngrp):
        tables.append(lax.ppermute(coeff_in, "grp", [(i, (i + k) % ngrp) for i in range(ngrp)]))

    shape = jax.ShapeDtypeStruct
    ct = shape((nwide, 4 * rank, 2 * rank), BF)
    tr = shape(((1 + BRANCH) * rank, BRANCH * rank), BF)
    ba = shape((nleaf * rank, points), BF)
    ct_h, ct_l, t_h, t_l, b_h, b_l, code = pl.pallas_call(
        prepare,
        out_shape=(ct, ct, tr, tr, ba, ba, shape((nwide, 8, 128), F32)),
        in_specs=[SMEM, SMEM, VMEM, VMEM, VMEM],
        out_specs=(VMEM,) * 7,
        compiler_params=pltpu.CompilerParams(vmem_limit_bytes=32 << 20),
        cost_estimate=pl.CostEstimate(flops=0, bytes_accessed=20 << 20, transcendentals=0),
        name="prepare",
    )(target, counts, coupling, transfer, basis.reshape(nleaf * rank, points))

    me = lax.axis_index("grp")
    member, local = source // ncl, source % ncl
    idx = lax.rem(me - member + ngrp, ngrp) * 128 + local
    payload = pl.pallas_call(
        functools.partial(couple, ngrp),
        out_shape=shape((nwide, 40, 128), F32),
        in_specs=[SMEM] + [ANY] * ngrp + [VMEM] * 3,
        out_specs=VMEM,
        scratch_shapes=[pltpu.VMEM((ngrp, ncl, width), F32), pltpu.SemaphoreType.DMA((ngrp,))],
        compiler_params=pltpu.CompilerParams(vmem_limit_bytes=32 << 20),
        name="couple",
    )(idx, *tables, ct_h, ct_l, code)

    arrived = lax.all_to_all(payload, "wide", split_axis=0, concat_axis=0, tiled=True)

    return pl.pallas_call(
        downward,
        out_shape=shape((RHS, nleaf * points), F32),
        in_specs=[VMEM] * 5,
        out_specs=VMEM,
        scratch_shapes=[pltpu.VMEM((ncl * RHS, 128), F32)],
        compiler_params=pltpu.CompilerParams(vmem_limit_bytes=32 << 20),
        name="downward",
    )(arrived, t_h, t_l, b_h, b_l)


def solution(mesh):
    placed = (
        P(("grp", "wide"), None),
        P(("grp", "wide"), None, None),
        P(("grp", "wide")),
        P(("grp", "wide")),
        P(("grp", "wide")),
        P(("grp", "wide"), None, None),
        P(("grp", "wide"), None, None),
    )
    return jax.shard_map(
        on_device, mesh=mesh, in_specs=placed, out_specs=P(None, ("grp", "wide")), check_vma=False
    )
```

time: 72.4 us -> 32.2 us (0.44)
  the two profiles are of different devices: /device:TPU:0 before, /device:TPU:8 now
where the time goes in v1:
time: 32.2 us; the launch traced here: 31.9 us
  blocking collectives  9.4 us (29%)
  Pallas kernels  7.43 us (23%)
  local copies, waits for them, and re-layouts  6.56 us (20%)
  starting transfers between devices  4.61 us (14%)
  waiting for transfers between devices  3.82 us (12%)
    all_to_all x1, blocking collectives, on_device(): lax.all_to_all(payload, 'wide', split_axis=0, concat_axis=0, tiled=True)  9.4 us
    unnamed x13, local copies, waits for them, and re-layouts  6.56 us
    ppermute x3, starting transfers between devices, on_device(): lax.ppermute(coeff_in, 'grp', [(i, (i + k) % ngrp) for i in range(ngrp)])  4.61 us
    ppermute x3, waiting for transfers between devices, on_device(): lax.ppermute(coeff_in, 'grp', [(i, (i + k) % ngrp) for i in range(ngrp)])  3.82 us
    pallas_call x1, Pallas kernels, on_device(): pl.pallas_call(functools.partial(couple, ngrp), out_shape=shape((nwide, 4...  3.02 us
    pallas_call x1, Pallas kernels, on_device(): pl.pallas_call(prepare, out_shape=(ct, ct, tr, tr, ba, ba, shape((nwide,...  2.44 us
    pallas_call x1, Pallas kernels, on_device(): pl.pallas_call(downward, out_shape=shape((RHS, nleaf * points), F32), in_...  1.97 us
  transfers between devices with their start and end apart: 3, of which 2 were waited for; matrix products, arithmetic and copies ran while one was open for 11% of the time, Pallas kernels for 8%

profile of v1, /device:TPU:8, one launch (start us, length us, event | category | flops | bytes accessed | tf_op | source)
XLA Modules:
  0.0 31.9 jit_solution(3322655846197814967)
XLA Ops:
  0.0 1.6 %collective-permute-start = (f32[73,512]{1,0:T(8,128)}, f32[73,512]{1,0:T(8,128)S(1)}, u32[]{:S(2)}, u32[]{:S(2)}) collective-permute-start(f32[73,512]{1,0:T(8,128)} %refs_0_.1), channel_id=1, source_target_pairs={{0,8},{8,16},{16,24},{24,0},{1,9},{9,17},{17,25},{25,1},{2,10},{10... | collective-permute-start | bytes 448520 | tf_op jit(solution)/shard_map/ppermute | solution.py:174
  1.6 1.0 %collective-permute-start.1 = (f32[73,512]{1,0:T(8,128)}, f32[73,512]{1,0:T(8,128)S(1)}, u32[]{:S(2)}, u32[]{:S(2)}) collective-permute-start(f32[73,512]{1,0:T(8,128)} %refs_0_.1), channel_id=1, source_target_pairs={{0,16},{8,24},{16,0},{24,8},{1,17},{9,25},{17,1},{25,9},{2,18},{10... | collective-permute-start | bytes 448520 | tf_op jit(solution)/shard_map/ppermute | solution.py:174
  2.6 2.0 %collective-permute-start.2 = (f32[73,512]{1,0:T(8,128)}, f32[73,512]{1,0:T(8,128)S(1)}, u32[]{:S(2)}, u32[]{:S(2)}) collective-permute-start(f32[73,512]{1,0:T(8,128)} %refs_0_.1), channel_id=1, source_target_pairs={{0,24},{8,0},{16,8},{24,16},{1,25},{9,1},{17,9},{25,17},{2,26},{10... | collective-permute-start | bytes 448520 | tf_op jit(solution)/shard_map/ppermute | solution.py:174
  4.6 0.0 copy-start.3
  4.6 0.0 copy-start.4
  4.6 3.4 %copy.8.transfer = f32[72,64,64]{2,1,0:T(8,128)S(1)} copy(f32[72,64,64]{0,2,1:T(8,128)} %param.12) | data formatting | bytes 2359296 | tf_op args[5]
  8.0 0.0 copy-done.3
  8.0 0.0 copy-done.4
  8.0 0.0 copy-start
  8.0 1.6 %copy-done = f32[64,64,64]{2,1,0:T(8,128)S(1)} copy-done((f32[64,64,64]{2,1,0:T(8,128)S(1)}, f32[64,64,64]{2,1,0:T(8,128)}, u32[]{:S(2)}) %copy-start) | copy-done | bytes 1048600
  9.6 0.0 copy-start.1
  9.6 1.6 %copy-done.1 = f32[64,64,128]{2,1,0:T(8,128)S(1)} copy-done((f32[64,64,128]{2,1,0:T(8,128)S(1)}, f32[64,64,128]{2,1,0:T(8,128)}, u32[]{:S(2)}) %copy-start.1) | copy-done | bytes 2097176
  11.2 0.0 copy-start.5
  11.2 0.0 copy-start.2
  11.2 2.4 %prepare.1 = (bf16[8,256,128]{2,1,0:T(8,128)(2,1)S(1)}, bf16[8,256,128]{2,1,0:T(8,128)(2,1)S(1)}, bf16[576,512]{1,0:T(8,128)(2,1)S(1)}, bf16[576,512]{1,0:T(8,12...) custom-call(s32[64]{0:T(128)S(1)} %copy-done.3, ...), custom_call_target="tpu_custom_call" | custom-call | bytes 20971520 | tf_op jit(solution)/shard_map/prepare/pallas_call | solution.py:180
  13.7 0.0 copy-done.5
  13.7 0.0 collective-permute-done.refs_1_
  13.7 2.2 %collective-permute-done.1.refs_2_ = f32[73,512]{1,0:T(8,128)S(1)} collective-permute-done((f32[73,512]{1,0:T(8,128)}, f32[73,512]{1,0:T(8,128)S(1)}, u32[]{:S(2)}, u32[]{:S(2)}) %collective-permute-start.1) | collective-permute-done | bytes 149536 | tf_op jit(solution)/shard_map/ppermute | solution.py:174
  15.9 1.6 %collective-permute-done.2.refs_3_ = f32[73,512]{1,0:T(8,128)S(1)} collective-permute-done((f32[73,512]{1,0:T(8,128)}, f32[73,512]{1,0:T(8,128)S(1)}, u32[]{:S(2)}, u32[]{:S(2)}) %collective-permute-start.2) | collective-permute-done | bytes 149536 | tf_op jit(solution)/shard_map/ppermute | solution.py:174
  17.5 0.0 copy-done.2
  17.5 3.0 %couple.1 = f32[8,40,128]{2,1,0:T(8,128)S(1)} custom-call(s32[64]{0:T(128)S(1)} %fusion.idx, f32[73,512]{1,0:T(8,128)S(1)} %copy-done.2, f32[73,512]{1,0:T(8,128)S(1)} %collective-permute-done.refs_1_, f32[73,512]{1,0:T(8,128)S(1)} %collective-permute-done.1.refs_2_, f32[73,512]{1,0:T(8,128)S(1)} %collective-permute-done.2.refs_3_, ...), custom_call_target="tpu_custom_call" | custom-call | tf_op jit(solution)/shard_map/couple/pallas_call | solution.py:193
  20.6 9.4 %all_to_all.5.arrived = f32[8,40,128]{2,1,0:T(8,128)S(1)} all-to-all(f32[8,40,128]{2,1,0:T(8,128)S(1)} %couple.1), channel_id=1, replica_groups=mesh['grp'=4,'wide'=8] {'wide'}, dimensions={0} | all-to-all | bytes 327680 | tf_op jit(solution)/shard_map/all_to_all | solution.py:203
  30.0 2.0 %downward.1 = f32[8,8192]{1,0:T(8,128)} custom-call(f32[8,40,128]{2,1,0:T(8,128)S(1)} %all_to_all.5.arrived, bf16[576,512]{1,0:T(8,128)(2,1)S(1)} %get-tuple-element.15.t_h, bf16[576,512]{1,0:T(8,128)(2,1)S(1)} %get-tuple-element.16.t_l, bf16[4096,128]{1,0:T(8,128)(2,1)S(1)} %get-tuple-element.17.b_h, bf16[4096,128]{1,0:T(8,128)(2,1)S(1)} %get-tuple-element.18.b_l), custom_call_target="tpu_custom_call" | custom-call | tf_op jit(solution)/shard_map/downward/pallas_call | solution.py:205
  (1 shorter events, 0.0 us)
Async XLA Ops:
  0.0 13.7 %collective-permute-start = (f32[73,512]{1,0:T(8,128)}, f32[73,512]{1,0:T(8,128)S(1)}, u32[]{:S(2)}, u32[]{:S(2)}) collective-permute-start(f32[73,512]{1,0:T(8,128)} %refs_0_.1), channel_id=1, source_target_pairs={{0,8},{8,16},{16,24},{24,0},{1,9},{9,17},{17,25},{25,1},{2,10},{10... | collective-permute-start | bytes 448520 | tf_op jit(solution)/shard_map/ppermute | solution.py:174
  1.6 14.3 %collective-permute-start.1 = (f32[73,512]{1,0:T(8,128)}, f32[73,512]{1,0:T(8,128)S(1)}, u32[]{:S(2)}, u32[]{:S(2)}) collective-permute-start(f32[73,512]{1,0:T(8,128)} %refs_0_.1), channel_id=1, source_target_pairs={{0,16},{8,24},{16,0},{24,8},{1,17},{9,25},{17,1},{25,9},{2,18},{10... | collective-permute-start | bytes 448520 | tf_op jit(solution)/shard_map/ppermute | solution.py:174
  2.6 14.9 %collective-permute-start.2 = (f32[73,512]{1,0:T(8,128)}, f32[73,512]{1,0:T(8,128)S(1)}, u32[]{:S(2)}, u32[]{:S(2)}) collective-permute-start(f32[73,512]{1,0:T(8,128)} %refs_0_.1), channel_id=1, source_target_pairs={{0,24},{8,0},{16,8},{24,16},{1,25},{9,1},{17,9},{25,17},{2,26},{10... | collective-permute-start | bytes 448520 | tf_op jit(solution)/shard_map/ppermute | solution.py:174
  4.6 3.4 %copy-start.3 = (s32[64]{0:T(128)S(1)}, s32[64]{0:T(128)}, u32[]{:S(2)}) copy-start(s32[64]{0:T(128)} %target.1) | copy-start | bytes 772
  4.6 3.4 %copy-start.4 = (s32[8]{0:T(128)S(1)}, s32[8]{0:T(128)}, u32[]{:S(2)}) copy-start(s32[8]{0:T(128)} %counts.1) | copy-start | bytes 100
  8.0 1.6 %copy-start = (f32[64,64,64]{2,1,0:T(8,128)S(1)}, f32[64,64,64]{2,1,0:T(8,128)}, u32[]{:S(2)}) copy-start(f32[64,64,64]{2,1,0:T(8,128)} %coupling.1) | copy-start | bytes 3145732
  9.6 1.6 %copy-start.1 = (f32[64,64,128]{2,1,0:T(8,128)S(1)}, f32[64,64,128]{2,1,0:T(8,128)}, u32[]{:S(2)}) copy-start(f32[64,64,128]{2,1,0:T(8,128)} %param.13) | copy-start | bytes 6291460
  11.2 2.5 %copy-start.5 = (s32[64]{0:T(128)S(1)}, s32[64]{0:T(128)}, u32[]{:S(2)}) copy-start(s32[64]{0:T(128)} %param.9) | copy-start | bytes 772
  11.2 6.3 %copy-start.2 = (f32[73,512]{1,0:T(8,128)S(1)}, f32[73,512]{1,0:T(8,128)}, u32[]{:S(2)}) copy-start(f32[73,512]{1,0:T(8,128)} %refs_0_.1) | copy-start | bytes 448516

commit v2 on v1

--- a/solution.py
+++ b/solution.py
@@ -37,7 +37,8 @@
     return lax.broadcasted_iota(jnp.int32, shape, dim)
 
 
-def prepare(target, counts, coupling, transfer, basis, ct_h, ct_l, t_h, t_l, b_h, b_l, code):
+def prepare(target, counts, after, coupling, transfer, ct_h, ct_l, t_h, t_l, code):
+    del after
     nwide = code.shape[0]
 
     def per_peer(p, carry):
@@ -62,29 +63,17 @@
         t_h[RANK * g : RANK * (g + 1), :] = high
         t_l[RANK * g : RANK * (g + 1), :] = low
 
-    def per_group(g, carry):
-        rows = pl.ds(pl.multiple_of(g * 256, 256), 256)
-        high, low = split(basis[rows, :])
-        b_h[rows, :] = high
-        b_l[rows, :] = low
-        return carry
-
-    lax.fori_loop(0, basis.shape[0] // 256, per_group, 0)
-
 
 def couple(ntab, idx, *refs):
-    tables, (ct_h, ct_l, code, out, held, sems) = refs[:ntab], refs[ntab:]
+    tables, (ct_h, ct_l, code, out, held, rows_h, spread_out) = refs[:ntab], refs[ntab:]
     nwide = out.shape[0]
-    copies = [pltpu.make_async_copy(tables[k], held.at[k], sems.at[k]) for k in range(ntab)]
-    for copy in copies:
-        copy.start()
     width = RANK * RHS
     gather = jnp.where(iota((width, 256), 0) // RHS == iota((width, 256), 1) % RANK, 1.0, 0.0).astype(BF)
     mine = iota((RHS, width), 0) == iota((RHS, width), 1) % RHS
     diagonal = (iota((64, 256), 0) // RHS) % HALF == iota((64, 256), 1) // RANK
     left = iota((32, 128), 1) < RANK
-    for copy in copies:
-        copy.wait()
+    for k in range(ntab):
+        held[k] = tables[k][...]
     for p in range(nwide):
         picked = []
         for slot in range(SLOTS):
@@ -92,14 +81,18 @@
             row = held[at // 128, pl.ds(at % 128, 1), :]
             picked.append(jnp.where(mine, jnp.broadcast_to(row, (RHS, width)), 0.0))
         high, low = split(jnp.concatenate(picked, axis=0))
-        x = mm(jnp.concatenate([high, low], axis=0), gather)
-        x = jnp.where(diagonal, x[:64] + x[64:], 0.0)
+        rows_h[128 * p : 128 * p + 64, :] = high
+        rows_h[128 * p + 64 : 128 * p + 128, :] = low
+    spread_out[...] = mm(rows_h[...], gather)
+    for p in range(nwide):
+        x = spread_out[128 * p : 128 * p + 64, :] + spread_out[128 * p + 64 : 128 * p + 128, :]
+        x = jnp.where(diagonal, x, 0.0)
         z = product3(x, ct_h[p], ct_l[p])
         out[p, :32, :] = jnp.where(left, z[:32], z[32:])
         out[p, 32:, :] = code[p]
 
 
-def downward(arrived, t_h, t_l, b_h, b_l, out, full):
+def downward(arrived, t_h, t_l, basis, out, full):
     nwide = arrived.shape[0]
     ncl = full.shape[0] // RHS
     value = jnp.concatenate([arrived[p, :32, :] for p in range(nwide)], axis=0)
@@ -154,7 +147,7 @@
             for half in range(2):
                 j = BRANCH * c + 4 * half
                 rows = slice(RANK * j, RANK * (j + 4))
-                far = product3(spread(leaves[:, 256 * half : 256 * (half + 1)]), b_h[rows, :], b_l[rows, :])
+                far = product3(spread(leaves[:, 256 * half : 256 * (half + 1)]), *split(basis[rows, :]))
                 for l4 in range(4):
                     out[:, 128 * (j + l4) : 128 * (j + l4 + 1)] = far[RHS * l4 : RHS * (l4 + 1), :]
 
@@ -162,6 +155,21 @@
 VMEM = pl.BlockSpec(memory_space=pltpu.VMEM)
 SMEM = pl.BlockSpec(memory_space=pltpu.SMEM)
 ANY = pl.BlockSpec(memory_space=pl.ANY)
+
+
+def gathered(x, n):
+    if n != 4:
+        rest = [lax.ppermute(x, "grp", [(i, (i + k) % n) for i in range(n)]) for k in range(1, n)]
+        return [x] + rest, lambda me, member: lax.rem(me - member + n, n)
+    far = lax.ppermute(x, "grp", [(i, 3 - i) for i in range(n)])
+    near = lax.ppermute(x, "grp", [(i, i ^ 1) for i in range(n)])
+    cross = lax.ppermute(far, "grp", [(i, i ^ 1) for i in range(n)])
+
+    def place(me, member):
+        other = jnp.where(member == me ^ 1, 2, 3)
+        return jnp.where(member == me, 0, jnp.where(member == 3 - me, 1, other))
+
+    return [x, far, near, cross], place
 
 
 def on_device(coeff_in, coupling, source, target, counts, transfer, basis):
@@ -169,33 +177,34 @@
     nblocks = coupling.shape[0]
     ncl, width = coeff_in.shape
     nleaf, rank, points = basis.shape
-    tables = [coeff_in]
-    for k in range(1, ngrp):
-        tables.append(lax.ppermute(coeff_in, "grp", [(i, (i + k) % ngrp) for i in range(ngrp)]))
+    tables, place = gathered(coeff_in, ngrp)
 
     shape = jax.ShapeDtypeStruct
     ct = shape((nwide, 4 * rank, 2 * rank), BF)
     tr = shape(((1 + BRANCH) * rank, BRANCH * rank), BF)
-    ba = shape((nleaf * rank, points), BF)
-    ct_h, ct_l, t_h, t_l, b_h, b_l, code = pl.pallas_call(
+    ct_h, ct_l, t_h, t_l, code = pl.pallas_call(
         prepare,
-        out_shape=(ct, ct, tr, tr, ba, ba, shape((nwide, 8, 128), F32)),
-        in_specs=[SMEM, SMEM, VMEM, VMEM, VMEM],
-        out_specs=(VMEM,) * 7,
+        out_shape=(ct, ct, tr, tr, shape((nwide, 8, 128), F32)),
+        in_specs=[SMEM, SMEM, ANY, VMEM, VMEM],
+        out_specs=(VMEM,) * 5,
         compiler_params=pltpu.CompilerParams(vmem_limit_bytes=32 << 20),
         cost_estimate=pl.CostEstimate(flops=0, bytes_accessed=20 << 20, transcendentals=0),
         name="prepare",
-    )(target, counts, coupling, transfer, basis.reshape(nleaf * rank, points))
+    )(target, counts, tables[1], coupling, transfer)
 
     me = lax.axis_index("grp")
     member, local = source // ncl, source % ncl
-    idx = lax.rem(me - member + ngrp, ngrp) * 128 + local
+    idx = place(me, member) * 128 + local
     payload = pl.pallas_call(
         functools.partial(couple, ngrp),
         out_shape=shape((nwide, 40, 128), F32),
-        in_specs=[SMEM] + [ANY] * ngrp + [VMEM] * 3,
+        in_specs=[SMEM] + [VMEM] * (ngrp + 3),
         out_specs=VMEM,
-        scratch_shapes=[pltpu.VMEM((ngrp, ncl, width), F32), pltpu.SemaphoreType.DMA((ngrp,))],
+        scratch_shapes=[
+            pltpu.VMEM((len(tables), ncl, width), F32),
+            pltpu.VMEM((2 * nblocks * RHS, width), BF),
+            pltpu.VMEM((2 * nblocks * RHS, 256), F32),
+        ],
         compiler_params=pltpu.CompilerParams(vmem_limit_bytes=32 << 20),
         name="couple",
     )(idx, *tables, ct_h, ct_l, code)
@@ -205,12 +214,12 @@
     return pl.pallas_call(
         downward,
         out_shape=shape((RHS, nleaf * points), F32),
-        in_specs=[VMEM] * 5,
+        in_specs=[VMEM] * 4,
         out_specs=VMEM,
         scratch_shapes=[pltpu.VMEM((ncl * RHS, 128), F32)],
         compiler_params=pltpu.CompilerParams(vmem_limit_bytes=32 << 20),
         name="downward",
-    )(arrived, t_h, t_l, b_h, b_l)
+    )(arrived, t_h, t_l, basis.reshape(nleaf * rank, points))
 
 
 def solution(mesh):

time: 32.2 us -> 29.8 us (0.925)
  the two profiles are of different devices: /device:TPU:8 before, /device:TPU:0 now
where the time goes in v2:
time: 29.8 us; the launch traced here: 29.6 us
  blocking collectives  9.4 us (32%)
  starting transfers between devices  7.4 us (25%)
  Pallas kernels  5.75 us (19%)
  local copies, waits for them, and re-layouts  4.99 us (17%)
  waiting for transfers between devices  1.94 us (7%)
    all_to_all x1, blocking collectives, on_device(): lax.all_to_all(payload, 'wide', split_axis=0, concat_axis=0, tiled=True)  9.4 us
    ppermute x1, starting transfers between devices, gathered(): far = lax.ppermute(x, 'grp', [(i, 3 - i) for i in range(n)])  5.05 us
    unnamed x13, local copies, waits for them, and re-layouts  4.99 us
    ppermute x1, starting transfers between devices, gathered(): cross = lax.ppermute(far, 'grp', [(i, i ^ 1) for i in range(n)])  2.35 us
    pallas_call x1, Pallas kernels, on_device(): pl.pallas_call(prepare, out_shape=(ct, ct, tr, tr, shape((nwide, 8, 128),...  2.16 us
    pallas_call x1, Pallas kernels, on_device(): pl.pallas_call(downward, out_shape=shape((RHS, nleaf * points), F32), in_...  1.98 us
    ppermute x1, waiting for transfers between devices, gathered(): far = lax.ppermute(x, 'grp', [(i, 3 - i) for i in range(n)])  1.88 us
    pallas_call x1, Pallas kernels, on_device(): pl.pallas_call(functools.partial(couple, ngrp), out_shape=shape((nwide, 4...  1.6 us
  transfers between devices with their start and end apart: 3, of which 2 were waited for; matrix products, arithmetic and copies ran while one was open for 11% of the time, Pallas kernels for 7%

profile of v2, /device:TPU:0, one launch (start us, length us, event | category | flops | bytes accessed | tf_op | source)
XLA Modules:
  0.0 29.6 jit_solution(12984065831435183304)
XLA Ops:
  0.0 5.0 %collective-permute-start = (f32[73,512]{1,0:T(8,128)}, f32[73,512]{1,0:T(8,128)S(1)}, u32[]{:S(2)}, u32[]{:S(2)}) collective-permute-start(f32[73,512]{1,0:T(8,128)} %refs_0_.1), channel_id=1, source_target_pairs={{0,24},{8,16},{16,8},{24,0},{1,25},{9,17},{17,9},{25,1},{2,26},{10... | collective-permute-start | bytes 448520 | tf_op jit(solution)/shard_map/ppermute | solution.py:164
  5.0 0.0 collective-permute-start.1
  5.1 0.0 copy-start.5
  5.1 0.0 copy-start.3
  5.1 0.0 copy-start.4
  5.1 3.4 %copy.8.transfer = f32[72,64,64]{2,1,0:T(8,128)S(1)} copy(f32[72,64,64]{0,2,1:T(8,128)} %param.12) | data formatting | bytes 2359296 | tf_op args[5]
  8.5 1.9 %collective-permute-done.after.refs_1_ = f32[73,512]{1,0:T(8,128)S(1)} collective-permute-done((f32[73,512]{1,0:T(8,128)}, f32[73,512]{1,0:T(8,128)S(1)}, u32[]{:S(2)}, u32[]{:S(2)}) %collective-permute-start) | collective-permute-done | bytes 149536 | tf_op jit(solution)/shard_map/ppermute | solution.py:164
  10.3 2.4 %collective-permute-start.2 = (f32[73,512]{1,0:T(8,128)S(1)}, f32[73,512]{1,0:T(8,128)S(1)}, u32[]{:S(2)}, u32[]{:S(2)}) collective-permute-start(f32[73,512]{1,0:T(8,128)S(1)} %collective-permute-done.after.refs_1_), channel_id=1, source_target_pairs={{0,8},{8,0},{16,24},{24,16},{1,9},{9,1},{17,25},{25,17},{2,10},{10... | collective-permute-start | bytes 448520 | tf_op jit(solution)/shard_map/ppermute | solution.py:166
  12.7 0.0 copy-done.5
  12.7 0.0 copy-done.3
  12.7 0.0 copy-done.4
  12.7 0.0 copy-start
  12.7 1.6 %copy-done = f32[64,64,64]{2,1,0:T(8,128)S(1)} copy-done((f32[64,64,64]{2,1,0:T(8,128)S(1)}, f32[64,64,64]{2,1,0:T(8,128)}, u32[]{:S(2)}) %copy-start) | copy-done | bytes 1048600
  14.3 0.0 copy-start.2
  14.3 2.2 %prepare.1 = (bf16[8,256,128]{2,1,0:T(8,128)(2,1)S(1)}, bf16[8,256,128]{2,1,0:T(8,128)(2,1)S(1)}, bf16[576,512]{1,0:T(8,128)(2,1)S(1)}, bf16[576,512]{1,0:T(8,128)(2,1)S(1)}, f32[8,8,128]{2,1,0:T(8,128)S(1)}) custom-call(s32[64]{0:T(128)S(1)} %copy-done.3, s32[8]{0:T(128)S(1)} %copy-done.4, f32[73,512]{1,0:T(8,128)S(1)} %collective-permute-done.after.refs_1_, ...), custom_call_target="tpu_custom_call" | custom-call | bytes 20971520 | tf_op jit(solution)/shard_map/prepare/pallas_call | solution.py:185
  16.5 0.0 copy-start.1
  16.5 0.0 collective-permute-done.1.refs_2_
  16.5 0.1 collective-permute-done.2.refs_3_
  16.6 0.0 copy-done.2
  16.6 1.6 %couple.1 = f32[8,40,128]{2,1,0:T(8,128)S(1)} custom-call(s32[64]{0:T(128)S(1)} %fusion.idx, f32[73,512]{1,0:T(8,128)S(1)} %copy-done.2, f32[73,512]{1,0:T(8,128)S(1)} %collective-permute-done.after.refs_1_, f32[73,512]{1,0:T(8,128)S(1)} %collective-permute-done.1.refs_2_, f32[73,512]{1,0:T(8,128)S(1)} %collective-permute-done.2.refs_3_, ...), custom_call_target="tpu_custom_call" | custom-call | tf_op jit(solution)/shard_map/couple/pallas_call | solution.py:198
  18.2 9.4 %all_to_all.5.arrived = f32[8,40,128]{2,1,0:T(8,128)S(1)} all-to-all(f32[8,40,128]{2,1,0:T(8,128)S(1)} %couple.1), channel_id=1, replica_groups=mesh['grp'=4,'wide'=8] {'wide'}, dimensions={0} | all-to-all | bytes 327680 | tf_op jit(solution)/shard_map/all_to_all | solution.py:212
  27.6 0.0 copy-done.1
  27.6 2.0 %downward.1 = f32[8,8192]{1,0:T(8,128)} custom-call(f32[8,40,128]{2,1,0:T(8,128)S(1)} %all_to_all.5.arrived, bf16[576,512]{1,0:T(8,128)(2,1)S(1)} %get-tuple-element.13.t_h, bf16[576,512]{1,0:T(8,128)(2,1)S(1)} %get-tuple-element.14.t_l, f32[4096,128]{1,0:T(8,128)S(1)} %bitcast.1), custom_call_target="tpu_custom_call" | custom-call | tf_op jit(solution)/shard_map/downward/pallas_call | solution.py:214
  (1 shorter events, 0.0 us)
Async XLA Ops:
  0.0 10.3 %collective-permute-start = (f32[73,512]{1,0:T(8,128)}, f32[73,512]{1,0:T(8,128)S(1)}, u32[]{:S(2)}, u32[]{:S(2)}) collective-permute-start(f32[73,512]{1,0:T(8,128)} %refs_0_.1), channel_id=1, source_target_pairs={{0,24},{8,16},{16,8},{24,0},{1,25},{9,17},{17,9},{25,1},{2,26},{10... | collective-permute-start | bytes 448520 | tf_op jit(solution)/shard_map/ppermute | solution.py:164
  5.0 11.5 %collective-permute-start.1 = (f32[73,512]{1,0:T(8,128)}, f32[73,512]{1,0:T(8,128)S(1)}, u32[]{:S(2)}, u32[]{:S(2)}) collective-permute-start(f32[73,512]{1,0:T(8,128)} %refs_0_.1), channel_id=1, source_target_pairs={{0,8},{8,0},{16,24},{24,16},{1,9},{9,1},{17,25},{25,17},{2,10},{10... | collective-permute-start | bytes 448520 | tf_op jit(solution)/shard_map/ppermute | solution.py:165
  5.1 7.6 %copy-start.5 = (s32[64]{0:T(128)S(1)}, s32[64]{0:T(128)}, u32[]{:S(2)}) copy-start(s32[64]{0:T(128)} %param.9) | copy-start | bytes 772
  5.1 7.7 %copy-start.3 = (s32[64]{0:T(128)S(1)}, s32[64]{0:T(128)}, u32[]{:S(2)}) copy-start(s32[64]{0:T(128)} %target.1) | copy-start | bytes 772
  5.1 7.7 %copy-start.4 = (s32[8]{0:T(128)S(1)}, s32[8]{0:T(128)}, u32[]{:S(2)}) copy-start(s32[8]{0:T(128)} %counts.1) | copy-start | bytes 100
  10.3 6.2 %collective-permute-start.2 = (f32[73,512]{1,0:T(8,128)S(1)}, f32[73,512]{1,0:T(8,128)S(1)}, u32[]{:S(2)}, u32[]{:S(2)}) collective-permute-start(f32[73,512]{1,0:T(8,128)S(1)} %collective-permute-done.after.refs_1_), channel_id=1, source_target_pairs={{0,8},{8,0},{16,24},{24,16},{1,9},{9,1},{17,25},{25,17},{2,10},{10... | collective-permute-start | bytes 448520 | tf_op jit(solution)/shard_map/ppermute | solution.py:166
  12.7 1.6 %copy-start = (f32[64,64,64]{2,1,0:T(8,128)S(1)}, f32[64,64,64]{2,1,0:T(8,128)}, u32[]{:S(2)}) copy-start(f32[64,64,64]{2,1,0:T(8,128)} %coupling.1) | copy-start | bytes 3145732
  14.3 2.3 %copy-start.2 = (f32[73,512]{1,0:T(8,128)S(1)}, f32[73,512]{1,0:T(8,128)}, u32[]{:S(2)}) copy-start(f32[73,512]{1,0:T(8,128)} %refs_0_.1) | copy-start | bytes 448516
  16.5 11.1 %copy-start.1 = (f32[64,64,128]{2,1,0:T(8,128)S(1)}, f32[64,64,128]{2,1,0:T(8,128)}, u32[]{:S(2)}) copy-start(f32[64,64,128]{2,1,0:T(8,128)} %param.13) | copy-start | bytes 6291460

commit v3 on v1

v3 whole, which is shorter than its diff:
```python
import functools

import jax
import jax.numpy as jnp
from jax import lax
from jax.experimental import pallas as pl
from jax.experimental.pallas import tpu as pltpu
from jax.sharding import PartitionSpec as P

BRANCH = 8
RANK = 64
RHS = 8
SLOTS = 8
HALF = 4
BF = jnp.bfloat16
F32 = jnp.float32


def split(x):
    high = x.astype(BF)
    low = (x - high.astype(F32)).astype(BF)
    return high, low


def mm(a, b):
    return jnp.dot(a, b, preferred_element_type=F32)


def product3(x, high_ref_value, low_ref_value):
    rows = x.shape[0]
    high, low = split(x)
    both = mm(jnp.concatenate([high, low], axis=0), high_ref_value)
    return both[:rows] + both[rows:] + mm(high, low_ref_value)


def iota(shape, dim):
    return lax.broadcasted_iota(jnp.int32, shape, dim)


CHUNKS = 4


def prepare(target, counts, coupling_in, transfer_in, ct, t_h, t_l, code, coupling, transfer, turned, sems):
    nwide = code.shape[0]
    ncl = transfer.shape[2]

    def chunks(source, held, at):
        size = held.shape[0] // CHUNKS
        return [
            pltpu.make_async_copy(source.at[pl.ds(size * k, size)], held.at[pl.ds(size * k, size)], sems.at[at + k])
            for k in range(CHUNKS)
        ]

    first, second = chunks(transfer_in, transfer, 0), chunks(coupling_in, coupling, CHUNKS)
    for copy in first + second:
        copy.start()

    def codes(p, carry):
        row, lane = iota((8, 128), 0), iota((8, 128), 1)
        value = jnp.zeros((8, 128), jnp.int32)
        for slot in range(SLOTS):
            here = (row == slot // HALF) & ((lane % 32) // RHS == slot % HALF)
            at = jnp.where(slot < counts[p], target[SLOTS * p + slot] * RHS, -RHS)
            value = jnp.where(here, at + lane % RHS, value)
        code[p] = value.astype(F32)
        return carry

    lax.fori_loop(0, nwide, codes, 0)
    for i in range(RANK):
        if i % (RANK // CHUNKS) == 0:
            first[i // (RANK // CHUNKS)].wait()
        turned[ncl * i : ncl * (i + 1), :] = transfer[i].T
    for g in range(1 + BRANCH):
        rows = [turned[pl.ds(BRANCH * g + c, RANK, stride=ncl), :] for c in range(BRANCH)]
        high, low = split(jnp.concatenate(rows, axis=0).T)
        t_h[RANK * g : RANK * (g + 1), :] = high
        t_l[RANK * g : RANK * (g + 1), :] = low

    def turn(p, carry):
        for s in range(HALF):
            pair = jnp.concatenate([coupling[SLOTS * p + s], coupling[SLOTS * p + HALF + s]], axis=0)
            high, low = split(pair.T)
            ct[p, RANK * s : RANK * (s + 1), :128] = high
            ct[p, RANK * s : RANK * (s + 1), 128:] = low
        return carry

    for k in range(CHUNKS):
        second[k].wait()
        lax.fori_loop(nwide // CHUNKS * k, nwide // CHUNKS * (k + 1), turn, 0, unroll=2)


def pick(two_step, last, source, *refs):
    tables, (early, hot, rows) = refs[:-3], refs[-3:]
    ntab = len(tables) + 1
    ncl = tables[0].shape[0]
    grp = lax.axis_index("grp")
    for k, table in enumerate(tables):
        rows[k] = table[...]
    rows[ntab - 1] = jnp.zeros(rows.shape[1:], F32)
    lane = iota((1, 128), 1)
    marks = []
    for b in range(early.shape[0]):
        at = source[b]
        member = sum(jnp.where(at >= ncl * k, 1, 0) for k in range(1, ntab))
        table = member ^ grp if two_step else lax.rem(grp - member + ntab, ntab)
        held = jnp.where(table == last, ntab - 1, table - jnp.where(table > last, 1, 0))
        local = at - ncl * member
        early[b : b + 1, :] = rows[held, pl.ds(local, 1), :]
        marks.append(jnp.where(lane == jnp.where(table == last, local, -1), 1.0, 0.0))
    hot[...] = jnp.concatenate(marks, axis=0).astype(BF)


def couple(two_step, early, hot, last, ct, code, same, other, held_a, held_b):
    nwide = code.shape[0]
    nblocks, width = early.shape
    ncl = last.shape[0]
    wide = lax.axis_index("wide") if two_step else 0
    high, low = split(jnp.concatenate([last[...], jnp.zeros((128 - ncl, width), F32)], axis=0))
    picked = early[...] + (mm(hot[...], high) + mm(hot[...], low))
    place, to = iota((width, 256), 0), iota((width, 256), 1)
    turn = (place // RHS == to % RANK) & (place % RHS // 2 == to // RANK)
    turn = jnp.where(turn, 1.0, 0.0).astype(BF)
    odd = iota((nblocks, width), 1) % 2
    high, low = split(jnp.concatenate([jnp.where(odd == i, picked, 0.0) for i in range(2)], axis=0))
    turned = mm(jnp.concatenate([high, low], axis=0), turn)
    turned = turned[: 2 * nblocks] + turned[2 * nblocks :]
    first = iota((nblocks, 128), 1) < RANK
    own = iota((nblocks, 128), 0) % HALF - iota((nblocks, 128), 1) // RANK
    for s in range(4):
        for i in range(2):
            x = turned[nblocks * i : nblocks * (i + 1), 128 * (s // 2) : 128 * (s // 2 + 1)]
            swapped = pltpu.roll(x, RANK, 1)
            x = jnp.where(first, x, swapped) if s % 2 == 0 else jnp.where(first, swapped, x)
            rows = pl.ds(2 * s + i, nblocks, stride=RHS)
            held_a[rows, :] = jnp.where(own == 0, x, 0.0)
            held_b[rows, :] = jnp.where(own == 2, x, 0.0)
    left = iota((32, 128), 1) < RANK
    for p in range(nwide):
        peer = p ^ wide
        at = pl.ds(pl.multiple_of(peer * 64, 64), 64)
        high, low = split(jnp.concatenate([held_a[at, :], held_b[at, :]], axis=1))
        z = mm(jnp.concatenate([high, low], axis=0), ct[peer])
        z = z[:64, :128] + (z[:64, 128:] + z[64:, :128])
        out = other if p % 2 else same
        out[p // 2, :32, :] = jnp.where(left, z[:32], z[32:])
        out[p // 2, 32:, :] = code[peer]


def downward(counts, *refs):
    arrays, (t_h, t_l, basis, out, full) = refs[: len(counts)], refs[len(counts) :]
    arrived = [array.at[i] for array, count in zip(arrays, counts) for i in range(count)]
    nwide = len(arrived)
    ncl = full.shape[0] // RHS
    value = jnp.concatenate([arrived[p][:32, :] for p in range(nwide)], axis=0)
    high, low = split(value)
    weights = jnp.concatenate([high, low], axis=1)
    lane = iota((1, 128), 1)
    codes = []
    for h in range(2):
        parts = []
        for q in range(nwide // 4):
            part = arrived[4 * q][32 + h : 33 + h, :]
            for e in range(1, 4):
                part = jnp.where(lane // 32 == e, arrived[4 * q + e][32 + h : 33 + h, :], part)
            parts.append(part)
        codes.append(jnp.concatenate(parts, axis=1).astype(jnp.int32))
    total = full.shape[0]
    step = 80
    for at in range(0, total, step):
        rows = min(step, total - at)
        sums = []
        for h in range(2):
            place = iota((rows, 32 * nwide), 0) + at
            hot = jnp.where(place == codes[h], 1.0, 0.0).astype(BF)
            r = mm(hot, weights)
            sums.append(r[:, :128] + r[:, 128:])
        s = jnp.where(iota((rows, 128), 1) < RANK, sums[0], sums[1])
        full[at : at + rows, :] = s + pltpu.roll(s, RANK, 1)

    first = iota((RHS, 128), 1) < RANK

    def pairs(cluster, count):
        parts = []
        for i in range(0, count, 2):
            a = full[RHS * (cluster + i) : RHS * (cluster + i + 1), :]
            b = full[RHS * (cluster + i + 1) : RHS * (cluster + i + 2), :]
            parts.append(jnp.where(first, a, b))
        return jnp.concatenate(parts, axis=1)

    diagonal = iota((32, 256), 0) // RHS == iota((32, 256), 1) // RANK

    def spread(x):
        return jnp.where(diagonal, jnp.concatenate([x] * 4, axis=0), 0.0)

    top = full[:RHS, :RANK]
    middle = pairs(1, BRANCH) + product3(top, t_h[:RANK, :], t_l[:RANK, :])
    for g in range(2):
        at = slice(RANK + 256 * g, RANK + 256 * (g + 1))
        down = product3(spread(middle[:, 256 * g : 256 * (g + 1)]), t_h[at, :], t_l[at, :])
        for c4 in range(4):
            c = 4 * g + c4
            leaves = pairs(1 + BRANCH + BRANCH * c, BRANCH) + down[RHS * c4 : RHS * (c4 + 1), :]
            for half in range(2):
                j = BRANCH * c + 4 * half
                rows = slice(RANK * j, RANK * (j + 4))
                far = product3(spread(leaves[:, 256 * half : 256 * (half + 1)]), *split(basis[rows, :]))
                for l4 in range(4):
                    out[:, 128 * (j + l4) : 128 * (j + l4 + 1)] = far[RHS * l4 : RHS * (l4 + 1), :]


VMEM = pl.BlockSpec(memory_space=pltpu.VMEM)
SMEM = pl.BlockSpec(memory_space=pltpu.SMEM)
ANY = pl.BlockSpec(memory_space=pl.ANY)


def on_device(coeff_in, coupling, source, target, counts, transfer, basis):
    nwide, ngrp = lax.axis_size("wide"), lax.axis_size("grp")
    nblocks = coupling.shape[0]
    ncl, width = coeff_in.shape
    nleaf, rank, points = basis.shape
    two_step = ngrp == 4 and nwide == 8

    shape = jax.ShapeDtypeStruct
    ct = shape((nwide, 4 * rank, 4 * rank), BF)
    tr = shape(((1 + BRANCH) * rank, BRANCH * rank), BF)
    turned = jnp.transpose(transfer, (1, 2, 0))
    ct, t_h, t_l, code = pl.pallas_call(
        prepare,
        out_shape=(ct, tr, tr, shape((nwide, 8, 128), F32)),
        in_specs=[SMEM, SMEM, ANY, ANY],
        out_specs=(VMEM,) * 4,
        scratch_shapes=[
            pltpu.VMEM(coupling.shape, F32),
            pltpu.VMEM(turned.shape, F32),
            pltpu.VMEM((rank * (ncl - 1), rank), F32),
            pltpu.SemaphoreType.DMA((2 * CHUNKS,)),
        ],
        compiler_params=pltpu.CompilerParams(vmem_limit_bytes=50 << 20),
        cost_estimate=pl.CostEstimate(flops=0, bytes_accessed=10 << 20, transcendentals=0),
        name="prepare",
    )(target, counts, coupling, turned)

    def moved(x, axis, n, to):
        return lax.ppermute(x, axis, [(i, to(i)) for i in range(n)])

    if two_step:
        far = moved(coeff_in, "grp", ngrp, lambda i: i ^ 3)
        near = moved(coeff_in, "grp", ngrp, lambda i: i ^ 1)
        far, code = lax.optimization_barrier((far, code))
        cross = moved(far, "grp", ngrp, lambda i: i ^ 1)
        tables = [coeff_in, near, cross, far]
    else:
        tables = [coeff_in]
        for k in range(1, ngrp):
            tables.append(moved(coeff_in, "grp", ngrp, lambda i: (i + k) % ngrp))

    last = 2 if two_step else ngrp - 1
    early, hot = pl.pallas_call(
        functools.partial(pick, two_step, last),
        out_shape=(shape((nblocks, width), F32), shape((nblocks, 128), BF)),
        in_specs=[SMEM] + [VMEM] * (ngrp - 1),
        out_specs=(VMEM, VMEM),
        scratch_shapes=[pltpu.VMEM((ngrp, ncl, width), F32)],
        compiler_params=pltpu.CompilerParams(vmem_limit_bytes=16 << 20),
        name="pick",
    )(source, *tables[:last], *tables[last + 1 :])

    half = shape((nwide // 2, 40, 128), F32)
    same, other = pl.pallas_call(
        functools.partial(couple, two_step),
        out_shape=(half, half),
        in_specs=[VMEM] * 5,
        out_specs=(VMEM, VMEM),
        scratch_shapes=[pltpu.VMEM((nblocks * RHS, 128), F32)] * 2,
        compiler_params=pltpu.CompilerParams(vmem_limit_bytes=32 << 20),
        name="couple",
    )(early, hot, tables[last], ct, code)

    if two_step:
        mate = moved(other, "wide", nwide, lambda i: i ^ 1)
        arrived = [same[:1], mate[:1]]
        for k in (3, 2, 1):
            arrived.append(moved(jnp.stack([same[k], mate[k]]), "wide", nwide, lambda i: i ^ (2 * k)))
    else:
        payload = jnp.stack([same, other], axis=1).reshape(nwide, 40, 128)
        arrived = [lax.all_to_all(payload, "wide", split_axis=0, concat_axis=0, tiled=True)]

    return pl.pallas_call(
        functools.partial(downward, tuple(a.shape[0] for a in arrived)),
        out_shape=shape((RHS, nleaf * points), F32),
        in_specs=[VMEM] * (len(arrived) + 3),
        out_specs=VMEM,
        scratch_shapes=[pltpu.VMEM((ncl * RHS, 128), F32)],
        compiler_params=pltpu.CompilerParams(vmem_limit_bytes=32 << 20),
        name="downward",
    )(*arrived, t_h, t_l, basis.reshape(nleaf * rank, points))


def solution(mesh):
    placed = (
        P(("grp", "wide"), None),
        P(("grp", "wide"), None, None),
        P(("grp", "wide")),
        P(("grp", "wide")),
        P(("grp", "wide")),
        P(("grp", "wide"), None, None),
        P(("grp", "wide"), None, None),
    )
    return jax.shard_map(
        on_device, mesh=mesh, in_specs=placed, out_specs=P(None, ("grp", "wide")), check_vma=False
    )
```

time: 32.2 us -> 28 us (0.87)
  the two profiles are of different devices: /device:TPU:8 before, /device:TPU:0 now
where the time goes in v3:
time: 28 us; the launch traced here: 27.9 us
  starting transfers between devices  11 us (39%)
  Pallas kernels  7.95 us (28%)
  waiting for transfers between devices  7.5 us (27%)
  local copies, waits for them, and re-layouts  1.34 us (5%)
    ppermute x7, starting transfers between devices, moved(): return lax.ppermute(x, axis, [(i, to(i)) for i in range(n)])  11 us
    ppermute x7, waiting for transfers between devices, moved(): return lax.ppermute(x, axis, [(i, to(i)) for i in range(n)])  7.5 us
    pallas_call x1, Pallas kernels, on_device(): pl.pallas_call(prepare, out_shape=(ct, tr, tr, shape((nwide, 8, 128), F32...  3.98 us
    pallas_call x1, Pallas kernels, on_device(): pl.pallas_call(functools.partial(downward, tuple((a.shape[0] for a in arr...  1.98 us
    unnamed x10, local copies, waits for them, and re-layouts  1.32 us
    pallas_call x1, Pallas kernels, on_device(): pl.pallas_call(functools.partial(pick, two_step, last), out_shape=(shape(...  1.1 us
    pallas_call x1, Pallas kernels, on_device(): pl.pallas_call(functools.partial(couple, two_step), out_shape=(half, half...  0.89 us
  transfers between devices with their start and end apart: 7, of which 6 were waited for; matrix products, arithmetic and copies ran while one was open for 0% of the time, Pallas kernels for 18%

profile of v3, /device:TPU:0, one launch (start us, length us, event | category | flops | bytes accessed | tf_op | source)
XLA Modules:
  0.0 27.9 jit_solution(13758292217958537591)
XLA Ops:
  0.0 5.0 %collective-permute-start.1 = (f32[73,512]{1,0:T(8,128)}, f32[73,512]{1,0:T(8,128)S(1)}, u32[]{:S(2)}, u32[]{:S(2)}) collective-permute-start(f32[73,512]{1,0:T(8,128)} %refs_0_.1), channel_id=1, source_target_pairs={{0,24},{8,16},{16,8},{24,0},{1,25},{9,17},{17,9},{25,1},{2,26},{10... | collective-permute-start | bytes 448520 | tf_op jit(solution)/shard_map/ppermute | solution.py:244
  5.0 0.0 collective-permute-start
  5.1 0.0 copy-start.2
  5.1 0.7 %copy-done.2 = s32[64]{0:T(128)S(1)} copy-done((s32[64]{0:T(128)S(1)}, s32[64]{0:T(128)}, u32[]{:S(2)}) %copy-start.2) | copy-done | bytes 280
  5.7 0.0 copy-start.3
  5.7 0.7 %copy-done.3 = s32[8]{0:T(128)S(1)} copy-done((s32[8]{0:T(128)S(1)}, s32[8]{0:T(128)}, u32[]{:S(2)}) %copy-start.3) | copy-done | bytes 56
  6.4 0.0 copy-start.1
  6.4 0.0 copy-start.4
  6.4 4.0 %prepare.1 = (bf16[8,256,256]{2,1,0:T(8,128)(2,1)S(1)}, bf16[576,512]{1,0:T(8,128)(2,1)S(1)}, bf16[576,512]{1,0:T(8,128)(2,1)S(1)}, f32[8,8,128]{2,1,0:T(8,128)S(1)}) custom-call(s32[64]{0:T(128)S(1)} %copy-done.2, s32[8]{0:T(128)S(1)} %copy-done.3, f32[64,64,64]{2,1,0:T(8,128)} %coupling_in.1, f32[64,64,72]{2,1,0:T(8,128)} %bitcast.3), custom_call_target="tpu_custom_call" | custom-call | bytes 10485760 | tf_op jit(solution)/shard_map/prepare/pallas_call | solution.py:227
  10.4 0.0 copy-start
  10.4 0.0 collective-permute-done.1.refs_2_
  10.4 2.3 %collective-permute-start.2 = (f32[73,512]{1,0:T(8,128)S(1)}, f32[73,512]{1,0:T(8,128)S(1)}, u32[]{:S(2)}, u32[]{:S(2)}) collective-permute-start(f32[73,512]{1,0:T(8,128)S(1)} %collective-permute-done.1.refs_2_), channel_id=1, source_target_pairs={{0,8},{8,0},{16,24},{24,16},{1,9},{9,1},{17,25},{25,17},{2,10},{10... | collective-permute-start | bytes 448520 | tf_op jit(solution)/shard_map/ppermute | solution.py:244
  12.7 0.5 %collective-permute-done.refs_1_ = f32[73,512]{1,0:T(8,128)S(1)} collective-permute-done((f32[73,512]{1,0:T(8,128)}, f32[73,512]{1,0:T(8,128)S(1)}, u32[]{:S(2)}, u32[]{:S(2)}) %collective-permute-start) | collective-permute-done | bytes 149536 | tf_op jit(solution)/shard_map/ppermute | solution.py:244
  13.2 0.0 copy-done.1
  13.2 0.0 copy-done.4
  13.2 1.1 %pick.1 = (f32[64,512]{1,0:T(8,128)S(1)}, bf16[64,128]{1,0:T(8,128)(2,1)S(1)}) custom-call(s32[64]{0:T(128)S(1)} %copy-done.4, f32[73,512]{1,0:T(8,128)S(1)} %copy-done.1, f32[73,512]{1,0:T(8,128)S(1)} %collective-permute-done.refs_1_, f32[73,512]{1,0:T(8,128)S(1)} %collective-permute-done.1.refs_2_), custom_call_target="tpu_custom_call" | custom-call | tf_op jit(solution)/shard_map/pick/pallas_call | solution.py:258
  14.3 2.3 %collective-permute-done.2.last = f32[73,512]{1,0:T(8,128)S(1)} collective-permute-done((f32[73,512]{1,0:T(8,128)S(1)}, f32[73,512]{1,0:T(8,128)S(1)}, u32[]{:S(2)}, u32[]{:S(2)}) %collective-permute-start.2) | collective-permute-done | bytes 149536 | tf_op jit(solution)/shard_map/ppermute | solution.py:244
  16.6 0.9 %couple.1 = (f32[4,40,128]{2,1,0:T(8,128)S(1)}, f32[4,40,128]{2,1,0:T(8,128)S(1)}) custom-call(f32[64,512]{1,0:T(8,128)S(1)} %get-tuple-element.17.early, bf16[64,128]{1,0:T(8,128)(2,1)S(1)} %get-tuple-element.18.hot, f32[73,512]{1,0:T(8,128)S(1)} %collective-permute-done.2.last, bf16[8,256,256]{2,1,0:T(8,128)(2,1)S(1)} %get-tuple-element.19.ct, ...), custom_call_target="tpu_custom_call" | custom-call | tf_op jit(solution)/shard_map/couple/pallas_call | solution.py:269
  17.5 0.1 collective-permute-start.3
  17.6 1.2 %collective-permute-done.3 = f32[4,40,128]{2,1,0:T(8,128)S(1)} collective-permute-done((f32[4,40,128]{2,1,0:T(8,128)S(1)}, f32[4,40,128]{2,1,0:T(8,128)S(1)}, u32[]{:S(2)}, u32[]{:S(2)}) %collective-permute-start.3) | collective-permute-done | bytes 81952 | tf_op jit(solution)/shard_map/ppermute | solution.py:244
  18.8 2.5 %collective-permute-start.4 = (f32[2,40,128]{2,1,0:T(8,128)S(1)}, f32[2,40,128]{2,1,0:T(8,128)S(1)}, u32[]{:S(2)}, u32[]{:S(2)}) collective-permute-start(f32[2,40,128]{2,1,0:T(8,128)S(1)} %pad_maximum_fusion), channel_id=1, source_target_pairs={{0,6},{1,7},{2,4},{3,5},{4,2},{5,3},{6,0},{7,1},{8,14},{9,15},{10,... | collective-permute-start | bytes 122888 | tf_op jit(solution)/shard_map/ppermute | solution.py:244
  21.4 0.5 %collective-permute-start.5 = (f32[2,40,128]{2,1,0:T(8,128)S(1)}, f32[2,40,128]{2,1,0:T(8,128)S(1)}, u32[]{:S(2)}, u32[]{:S(2)}) collective-permute-start(f32[2,40,128]{2,1,0:T(8,128)S(1)} %pad_maximum_fusion.1), channel_id=1, source_target_pairs={{0,4},{1,5},{2,6},{3,7},{4,0},{5,1},{6,2},{7,3},{8,12},{9,13},{10,... | collective-permute-start | bytes 122888 | tf_op jit(solution)/shard_map/ppermute | solution.py:244
  21.9 0.5 %collective-permute-start.6 = (f32[2,40,128]{2,1,0:T(8,128)S(1)}, f32[2,40,128]{2,1,0:T(8,128)S(1)}, u32[]{:S(2)}, u32[]{:S(2)}) collective-permute-start(f32[2,40,128]{2,1,0:T(8,128)S(1)} %pad_maximum_fusion.2), channel_id=1, source_target_pairs={{0,2},{1,3},{2,0},{3,1},{4,6},{5,7},{6,4},{7,5},{8,10},{9,11},{10,... | collective-permute-start | bytes 122888 | tf_op jit(solution)/shard_map/ppermute | solution.py:244
  22.4 1.4 %collective-permute-done.4.refs_2_ = f32[2,40,128]{2,1,0:T(8,128)S(1)} collective-permute-done((f32[2,40,128]{2,1,0:T(8,128)S(1)}, f32[2,40,128]{2,1,0:T(8,128)S(1)}, u32[]{:S(2)}, u32[]{:S(2)}) %collective-permute-start.4) | collective-permute-done | bytes 40992 | tf_op jit(solution)/shard_map/ppermute | solution.py:244
  23.8 1.6 %collective-permute-done.5.refs_3_ = f32[2,40,128]{2,1,0:T(8,128)S(1)} collective-permute-done((f32[2,40,128]{2,1,0:T(8,128)S(1)}, f32[2,40,128]{2,1,0:T(8,128)S(1)}, u32[]{:S(2)}, u32[]{:S(2)}) %collective-permute-start.5) | collective-permute-done | bytes 40992 | tf_op jit(solution)/shard_map/ppermute | solution.py:244
  25.4 0.5 %collective-permute-done.6.refs_4_ = f32[2,40,128]{2,1,0:T(8,128)S(1)} collective-permute-done((f32[2,40,128]{2,1,0:T(8,128)S(1)}, f32[2,40,128]{2,1,0:T(8,128)S(1)}, u32[]{:S(2)}, u32[]{:S(2)}) %collective-permute-start.6) | collective-permute-done | bytes 40992 | tf_op jit(solution)/shard_map/ppermute | solution.py:244
  25.9 0.0 copy-done
  25.9 2.0 %downward.1 = f32[8,8192]{1,0:T(8,128)} custom-call(f32[1,40,128]{2,1,0:T(8,128)S(1)} %get-tuple-element.28.refs_0_, f32[1,40,128]{2,1,0:T(8,128)S(1)} %get-tuple-element.32.refs_1_, f32[2,40,128]{2,1,0:T(8,128)S(1)} %collective-permute-done.4.refs_2_, f32[2,40,128]{2,1,0:T(8,128)S(1)} %collective-permute-done.5.refs_3_, ...), custom_call_target="tpu_custom_call" | custom-call | tf_op jit(solution)/shard_map/downward/pallas_call | solution.py:288
  (5 shorter events, 0.0 us)
Async XLA Ops:
  0.0 10.4 %collective-permute-start.1 = (f32[73,512]{1,0:T(8,128)}, f32[73,512]{1,0:T(8,128)S(1)}, u32[]{:S(2)}, u32[]{:S(2)}) collective-permute-start(f32[73,512]{1,0:T(8,128)} %refs_0_.1), channel_id=1, source_target_pairs={{0,24},{8,16},{16,8},{24,0},{1,25},{9,17},{17,9},{25,1},{2,26},{10... | collective-permute-start | bytes 448520 | tf_op jit(solution)/shard_map/ppermute | solution.py:244
  5.0 8.1 %collective-permute-start = (f32[73,512]{1,0:T(8,128)}, f32[73,512]{1,0:T(8,128)S(1)}, u32[]{:S(2)}, u32[]{:S(2)}) collective-permute-start(f32[73,512]{1,0:T(8,128)} %refs_0_.1), channel_id=1, source_target_pairs={{0,8},{8,0},{16,24},{24,16},{1,9},{9,1},{17,25},{25,17},{2,10},{10... | collective-permute-start | bytes 448520 | tf_op jit(solution)/shard_map/ppermute | solution.py:244
  5.1 0.7 %copy-start.2 = (s32[64]{0:T(128)S(1)}, s32[64]{0:T(128)}, u32[]{:S(2)}) copy-start(s32[64]{0:T(128)} %target.1) | copy-start | bytes 772
  5.7 0.7 %copy-start.3 = (s32[8]{0:T(128)S(1)}, s32[8]{0:T(128)}, u32[]{:S(2)}) copy-start(s32[8]{0:T(128)} %counts.1) | copy-start | bytes 100
  6.4 6.8 %copy-start.1 = (f32[73,512]{1,0:T(8,128)S(1)}, f32[73,512]{1,0:T(8,128)}, u32[]{:S(2)}) copy-start(f32[73,512]{1,0:T(8,128)} %refs_0_.1) | copy-start | bytes 448516
  6.4 6.8 %copy-start.4 = (s32[64]{0:T(128)S(1)}, s32[64]{0:T(128)}, u32[]{:S(2)}) copy-start(s32[64]{0:T(128)} %source.1) | copy-start | bytes 772
  10.4 15.5 %copy-start = (f32[64,64,128]{2,1,0:T(8,128)S(1)}, f32[64,64,128]{2,1,0:T(8,128)}, u32[]{:S(2)}) copy-start(f32[64,64,128]{2,1,0:T(8,128)} %param.13) | copy-start | bytes 6291460
  10.4 6.2 %collective-permute-start.2 = (f32[73,512]{1,0:T(8,128)S(1)}, f32[73,512]{1,0:T(8,128)S(1)}, u32[]{:S(2)}, u32[]{:S(2)}) collective-permute-start(f32[73,512]{1,0:T(8,128)S(1)} %collective-permute-done.1.refs_2_), channel_id=1, source_target_pairs={{0,8},{8,0},{16,24},{24,16},{1,9},{9,1},{17,25},{25,17},{2,10},{10... | collective-permute-start | bytes 448520 | tf_op jit(solution)/shard_map/ppermute | solution.py:244
  17.5 1.3 %collective-permute-start.3 = (f32[4,40,128]{2,1,0:T(8,128)S(1)}, f32[4,40,128]{2,1,0:T(8,128)S(1)}, u32[]{:S(2)}, u32[]{:S(2)}) collective-permute-start(f32[4,40,128]{2,1,0:T(8,128)S(1)} %get-tuple-element.22), channel_id=1, source_target_pairs={{0,1},{1,0},{2,3},{3,2},{4,5},{5,4},{6,7},{7,6},{8,9},{9,8},{10,11... | collective-permute-start | bytes 245768 | tf_op jit(solution)/shard_map/ppermute | solution.py:244
  18.8 5.0 %collective-permute-start.4 = (f32[2,40,128]{2,1,0:T(8,128)S(1)}, f32[2,40,128]{2,1,0:T(8,128)S(1)}, u32[]{:S(2)}, u32[]{:S(2)}) collective-permute-start(f32[2,40,128]{2,1,0:T(8,128)S(1)} %pad_maximum_fusion), channel_id=1, source_target_pairs={{0,6},{1,7},{2,4},{3,5},{4,2},{5,3},{6,0},{7,1},{8,14},{9,15},{10,... | collective-permute-start | bytes 122888 | tf_op jit(solution)/shard_map/ppermute | solution.py:244
  21.4 4.0 %collective-permute-start.5 = (f32[2,40,128]{2,1,0:T(8,128)S(1)}, f32[2,40,128]{2,1,0:T(8,128)S(1)}, u32[]{:S(2)}, u32[]{:S(2)}) collective-permute-start(f32[2,40,128]{2,1,0:T(8,128)S(1)} %pad_maximum_fusion.1), channel_id=1, source_target_pairs={{0,4},{1,5},{2,6},{3,7},{4,0},{5,1},{6,2},{7,3},{8,12},{9,13},{10,... | collective-permute-start | bytes 122888 | tf_op jit(solution)/shard_map/ppermute | solution.py:244
  21.9 4.0 %collective-permute-start.6 = (f32[2,40,128]{2,1,0:T(8,128)S(1)}, f32[2,40,128]{2,1,0:T(8,128)S(1)}, u32[]{:S(2)}, u32[]{:S(2)}) collective-permute-start(f32[2,40,128]{2,1,0:T(8,128)S(1)} %pad_maximum_fusion.2), channel_id=1, source_target_pairs={{0,2},{1,3},{2,0},{3,1},{4,6},{5,7},{6,4},{7,5},{8,10},{9,11},{10,... | collective-permute-start | bytes 122888 | tf_op jit(solution)/shard_map/ppermute | solution.py:244

commit v4 on v3

--- a/solution.py
+++ b/solution.py
@@ -26,11 +26,10 @@
     return jnp.dot(a, b, preferred_element_type=F32)
 
 
-def product3(x, high_ref_value, low_ref_value):
-    rows = x.shape[0]
-    high, low = split(x)
-    both = mm(jnp.concatenate([high, low], axis=0), high_ref_value)
-    return both[:rows] + both[rows:] + mm(high, low_ref_value)
+def product3(x, weights):
+    rows, columns = x.shape[0], weights.shape[1] // 2
+    both = mm(jnp.concatenate(split(x), axis=0), weights)
+    return both[:rows, :columns] + (both[:rows, columns:] + both[rows:, :columns])
 
 
 def iota(shape, dim):
@@ -40,7 +39,7 @@
 CHUNKS = 4
 
 
-def prepare(target, counts, coupling_in, transfer_in, ct, t_h, t_l, code, coupling, transfer, turned, sems):
+def prepare(target, counts, coupling_in, transfer_in, ct, tr, code, coupling, transfer, turned, sems):
     nwide = code.shape[0]
     ncl = transfer.shape[2]
 
@@ -73,8 +72,8 @@
     for g in range(1 + BRANCH):
         rows = [turned[pl.ds(BRANCH * g + c, RANK, stride=ncl), :] for c in range(BRANCH)]
         high, low = split(jnp.concatenate(rows, axis=0).T)
-        t_h[RANK * g : RANK * (g + 1), :] = high
-        t_l[RANK * g : RANK * (g + 1), :] = low
+        tr[RANK * g : RANK * (g + 1), : BRANCH * RANK] = high
+        tr[RANK * g : RANK * (g + 1), BRANCH * RANK :] = low
 
     def turn(p, carry):
         for s in range(HALF):
@@ -110,8 +109,7 @@
     hot[...] = jnp.concatenate(marks, axis=0).astype(BF)
 
 
-def couple(two_step, early, hot, last, ct, code, same, other, held_a, held_b):
-    nwide = code.shape[0]
+def couple(two_step, early, hot, last, ct, code, other, held_a, held_b):
     nblocks, width = early.shape
     ncl = last.shape[0]
     wide = lax.axis_index("wide") if two_step else 0
@@ -134,24 +132,27 @@
             rows = pl.ds(2 * s + i, nblocks, stride=RHS)
             held_a[rows, :] = jnp.where(own == 0, x, 0.0)
             held_b[rows, :] = jnp.where(own == 2, x, 0.0)
+    towards(1, wide, 2 if two_step else 0, held_a, held_b, ct, code, other)
+
+
+def couple_more(two_step, held_a, held_b, ct, code, same):
+    towards(0, lax.axis_index("wide") if two_step else 0, 0, held_a, held_b, ct, code, same)
+
+
+def towards(parity, wide, shift, held_a, held_b, ct, code, out):
     left = iota((32, 128), 1) < RANK
-    for p in range(nwide):
-        peer = p ^ wide
+    for p in range(out.shape[0]):
+        peer = (2 * p + parity) ^ wide
         at = pl.ds(pl.multiple_of(peer * 64, 64), 64)
-        high, low = split(jnp.concatenate([held_a[at, :], held_b[at, :]], axis=1))
-        z = mm(jnp.concatenate([high, low], axis=0), ct[peer])
-        z = z[:64, :128] + (z[:64, 128:] + z[64:, :128])
-        out = other if p % 2 else same
-        out[p // 2, :32, :] = jnp.where(left, z[:32], z[32:])
-        out[p // 2, 32:, :] = code[peer]
-
-
-def downward(counts, *refs):
-    arrays, (t_h, t_l, basis, out, full) = refs[: len(counts)], refs[len(counts) :]
-    arrived = [array.at[i] for array, count in zip(arrays, counts) for i in range(count)]
-    nwide = len(arrived)
-    ncl = full.shape[0] // RHS
-    value = jnp.concatenate([arrived[p][:32, :] for p in range(nwide)], axis=0)
+        z = product3(jnp.concatenate([held_a[at, :], held_b[at, :]], axis=1), ct[peer])
+        out[p, :32, :] = jnp.where(left, z[:32], z[32:])
+        out[p, 32:, :] = pltpu.roll(code[peer], shift, 0) if shift else code[peer]
+
+
+def downward(messages, sets, *refs):
+    arrived, (tr, basis, out, full, held, sems) = refs[:messages], refs[messages:]
+    nwide = messages * sets
+    value = jnp.concatenate([message[: 32 * sets, :] for message in arrived], axis=0)
     high, low = split(value)
     weights = jnp.concatenate([high, low], axis=1)
     lane = iota((1, 128), 1)
@@ -159,9 +160,11 @@
     for h in range(2):
         parts = []
         for q in range(nwide // 4):
-            part = arrived[4 * q][32 + h : 33 + h, :]
-            for e in range(1, 4):
-                part = jnp.where(lane // 32 == e, arrived[4 * q + e][32 + h : 33 + h, :], part)
+            part = None
+            for e in range(4):
+                at = 32 * sets + 2 * (e % sets) + h
+                row = arrived[(4 * q + e) // sets][at : at + 1, :]
+                part = row if part is None else jnp.where(lane // 32 == e, row, part)
             parts.append(part)
         codes.append(jnp.concatenate(parts, axis=1).astype(jnp.int32))
     total = full.shape[0]
@@ -192,20 +195,26 @@
     def spread(x):
         return jnp.where(diagonal, jnp.concatenate([x] * 4, axis=0), 0.0)
 
+    copies = []
     top = full[:RHS, :RANK]
-    middle = pairs(1, BRANCH) + product3(top, t_h[:RANK, :], t_l[:RANK, :])
+    middle = pairs(1, BRANCH) + product3(top, tr[:RANK, :])
     for g in range(2):
         at = slice(RANK + 256 * g, RANK + 256 * (g + 1))
-        down = product3(spread(middle[:, 256 * g : 256 * (g + 1)]), t_h[at, :], t_l[at, :])
+        down = product3(spread(middle[:, 256 * g : 256 * (g + 1)]), tr[at, :])
         for c4 in range(4):
             c = 4 * g + c4
             leaves = pairs(1 + BRANCH + BRANCH * c, BRANCH) + down[RHS * c4 : RHS * (c4 + 1), :]
             for half in range(2):
                 j = BRANCH * c + 4 * half
                 rows = slice(RANK * j, RANK * (j + 4))
-                far = product3(spread(leaves[:, 256 * half : 256 * (half + 1)]), *split(basis[rows, :]))
+                far = product3(spread(leaves[:, 256 * half : 256 * (half + 1)]), jnp.concatenate(split(basis[rows, :]), axis=1))
                 for l4 in range(4):
-                    out[:, 128 * (j + l4) : 128 * (j + l4 + 1)] = far[RHS * l4 : RHS * (l4 + 1), :]
+                    held[:, 128 * (j + l4) : 128 * (j + l4 + 1)] = far[RHS * l4 : RHS * (l4 + 1), :]
+            at = pl.ds(128 * BRANCH * c, 128 * BRANCH)
+            copies.append(pltpu.make_async_copy(held.at[:, at], out.at[:, at], sems.at[c]))
+            copies[-1].start()
+    for copy in copies:
+        copy.wait()
 
 
 VMEM = pl.BlockSpec(memory_space=pltpu.VMEM)
@@ -222,13 +231,13 @@
 
     shape = jax.ShapeDtypeStruct
     ct = shape((nwide, 4 * rank, 4 * rank), BF)
-    tr = shape(((1 + BRANCH) * rank, BRANCH * rank), BF)
+    tr = shape(((1 + BRANCH) * rank, 2 * BRANCH * rank), BF)
     turned = jnp.transpose(transfer, (1, 2, 0))
-    ct, t_h, t_l, code = pl.pallas_call(
+    ct, tr, code = pl.pallas_call(
         prepare,
-        out_shape=(ct, tr, tr, shape((nwide, 8, 128), F32)),
+        out_shape=(ct, tr, shape((nwide, 8, 128), F32)),
         in_specs=[SMEM, SMEM, ANY, ANY],
-        out_specs=(VMEM,) * 4,
+        out_specs=(VMEM,) * 3,
         scratch_shapes=[
             pltpu.VMEM(coupling.shape, F32),
             pltpu.VMEM(turned.shape, F32),
@@ -266,34 +275,51 @@
     )(source, *tables[:last], *tables[last + 1 :])
 
     half = shape((nwide // 2, 40, 128), F32)
-    same, other = pl.pallas_call(
+    spread = shape((nblocks * RHS, 128), F32)
+    other, held_a, held_b = pl.pallas_call(
         functools.partial(couple, two_step),
-        out_shape=(half, half),
+        out_shape=(half, spread, spread),
         in_specs=[VMEM] * 5,
-        out_specs=(VMEM, VMEM),
-        scratch_shapes=[pltpu.VMEM((nblocks * RHS, 128), F32)] * 2,
+        out_specs=(VMEM,) * 3,
         compiler_params=pltpu.CompilerParams(vmem_limit_bytes=32 << 20),
         name="couple",
     )(early, hot, tables[last], ct, code)
+    same = pl.pallas_call(
+        functools.partial(couple_more, two_step),
+        out_shape=half,
+        in_specs=[VMEM] * 4,
+        out_specs=VMEM,
+        compiler_params=pltpu.CompilerParams(vmem_limit_bytes=16 << 20),
+        cost_estimate=pl.CostEstimate(flops=0, bytes_accessed=4 << 20, transcendentals=0),
+        name="couple_more",
+    )(held_a, held_b, ct, code)
 
     if two_step:
         mate = moved(other, "wide", nwide, lambda i: i ^ 1)
-        arrived = [same[:1], mate[:1]]
-        for k in (3, 2, 1):
-            arrived.append(moved(jnp.stack([same[k], mate[k]]), "wide", nwide, lambda i: i ^ (2 * k)))
+        both = jnp.concatenate([same[:, :32], mate[:, :32], same[:, 32:] + mate[:, 32:]], axis=1)
+        arrived = [both[0]]
+        for k in (1, 2, 3):
+            arrived.append(moved(both[k], "wide", nwide, lambda i: i ^ (2 * k)))
+        sets = 2
     else:
         payload = jnp.stack([same, other], axis=1).reshape(nwide, 40, 128)
-        arrived = [lax.all_to_all(payload, "wide", split_axis=0, concat_axis=0, tiled=True)]
+        payload = lax.all_to_all(payload, "wide", split_axis=0, concat_axis=0, tiled=True)
+        arrived = [payload[p] for p in range(nwide)]
+        sets = 1
 
     return pl.pallas_call(
-        functools.partial(downward, tuple(a.shape[0] for a in arrived)),
+        functools.partial(downward, len(arrived), sets),
         out_shape=shape((RHS, nleaf * points), F32),
-        in_specs=[VMEM] * (len(arrived) + 3),
-        out_specs=VMEM,
-        scratch_shapes=[pltpu.VMEM((ncl * RHS, 128), F32)],
+        in_specs=[VMEM] * (len(arrived) + 2),
+        out_specs=ANY,
+        scratch_shapes=[
+            pltpu.VMEM((ncl * RHS, 128), F32),
+            pltpu.VMEM((RHS, nleaf * points), F32),
+            pltpu.SemaphoreType.DMA((BRANCH,)),
+        ],
         compiler_params=pltpu.CompilerParams(vmem_limit_bytes=32 << 20),
         name="downward",
-    )(*arrived, t_h, t_l, basis.reshape(nleaf * rank, points))
+    )(*arrived, tr, basis.reshape(nleaf * rank, points))
 
 
 def solution(mesh):

time: 28 us -> 27.9 us (level)
  waiting for transfers between devices: 7.5 us -> 7.19 us
    ppermute x7, waiting for transfers between devices: 7.5 us -> 7.19 us  [moved(): return lax.ppermute(x, axis, [(i, to(i)) for i in range(n)])]
    pallas_call x3 -> x4, Pallas kernels: 6.85 us -> 6.99 us  [the longest x1 3.98 us: on_device(): pl.pallas_call(prepare, out_shape=(ct, tr, shape((nwide, 8, 128), F32)),...]
  transfers between devices with their start and end apart: 7 -> 7, of which waited for: 6 -> 6; matrix products, arithmetic and copies ran while one was open for 0% -> 0% of each run, Pallas kernels for 18% -> 19%
where the time goes in v4:
time: 27.9 us; the launch traced here: 27.7 us
  starting transfers between devices  11 us (39%)
  Pallas kernels  8.09 us (29%)
  waiting for transfers between devices  7.19 us (26%)
  local copies, waits for them, and re-layouts  1.35 us (5%)
    ppermute x7, starting transfers between devices, moved(): return lax.ppermute(x, axis, [(i, to(i)) for i in range(n)])  11 us
    ppermute x7, waiting for transfers between devices, moved(): return lax.ppermute(x, axis, [(i, to(i)) for i in range(n)])  7.19 us
    pallas_call x1, Pallas kernels, on_device(): pl.pallas_call(prepare, out_shape=(ct, tr, shape((nwide, 8, 128), F32)),...  3.98 us
    pallas_call x1, Pallas kernels, on_device(): pl.pallas_call(functools.partial(downward, len(arrived), sets), out_shape...  1.97 us
    unnamed x10, local copies, waits for them, and re-layouts  1.32 us
    pallas_call x1, Pallas kernels, on_device(): pl.pallas_call(functools.partial(pick, two_step, last), out_shape=(shape(...  1.1 us
    pallas_call x1, Pallas kernels, on_device(): pl.pallas_call(functools.partial(couple, two_step), out_shape=(half, spre...  0.8 us
  transfers between devices with their start and end apart: 7, of which 6 were waited for; matrix products, arithmetic and copies ran while one was open for 0% of the time, Pallas kernels for 19%

profile of v4, /device:TPU:0, one launch (start us, length us, event | category | flops | bytes accessed | tf_op | source)
XLA Modules:
  0.0 27.7 jit_solution(8494069548517472126)
XLA Ops:
  0.0 5.0 %collective-permute-start.1 = (f32[73,512]{1,0:T(8,128)}, f32[73,512]{1,0:T(8,128)S(1)}, u32[]{:S(2)}, u32[]{:S(2)}) collective-permute-start(f32[73,512]{1,0:T(8,128)} %refs_0_.1), channel_id=1, source_target_pairs={{0,24},{8,16},{16,8},{24,0},{1,25},{9,17},{17,9},{25,1},{2,26},{10... | collective-permute-start | bytes 448520 | tf_op jit(solution)/shard_map/ppermute | solution.py:253
  5.0 0.0 collective-permute-start
  5.1 0.0 copy-start.2
  5.1 0.7 %copy-done.2 = s32[64]{0:T(128)S(1)} copy-done((s32[64]{0:T(128)S(1)}, s32[64]{0:T(128)}, u32[]{:S(2)}) %copy-start.2) | copy-done | bytes 280
  5.7 0.0 copy-start.3
  5.7 0.7 %copy-done.3 = s32[8]{0:T(128)S(1)} copy-done((s32[8]{0:T(128)S(1)}, s32[8]{0:T(128)}, u32[]{:S(2)}) %copy-start.3) | copy-done | bytes 56
  6.4 0.0 copy-start.1
  6.4 0.0 copy-start.4
  6.4 4.0 %prepare.1 = (bf16[8,256,256]{2,1,0:T(8,128)(2,1)S(1)}, bf16[576,1024]{1,0:T(8,128)(2,1)S(1)}, f32[8,8,128]{2,1,0:T(8,128)S(1)}) custom-call(s32[64]{0:T(128)S(1)} %copy-done.2, s32[8]{0:T(128)S(1)} %copy-done.3, f32[64,64,64]{2,1,0:T(8,128)} %coupling_in.1, f32[64,64,72]{2,1,0:T(8,128)} %bitcast.11), custom_call_target="tpu_custom_call" | custom-call | bytes 10485760 | tf_op jit(solution)/shard_map/prepare/pallas_call | solution.py:236
  10.4 0.0 collective-permute-done.1.refs_2_
  10.4 2.3 %collective-permute-start.2 = (f32[73,512]{1,0:T(8,128)S(1)}, f32[73,512]{1,0:T(8,128)S(1)}, u32[]{:S(2)}, u32[]{:S(2)}) collective-permute-start(f32[73,512]{1,0:T(8,128)S(1)} %collective-permute-done.1.refs_2_), channel_id=1, source_target_pairs={{0,8},{8,0},{16,24},{24,16},{1,9},{9,1},{17,25},{25,17},{2,10},{10... | collective-permute-start | bytes 448520 | tf_op jit(solution)/shard_map/ppermute | solution.py:253
  12.7 0.5 %collective-permute-done.refs_1_ = f32[73,512]{1,0:T(8,128)S(1)} collective-permute-done((f32[73,512]{1,0:T(8,128)}, f32[73,512]{1,0:T(8,128)S(1)}, u32[]{:S(2)}, u32[]{:S(2)}) %collective-permute-start) | collective-permute-done | bytes 149536 | tf_op jit(solution)/shard_map/ppermute | solution.py:253
  13.2 0.0 copy-done.1
  13.2 0.0 copy-done.4
  13.2 1.1 %pick.1 = (f32[64,512]{1,0:T(8,128)S(1)}, bf16[64,128]{1,0:T(8,128)(2,1)S(1)}) custom-call(s32[64]{0:T(128)S(1)} %copy-done.4, f32[73,512]{1,0:T(8,128)S(1)} %copy-done.1, f32[73,512]{1,0:T(8,128)S(1)} %collective-permute-done.refs_1_, f32[73,512]{1,0:T(8,128)S(1)} %collective-permute-done.1.refs_2_), custom_call_target="tpu_custom_call" | custom-call | tf_op jit(solution)/shard_map/pick/pallas_call | solution.py:267
  14.3 0.0 copy-start
  14.3 2.3 %collective-permute-done.2.last = f32[73,512]{1,0:T(8,128)S(1)} collective-permute-done((f32[73,512]{1,0:T(8,128)S(1)}, f32[73,512]{1,0:T(8,128)S(1)}, u32[]{:S(2)}, u32[]{:S(2)}) %collective-permute-start.2) | collective-permute-done | bytes 149536 | tf_op jit(solution)/shard_map/ppermute | solution.py:253
  16.6 0.8 %couple.1 = (f32[4,40,128]{2,1,0:T(8,128)S(1)}, f32[512,128]{1,0:T(8,128)S(1)}, f32[512,128]{1,0:T(8,128)S(1)}) custom-call(f32[64,512]{1,0:T(8,128)S(1)} %get-tuple-element.17.early, bf16[64,128]{1,0:T(8,128)(2,1)S(1)} %get-tuple-element.18.hot, f32[73,512]{1,0:T(8,128)S(1)} %collective-permute-done.2.last, bf16[8,256,256]{2,1,0:T(8,128)(2,1)S(1)} %get-tuple-element.19.ct, ...), custom_call_target="tpu_custom_call" | custom-call | tf_op jit(solution)/shard_map/couple/pallas_call | solution.py:279
  17.4 0.1 collective-permute-start.3
  17.5 0.2 couple_more.1
  17.7 1.0 %collective-permute-done.3 = f32[4,40,128]{2,1,0:T(8,128)S(1)} collective-permute-done((f32[4,40,128]{2,1,0:T(8,128)S(1)}, f32[4,40,128]{2,1,0:T(8,128)S(1)}, u32[]{:S(2)}, u32[]{:S(2)}) %collective-permute-start.3) | collective-permute-done | bytes 81952 | tf_op jit(solution)/shard_map/ppermute | solution.py:253
  18.8 2.5 %collective-permute-start.6 = (f32[72,128]{1,0:T(8,128)S(1)}, f32[72,128]{1,0:T(8,128)S(1)}, u32[]{:S(2)}, u32[]{:S(2)}) collective-permute-start(f32[72,128]{1,0:T(8,128)S(1)} %get-tuple-element.25), channel_id=1, source_target_pairs={{0,6},{1,7},{2,4},{3,5},{4,2},{5,3},{6,0},{7,1},{8,14},{9,15},{10,... | collective-permute-start | bytes 110600 | tf_op jit(solution)/shard_map/ppermute | solution.py:253
  21.3 0.5 %collective-permute-start.5 = (f32[72,128]{1,0:T(8,128)S(1)}, f32[72,128]{1,0:T(8,128)S(1)}, u32[]{:S(2)}, u32[]{:S(2)}) collective-permute-start(f32[72,128]{1,0:T(8,128)S(1)} %get-tuple-element.26), channel_id=1, source_target_pairs={{0,4},{1,5},{2,6},{3,7},{4,0},{5,1},{6,2},{7,3},{8,12},{9,13},{10,... | collective-permute-start | bytes 110600 | tf_op jit(solution)/shard_map/ppermute | solution.py:253
  21.8 0.5 %collective-permute-start.4 = (f32[72,128]{1,0:T(8,128)S(1)}, f32[72,128]{1,0:T(8,128)S(1)}, u32[]{:S(2)}, u32[]{:S(2)}) collective-permute-start(f32[72,128]{1,0:T(8,128)S(1)} %get-tuple-element.27), channel_id=1, source_target_pairs={{0,2},{1,3},{2,0},{3,1},{4,6},{5,7},{6,4},{7,5},{8,10},{9,11},{10,... | collective-permute-start | bytes 110600 | tf_op jit(solution)/shard_map/ppermute | solution.py:253
  22.3 1.4 %collective-permute-done.6.refs_3_ = f32[72,128]{1,0:T(8,128)S(1)} collective-permute-done((f32[72,128]{1,0:T(8,128)S(1)}, f32[72,128]{1,0:T(8,128)S(1)}, u32[]{:S(2)}, u32[]{:S(2)}) %collective-permute-start.6) | collective-permute-done | bytes 36896 | tf_op jit(solution)/shard_map/ppermute | solution.py:253
  23.7 1.5 %collective-permute-done.5.refs_2_ = f32[72,128]{1,0:T(8,128)S(1)} collective-permute-done((f32[72,128]{1,0:T(8,128)S(1)}, f32[72,128]{1,0:T(8,128)S(1)}, u32[]{:S(2)}, u32[]{:S(2)}) %collective-permute-start.5) | collective-permute-done | bytes 36896 | tf_op jit(solution)/shard_map/ppermute | solution.py:253
  25.3 0.5 %collective-permute-done.4.refs_1_ = f32[72,128]{1,0:T(8,128)S(1)} collective-permute-done((f32[72,128]{1,0:T(8,128)S(1)}, f32[72,128]{1,0:T(8,128)S(1)}, u32[]{:S(2)}, u32[]{:S(2)}) %collective-permute-start.4) | collective-permute-done | bytes 36896 | tf_op jit(solution)/shard_map/ppermute | solution.py:253
  25.8 0.0 copy-done
  25.8 2.0 %downward.1 = f32[8,8192]{1,0:T(8,128)} custom-call(f32[72,128]{1,0:T(8,128)S(1)} %get-tuple-element.28.refs_0_, f32[72,128]{1,0:T(8,128)S(1)} %collective-permute-done.4.refs_1_, f32[72,128]{1,0:T(8,128)S(1)} %collective-permute-done.5.refs_2_, f32[72,128]{1,0:T(8,128)S(1)} %collective-permute-done.6.refs_3_, ...), custom_call_target="tpu_custom_call" | custom-call | tf_op jit(solution)/shard_map/downward/pallas_call | solution.py:310
  (5 shorter events, 0.0 us)
Async XLA Ops:
  0.0 10.4 %collective-permute-start.1 = (f32[73,512]{1,0:T(8,128)}, f32[73,512]{1,0:T(8,128)S(1)}, u32[]{:S(2)}, u32[]{:S(2)}) collective-permute-start(f32[73,512]{1,0:T(8,128)} %refs_0_.1), channel_id=1, source_target_pairs={{0,24},{8,16},{16,8},{24,0},{1,25},{9,17},{17,9},{25,1},{2,26},{10... | collective-permute-start | bytes 448520 | tf_op jit(solution)/shard_map/ppermute | solution.py:253
  5.0 8.1 %collective-permute-start = (f32[73,512]{1,0:T(8,128)}, f32[73,512]{1,0:T(8,128)S(1)}, u32[]{:S(2)}, u32[]{:S(2)}) collective-permute-start(f32[73,512]{1,0:T(8,128)} %refs_0_.1), channel_id=1, source_target_pairs={{0,8},{8,0},{16,24},{24,16},{1,9},{9,1},{17,25},{25,17},{2,10},{10... | collective-permute-start | bytes 448520 | tf_op jit(solution)/shard_map/ppermute | solution.py:253
  5.1 0.7 %copy-start.2 = (s32[64]{0:T(128)S(1)}, s32[64]{0:T(128)}, u32[]{:S(2)}) copy-start(s32[64]{0:T(128)} %target.1) | copy-start | bytes 772
  5.7 0.7 %copy-start.3 = (s32[8]{0:T(128)S(1)}, s32[8]{0:T(128)}, u32[]{:S(2)}) copy-start(s32[8]{0:T(128)} %counts.1) | copy-start | bytes 100
  6.4 6.8 %copy-start.1 = (f32[73,512]{1,0:T(8,128)S(1)}, f32[73,512]{1,0:T(8,128)}, u32[]{:S(2)}) copy-start(f32[73,512]{1,0:T(8,128)} %refs_0_.1) | copy-start | bytes 448516
  6.4 6.8 %copy-start.4 = (s32[64]{0:T(128)S(1)}, s32[64]{0:T(128)}, u32[]{:S(2)}) copy-start(s32[64]{0:T(128)} %source.1) | copy-start | bytes 772
  10.4 6.2 %collective-permute-start.2 = (f32[73,512]{1,0:T(8,128)S(1)}, f32[73,512]{1,0:T(8,128)S(1)}, u32[]{:S(2)}, u32[]{:S(2)}) collective-permute-start(f32[73,512]{1,0:T(8,128)S(1)} %collective-permute-done.1.refs_2_), channel_id=1, source_target_pairs={{0,8},{8,0},{16,24},{24,16},{1,9},{9,1},{17,25},{25,17},{2,10},{10... | collective-permute-start | bytes 448520 | tf_op jit(solution)/shard_map/ppermute | solution.py:253
  14.3 11.5 %copy-start = (f32[64,64,128]{2,1,0:T(8,128)S(1)}, f32[64,64,128]{2,1,0:T(8,128)}, u32[]{:S(2)}) copy-start(f32[64,64,128]{2,1,0:T(8,128)} %param.13) | copy-start | bytes 6291460
  17.4 1.3 %collective-permute-start.3 = (f32[4,40,128]{2,1,0:T(8,128)S(1)}, f32[4,40,128]{2,1,0:T(8,128)S(1)}, u32[]{:S(2)}, u32[]{:S(2)}) collective-permute-start(f32[4,40,128]{2,1,0:T(8,128)S(1)} %get-tuple-element.23), channel_id=1, source_target_pairs={{0,1},{1,0},{2,3},{3,2},{4,5},{5,4},{6,7},{7,6},{8,9},{9,8},{10,11... | collective-permute-start | bytes 245768 | tf_op jit(solution)/shard_map/ppermute | solution.py:253
  18.8 4.9 %collective-permute-start.6 = (f32[72,128]{1,0:T(8,128)S(1)}, f32[72,128]{1,0:T(8,128)S(1)}, u32[]{:S(2)}, u32[]{:S(2)}) collective-permute-start(f32[72,128]{1,0:T(8,128)S(1)} %get-tuple-element.25), channel_id=1, source_target_pairs={{0,6},{1,7},{2,4},{3,5},{4,2},{5,3},{6,0},{7,1},{8,14},{9,15},{10,... | collective-permute-start | bytes 110600 | tf_op jit(solution)/shard_map/ppermute | solution.py:253
  21.3 4.0 %collective-permute-start.5 = (f32[72,128]{1,0:T(8,128)S(1)}, f32[72,128]{1,0:T(8,128)S(1)}, u32[]{:S(2)}, u32[]{:S(2)}) collective-permute-start(f32[72,128]{1,0:T(8,128)S(1)} %get-tuple-element.26), channel_id=1, source_target_pairs={{0,4},{1,5},{2,6},{3,7},{4,0},{5,1},{6,2},{7,3},{8,12},{9,13},{10,... | collective-permute-start | bytes 110600 | tf_op jit(solution)/shard_map/ppermute | solution.py:253
  21.8 4.0 %collective-permute-start.4 = (f32[72,128]{1,0:T(8,128)S(1)}, f32[72,128]{1,0:T(8,128)S(1)}, u32[]{:S(2)}, u32[]{:S(2)}) collective-permute-start(f32[72,128]{1,0:T(8,128)S(1)} %get-tuple-element.27), channel_id=1, source_target_pairs={{0,2},{1,3},{2,0},{3,1},{4,6},{5,7},{6,4},{7,5},{8,10},{9,11},{10,... | collective-permute-start | bytes 110600 | tf_op jit(solution)/shard_map/ppermute | solution.py:253

commit v5 on v4

--- a/solution.py
+++ b/solution.py
@@ -39,8 +39,8 @@
 CHUNKS = 4
 
 
-def prepare(target, counts, coupling_in, transfer_in, ct, tr, code, coupling, transfer, turned, sems):
-    nwide = code.shape[0]
+def prepare(coupling_in, transfer_in, ct, tr, coupling, transfer, turned, sems):
+    nwide = ct.shape[0]
     ncl = transfer.shape[2]
 
     def chunks(source, held, at):
@@ -54,17 +54,6 @@
     for copy in first + second:
         copy.start()
 
-    def codes(p, carry):
-        row, lane = iota((8, 128), 0), iota((8, 128), 1)
-        value = jnp.zeros((8, 128), jnp.int32)
-        for slot in range(SLOTS):
-            here = (row == slot // HALF) & ((lane % 32) // RHS == slot % HALF)
-            at = jnp.where(slot < counts[p], target[SLOTS * p + slot] * RHS, -RHS)
-            value = jnp.where(here, at + lane % RHS, value)
-        code[p] = value.astype(F32)
-        return carry
-
-    lax.fori_loop(0, nwide, codes, 0)
     for i in range(RANK):
         if i % (RANK // CHUNKS) == 0:
             first[i // (RANK // CHUNKS)].wait()
@@ -88,33 +77,50 @@
         lax.fori_loop(nwide // CHUNKS * k, nwide // CHUNKS * (k + 1), turn, 0, unroll=2)
 
 
-def pick(two_step, last, source, *refs):
-    tables, (early, hot, rows) = refs[:-3], refs[-3:]
-    ntab = len(tables) + 1
-    ncl = tables[0].shape[0]
+def pick(two_step, source, target, counts, *refs):
+    tables, (early, code, rows) = refs[:-3], refs[-3:]
+    nmember, ncl = rows.shape[:2]
+    nmember = nmember + 1 if two_step else nmember
     grp = lax.axis_index("grp")
     for k, table in enumerate(tables):
         rows[k] = table[...]
-    rows[ntab - 1] = jnp.zeros(rows.shape[1:], F32)
-    lane = iota((1, 128), 1)
-    marks = []
+    if two_step:
+        rows[2] = jnp.zeros(rows.shape[1:], F32)
     for b in range(early.shape[0]):
         at = source[b]
-        member = sum(jnp.where(at >= ncl * k, 1, 0) for k in range(1, ntab))
-        table = member ^ grp if two_step else lax.rem(grp - member + ntab, ntab)
-        held = jnp.where(table == last, ntab - 1, table - jnp.where(table > last, 1, 0))
-        local = at - ncl * member
-        early[b : b + 1, :] = rows[held, pl.ds(local, 1), :]
-        marks.append(jnp.where(lane == jnp.where(table == last, local, -1), 1.0, 0.0))
-    hot[...] = jnp.concatenate(marks, axis=0).astype(BF)
-
-
-def couple(two_step, early, hot, last, ct, code, other, held_a, held_b):
-    nblocks, width = early.shape
-    ncl = last.shape[0]
+        member = sum(jnp.where(at >= ncl * k, 1, 0) for k in range(1, nmember))
+        if two_step:
+            apart = member ^ grp
+            table = jnp.where(apart == 0, 0, jnp.where(apart == 3, 1, 2))
+        else:
+            table = lax.rem(grp - member + nmember, nmember)
+        early[b : b + 1, :] = rows[table, pl.ds(at - ncl * member, 1), :]
+    row, lane = iota((8, 128), 0), iota((8, 128), 1)
+    for p in range(code.shape[0]):
+        value = jnp.zeros((8, 128), jnp.int32)
+        for slot in range(SLOTS):
+            here = (row == slot // HALF) & ((lane % 32) // RHS == slot % HALF)
+            at = jnp.where(slot < counts[p], target[SLOTS * p + slot] * RHS, -RHS)
+            value = jnp.where(here, at + lane % RHS, value)
+        code[p] = value.astype(F32)
+
+
+def relay(theirs, own, far, out):
+    ncl, width = own.shape
+    grp = lax.axis_index("grp")
+    row = iota((128, theirs.shape[1]), 0)
+    hot = jnp.concatenate([theirs[...] - ncl * grp == row, theirs[...] - ncl * (grp ^ 3) == row], axis=0)
+    hot = jnp.where(hot, 1.0, 0.0).T.astype(BF)
+    none = jnp.zeros((128 - ncl, width), F32)
+    high, low = split(jnp.concatenate([own[...], none, far[...], none], axis=0))
+    out[...] = mm(hot, high) + mm(hot, low)
+
+
+def couple(two_step, parts, *refs):
+    early, (ct, code, other, held_a, held_b) = refs[:parts], refs[parts:]
+    nblocks, width = early[0].shape
     wide = lax.axis_index("wide") if two_step else 0
-    high, low = split(jnp.concatenate([last[...], jnp.zeros((128 - ncl, width), F32)], axis=0))
-    picked = early[...] + (mm(hot[...], high) + mm(hot[...], low))
+    picked = sum(part[...] for part in early)
     place, to = iota((width, 256), 0), iota((width, 256), 1)
     turn = (place // RHS == to % RANK) & (place % RHS // 2 == to // RANK)
     turn = jnp.where(turn, 1.0, 0.0).astype(BF)
@@ -233,11 +239,11 @@
     ct = shape((nwide, 4 * rank, 4 * rank), BF)
     tr = shape(((1 + BRANCH) * rank, 2 * BRANCH * rank), BF)
     turned = jnp.transpose(transfer, (1, 2, 0))
-    ct, tr, code = pl.pallas_call(
+    ct, tr = pl.pallas_call(
         prepare,
-        out_shape=(ct, tr, shape((nwide, 8, 128), F32)),
-        in_specs=[SMEM, SMEM, ANY, ANY],
-        out_specs=(VMEM,) * 3,
+        out_shape=(ct, tr),
+        in_specs=[ANY, ANY],
+        out_specs=(VMEM,) * 2,
         scratch_shapes=[
             pltpu.VMEM(coupling.shape, F32),
             pltpu.VMEM(turned.shape, F32),
@@ -247,43 +253,53 @@
         compiler_params=pltpu.CompilerParams(vmem_limit_bytes=50 << 20),
         cost_estimate=pl.CostEstimate(flops=0, bytes_accessed=10 << 20, transcendentals=0),
         name="prepare",
-    )(target, counts, coupling, turned)
+    )(coupling, turned)
 
     def moved(x, axis, n, to):
         return lax.ppermute(x, axis, [(i, to(i)) for i in range(n)])
 
     if two_step:
         far = moved(coeff_in, "grp", ngrp, lambda i: i ^ 3)
-        near = moved(coeff_in, "grp", ngrp, lambda i: i ^ 1)
-        far, code = lax.optimization_barrier((far, code))
-        cross = moved(far, "grp", ngrp, lambda i: i ^ 1)
-        tables = [coeff_in, near, cross, far]
+        theirs = moved(source, "grp", ngrp, lambda i: i ^ 1)
+        far, theirs = lax.optimization_barrier((far, theirs))
+        far, ct = lax.optimization_barrier((far, ct))
+        across = pl.pallas_call(
+            relay,
+            out_shape=shape((nblocks, width), F32),
+            in_specs=[VMEM] * 3,
+            out_specs=VMEM,
+            compiler_params=pltpu.CompilerParams(vmem_limit_bytes=16 << 20),
+            name="relay",
+        )(theirs.reshape(1, nblocks), coeff_in, far)
+        across = moved(across, "grp", ngrp, lambda i: i ^ 1)
+        tables = [coeff_in, far]
     else:
         tables = [coeff_in]
         for k in range(1, ngrp):
             tables.append(moved(coeff_in, "grp", ngrp, lambda i: (i + k) % ngrp))
 
-    last = 2 if two_step else ngrp - 1
-    early, hot = pl.pallas_call(
-        functools.partial(pick, two_step, last),
-        out_shape=(shape((nblocks, width), F32), shape((nblocks, 128), BF)),
-        in_specs=[SMEM] + [VMEM] * (ngrp - 1),
-        out_specs=(VMEM, VMEM),
-        scratch_shapes=[pltpu.VMEM((ngrp, ncl, width), F32)],
+    held = (3 if two_step else ngrp, ncl, width)
+    early, code = pl.pallas_call(
+        functools.partial(pick, two_step),
+        out_shape=(shape((nblocks, width), F32), shape((nwide, 8, 128), F32)),
+        in_specs=[SMEM] * 3 + [VMEM] * len(tables),
+        out_specs=(VMEM,) * 2,
+        scratch_shapes=[pltpu.VMEM(held, F32)],
         compiler_params=pltpu.CompilerParams(vmem_limit_bytes=16 << 20),
         name="pick",
-    )(source, *tables[:last], *tables[last + 1 :])
+    )(source, target, counts, *tables)
+    picked = [early, across] if two_step else [early]
 
     half = shape((nwide // 2, 40, 128), F32)
     spread = shape((nblocks * RHS, 128), F32)
     other, held_a, held_b = pl.pallas_call(
-        functools.partial(couple, two_step),
+        functools.partial(couple, two_step, len(picked)),
         out_shape=(half, spread, spread),
-        in_specs=[VMEM] * 5,
+        in_specs=[VMEM] * (len(picked) + 2),
         out_specs=(VMEM,) * 3,
         compiler_params=pltpu.CompilerParams(vmem_limit_bytes=32 << 20),
         name="couple",
-    )(early, hot, tables[last], ct, code)
+    )(*picked, ct, code)
     same = pl.pallas_call(
         functools.partial(couple_more, two_step),
         out_shape=half,

time: 27.9 us -> 27.2 us (0.975)
  local copies, waits for them, and re-layouts: 1.35 us -> 0.05 us
  starting transfers between devices: 11 us -> 11.9 us
  Pallas kernels: 8.09 us -> 7.76 us
    unnamed x10, local copies, waits for them, and re-layouts: 1.32 us -> 0.02 us
    ppermute x7, starting transfers between devices: 11 us -> 11.9 us  [moved(): return lax.ppermute(x, axis, [(i, to(i)) for i in range(n)])]
    pallas_call x3 -> x4, Pallas kernels: 5.88 us -> 5.55 us  [the longest x1 3.47 us: on_device(): pl.pallas_call(prepare, out_shape=(ct, tr), in_specs=[ANY, ANY], out_spec...]
  transfers between devices with their start and end apart: 7 -> 7, of which waited for: 6 -> 7; matrix products, arithmetic and copies ran while one was open for 0% -> 0% of each run, Pallas kernels for 19% -> 18%
where the time goes in v5:
time: 27.2 us; the launch traced here: 27 us
  starting transfers between devices  11.9 us (44%)
  Pallas kernels  7.76 us (29%)
  waiting for transfers between devices  7.26 us (27%)
    ppermute x7, starting transfers between devices, moved(): return lax.ppermute(x, axis, [(i, to(i)) for i in range(n)])  11.9 us
    ppermute x7, waiting for transfers between devices, moved(): return lax.ppermute(x, axis, [(i, to(i)) for i in range(n)])  7.26 us
    pallas_call x1, Pallas kernels, on_device(): pl.pallas_call(prepare, out_shape=(ct, tr), in_specs=[ANY, ANY], out_spec...  3.47 us
    pallas_call x1, Pallas kernels, on_device(): pl.pallas_call(functools.partial(downward, len(arrived), sets), out_shape...  1.96 us
    pallas_call x1, Pallas kernels, on_device(): pl.pallas_call(functools.partial(pick, two_step), out_shape=(shape((nbloc...  1.1 us
    pallas_call x1, Pallas kernels, on_device(): pl.pallas_call(functools.partial(couple, two_step, len(picked)), out_shap...  0.72 us
  transfers between devices with their start and end apart: 7, of which 7 were waited for; matrix products, arithmetic and copies ran while one was open for 0% of the time, Pallas kernels for 18%

profile of v5, /device:TPU:0, one launch (start us, length us, event | category | flops | bytes accessed | tf_op | source)
XLA Modules:
  0.0 27.0 jit_solution(8806321005647521357)
XLA Ops:
  0.0 5.0 %collective-permute-start = (f32[73,512]{1,0:T(8,128)}, f32[73,512]{1,0:T(8,128)S(1)}, u32[]{:S(2)}, u32[]{:S(2)}) collective-permute-start(f32[73,512]{1,0:T(8,128)} %own.1), channel_id=1, source_target_pairs={{0,24},{8,16},{16,8},{24,0},{1,25},{9,17},{17,9},{25,1},{2,26},{10... | collective-permute-start | bytes 448520 | tf_op jit(solution)/shard_map/ppermute | solution.py:259
  5.0 0.0 collective-permute-start.1
  5.1 0.0 copy-start.1
  5.1 0.0 copy-start.2
  5.1 0.0 copy-start.3
  5.1 0.0 copy-start.4
  5.1 3.5 %prepare.1 = (bf16[8,256,256]{2,1,0:T(8,128)(2,1)S(1)}, bf16[576,1024]{1,0:T(8,128)(2,1)S(1)}) custom-call(f32[64,64,64]{2,1,0:T(8,128)} %coupling_in.1, f32[64,64,72]{2,1,0:T(8,128)} %bitcast.13), custom_call_target="tpu_custom_call" | custom-call | bytes 10485760 | tf_op jit(solution)/shard_map/prepare/pallas_call | solution.py:242
  8.6 0.3 %collective-permute-done.1 = s32[64]{0:T(128)S(1)} collective-permute-done((s32[64]{0:T(128)}, s32[64]{0:T(128)S(1)}, u32[]{:S(2)}, u32[]{:S(2)}) %collective-permute-start.1) | collective-permute-done | bytes 288 | tf_op jit(solution)/shard_map/ppermute | solution.py:259
  8.9 0.7 %collective-permute-done.refs_1_.far = f32[73,512]{1,0:T(8,128)S(1)} collective-permute-done((f32[73,512]{1,0:T(8,128)}, f32[73,512]{1,0:T(8,128)S(1)}, u32[]{:S(2)}, u32[]{:S(2)}) %collective-permute-start) | collective-permute-done | bytes 149536 | tf_op jit(solution)/shard_map/ppermute | solution.py:259
  9.6 0.0 copy-done.1
  9.6 0.2 relay.1
  9.8 0.0 copy-start
  9.8 3.2 %collective-permute-start.2 = (f32[64,512]{1,0:T(8,128)S(1)}, f32[64,512]{1,0:T(8,128)S(1)}, u32[]{:S(2)}, u32[]{:S(2)}) collective-permute-start(f32[64,512]{1,0:T(8,128)S(1)} %relay.1), channel_id=1, source_target_pairs={{0,8},{8,0},{16,24},{24,16},{1,9},{9,1},{17,25},{25,17},{2,10},{10... | collective-permute-start | bytes 393224 | tf_op jit(solution)/shard_map/ppermute | solution.py:259
  13.0 0.0 copy-done.2
  13.0 0.0 copy-done.3
  13.0 0.0 copy-done.4
  13.0 1.1 %pick.1 = (f32[64,512]{1,0:T(8,128)S(1)}, f32[8,8,128]{2,1,0:T(8,128)S(1)}) custom-call(s32[64]{0:T(128)S(1)} %copy-done.2, s32[64]{0:T(128)S(1)} %copy-done.3, s32[8]{0:T(128)S(1)} %copy-done.4, f32[73,512]{1,0:T(8,128)S(1)} %copy-done.1, f32[73,512]{1,0:T(8,128)S(1)} %collective-permute-done.refs_1_.far), custom_call_target="tpu_custom_call" | custom-call | tf_op jit(solution)/shard_map/pick/pallas_call | solution.py:282
  14.1 1.8 %collective-permute-done.2.refs_1_ = f32[64,512]{1,0:T(8,128)S(1)} collective-permute-done((f32[64,512]{1,0:T(8,128)S(1)}, f32[64,512]{1,0:T(8,128)S(1)}, u32[]{:S(2)}, u32[]{:S(2)}) %collective-permute-start.2) | collective-permute-done | bytes 131104 | tf_op jit(solution)/shard_map/ppermute | solution.py:259
  16.0 0.7 %couple.1 = (f32[4,40,128]{2,1,0:T(8,128)S(1)}, f32[512,128]{1,0:T(8,128)S(1)}, f32[512,128]{1,0:T(8,128)S(1)}) custom-call(f32[64,512]{1,0:T(8,128)S(1)} %get-tuple-element.19.refs_0_, f32[64,512]{1,0:T(8,128)S(1)} %collective-permute-done.2.refs_1_, bf16[8,256,256]{2,1,0:T(8,128)(2,1)S(1)} %get-tuple-element.21.refs_2_.ct, ...), custom_call_target="tpu_custom_call" | custom-call | tf_op jit(solution)/shard_map/couple/pallas_call | solution.py:295
  16.7 0.1 collective-permute-start.3
  16.8 0.2 couple_more.1
  17.1 1.0 %collective-permute-done.3 = f32[4,40,128]{2,1,0:T(8,128)S(1)} collective-permute-done((f32[4,40,128]{2,1,0:T(8,128)S(1)}, f32[4,40,128]{2,1,0:T(8,128)S(1)}, u32[]{:S(2)}, u32[]{:S(2)}) %collective-permute-start.3) | collective-permute-done | bytes 81952 | tf_op jit(solution)/shard_map/ppermute | solution.py:259
  18.1 2.5 %collective-permute-start.6 = (f32[72,128]{1,0:T(8,128)S(1)}, f32[72,128]{1,0:T(8,128)S(1)}, u32[]{:S(2)}, u32[]{:S(2)}) collective-permute-start(f32[72,128]{1,0:T(8,128)S(1)} %get-tuple-element.27), channel_id=1, source_target_pairs={{0,6},{1,7},{2,4},{3,5},{4,2},{5,3},{6,0},{7,1},{8,14},{9,15},{10,... | collective-permute-start | bytes 110600 | tf_op jit(solution)/shard_map/ppermute | solution.py:259
  20.6 0.5 %collective-permute-start.5 = (f32[72,128]{1,0:T(8,128)S(1)}, f32[72,128]{1,0:T(8,128)S(1)}, u32[]{:S(2)}, u32[]{:S(2)}) collective-permute-start(f32[72,128]{1,0:T(8,128)S(1)} %get-tuple-element.28), channel_id=1, source_target_pairs={{0,4},{1,5},{2,6},{3,7},{4,0},{5,1},{6,2},{7,3},{8,12},{9,13},{10,... | collective-permute-start | bytes 110600 | tf_op jit(solution)/shard_map/ppermute | solution.py:259
  21.1 0.5 %collective-permute-start.4 = (f32[72,128]{1,0:T(8,128)S(1)}, f32[72,128]{1,0:T(8,128)S(1)}, u32[]{:S(2)}, u32[]{:S(2)}) collective-permute-start(f32[72,128]{1,0:T(8,128)S(1)} %get-tuple-element.29), channel_id=1, source_target_pairs={{0,2},{1,3},{2,0},{3,1},{4,6},{5,7},{6,4},{7,5},{8,10},{9,11},{10,... | collective-permute-start | bytes 110600 | tf_op jit(solution)/shard_map/ppermute | solution.py:259
  21.7 1.4 %collective-permute-done.6.refs_3_ = f32[72,128]{1,0:T(8,128)S(1)} collective-permute-done((f32[72,128]{1,0:T(8,128)S(1)}, f32[72,128]{1,0:T(8,128)S(1)}, u32[]{:S(2)}, u32[]{:S(2)}) %collective-permute-start.6) | collective-permute-done | bytes 36896 | tf_op jit(solution)/shard_map/ppermute | solution.py:259
  23.0 1.5 %collective-permute-done.5.refs_2_ = f32[72,128]{1,0:T(8,128)S(1)} collective-permute-done((f32[72,128]{1,0:T(8,128)S(1)}, f32[72,128]{1,0:T(8,128)S(1)}, u32[]{:S(2)}, u32[]{:S(2)}) %collective-permute-start.5) | collective-permute-done | bytes 36896 | tf_op jit(solution)/shard_map/ppermute | solution.py:259
  24.6 0.5 %collective-permute-done.4.refs_1_ = f32[72,128]{1,0:T(8,128)S(1)} collective-permute-done((f32[72,128]{1,0:T(8,128)S(1)}, f32[72,128]{1,0:T(8,128)S(1)}, u32[]{:S(2)}, u32[]{:S(2)}) %collective-permute-start.4) | collective-permute-done | bytes 36896 | tf_op jit(solution)/shard_map/ppermute | solution.py:259
  25.1 0.0 copy-done
  25.1 2.0 %downward.1 = f32[8,8192]{1,0:T(8,128)} custom-call(f32[72,128]{1,0:T(8,128)S(1)} %get-tuple-element.30.refs_0_, f32[72,128]{1,0:T(8,128)S(1)} %collective-permute-done.4.refs_1_, f32[72,128]{1,0:T(8,128)S(1)} %collective-permute-done.5.refs_2_, f32[72,128]{1,0:T(8,128)S(1)} %collective-permute-done.6.refs_3_, ...), custom_call_target="tpu_custom_call" | custom-call | tf_op jit(solution)/shard_map/downward/pallas_call | solution.py:326
  (5 shorter events, 0.0 us)
Async XLA Ops:
  0.0 9.6 %collective-permute-start = (f32[73,512]{1,0:T(8,128)}, f32[73,512]{1,0:T(8,128)S(1)}, u32[]{:S(2)}, u32[]{:S(2)}) collective-permute-start(f32[73,512]{1,0:T(8,128)} %own.1), channel_id=1, source_target_pairs={{0,24},{8,16},{16,8},{24,0},{1,25},{9,17},{17,9},{25,1},{2,26},{10... | collective-permute-start | bytes 448520 | tf_op jit(solution)/shard_map/ppermute | solution.py:259
  5.0 3.8 %collective-permute-start.1 = (s32[64]{0:T(128)}, s32[64]{0:T(128)S(1)}, u32[]{:S(2)}, u32[]{:S(2)}) collective-permute-start(s32[64]{0:T(128)} %source.1), channel_id=1, source_target_pairs={{0,8},{8,0},{16,24},{24,16},{1,9},{9,1},{17,25},{25,17},{2,10},{10... | collective-permute-start | bytes 776 | tf_op jit(solution)/shard_map/ppermute | solution.py:259
  5.1 4.5 %copy-start.1 = (f32[73,512]{1,0:T(8,128)S(1)}, f32[73,512]{1,0:T(8,128)}, u32[]{:S(2)}) copy-start(f32[73,512]{1,0:T(8,128)} %own.1) | copy-start | bytes 448516
  5.1 8.0 %copy-start.2 = (s32[64]{0:T(128)S(1)}, s32[64]{0:T(128)}, u32[]{:S(2)}) copy-start(s32[64]{0:T(128)} %source.1) | copy-start | bytes 772
  5.1 8.0 %copy-start.3 = (s32[64]{0:T(128)S(1)}, s32[64]{0:T(128)}, u32[]{:S(2)}) copy-start(s32[64]{0:T(128)} %target.1) | copy-start | bytes 772
  5.1 8.0 %copy-start.4 = (s32[8]{0:T(128)S(1)}, s32[8]{0:T(128)}, u32[]{:S(2)}) copy-start(s32[8]{0:T(128)} %counts.1) | copy-start | bytes 100
  9.8 15.2 %copy-start = (f32[64,64,128]{2,1,0:T(8,128)S(1)}, f32[64,64,128]{2,1,0:T(8,128)}, u32[]{:S(2)}) copy-start(f32[64,64,128]{2,1,0:T(8,128)} %param.13) | copy-start | bytes 6291460
  9.8 6.1 %collective-permute-start.2 = (f32[64,512]{1,0:T(8,128)S(1)}, f32[64,512]{1,0:T(8,128)S(1)}, u32[]{:S(2)}, u32[]{:S(2)}) collective-permute-start(f32[64,512]{1,0:T(8,128)S(1)} %relay.1), channel_id=1, source_target_pairs={{0,8},{8,0},{16,24},{24,16},{1,9},{9,1},{17,25},{25,17},{2,10},{10... | collective-permute-start | bytes 393224 | tf_op jit(solution)/shard_map/ppermute | solution.py:259
  16.7 1.3 %collective-permute-start.3 = (f32[4,40,128]{2,1,0:T(8,128)S(1)}, f32[4,40,128]{2,1,0:T(8,128)S(1)}, u32[]{:S(2)}, u32[]{:S(2)}) collective-permute-start(f32[4,40,128]{2,1,0:T(8,128)S(1)} %get-tuple-element.25), channel_id=1, source_target_pairs={{0,1},{1,0},{2,3},{3,2},{4,5},{5,4},{6,7},{7,6},{8,9},{9,8},{10,11... | collective-permute-start | bytes 245768 | tf_op jit(solution)/shard_map/ppermute | solution.py:259
  18.1 4.9 %collective-permute-start.6 = (f32[72,128]{1,0:T(8,128)S(1)}, f32[72,128]{1,0:T(8,128)S(1)}, u32[]{:S(2)}, u32[]{:S(2)}) collective-permute-start(f32[72,128]{1,0:T(8,128)S(1)} %get-tuple-element.27), channel_id=1, source_target_pairs={{0,6},{1,7},{2,4},{3,5},{4,2},{5,3},{6,0},{7,1},{8,14},{9,15},{10,... | collective-permute-start | bytes 110600 | tf_op jit(solution)/shard_map/ppermute | solution.py:259
  20.6 4.0 %collective-permute-start.5 = (f32[72,128]{1,0:T(8,128)S(1)}, f32[72,128]{1,0:T(8,128)S(1)}, u32[]{:S(2)}, u32[]{:S(2)}) collective-permute-start(f32[72,128]{1,0:T(8,128)S(1)} %get-tuple-element.28), channel_id=1, source_target_pairs={{0,4},{1,5},{2,6},{3,7},{4,0},{5,1},{6,2},{7,3},{8,12},{9,13},{10,... | collective-permute-start | bytes 110600 | tf_op jit(solution)/shard_map/ppermute | solution.py:259
  21.1 4.0 %collective-permute-start.4 = (f32[72,128]{1,0:T(8,128)S(1)}, f32[72,128]{1,0:T(8,128)S(1)}, u32[]{:S(2)}, u32[]{:S(2)}) collective-permute-start(f32[72,128]{1,0:T(8,128)S(1)} %get-tuple-element.29), channel_id=1, source_target_pairs={{0,2},{1,3},{2,0},{3,1},{4,6},{5,7},{6,4},{7,5},{8,10},{9,11},{10,... | collective-permute-start | bytes 110600 | tf_op jit(solution)/shard_map/ppermute | solution.py:259

commit v6 on v5

--- a/solution.py
+++ b/solution.py
@@ -173,18 +173,14 @@
                 part = row if part is None else jnp.where(lane // 32 == e, row, part)
             parts.append(part)
         codes.append(jnp.concatenate(parts, axis=1).astype(jnp.int32))
-    total = full.shape[0]
-    step = 80
-    for at in range(0, total, step):
-        rows = min(step, total - at)
-        sums = []
-        for h in range(2):
-            place = iota((rows, 32 * nwide), 0) + at
-            hot = jnp.where(place == codes[h], 1.0, 0.0).astype(BF)
-            r = mm(hot, weights)
-            sums.append(r[:, :128] + r[:, 128:])
-        s = jnp.where(iota((rows, 128), 1) < RANK, sums[0], sums[1])
-        full[at : at + rows, :] = s + pltpu.roll(s, RANK, 1)
+    rows = full.shape[0]
+    place = iota((rows, 32 * nwide), 0)
+    sums = []
+    for h in range(2):
+        r = mm(jnp.where(place == codes[h], 1.0, 0.0).astype(BF), weights)
+        sums.append(r[:, :128] + r[:, 128:])
+    s = jnp.where(iota((rows, 128), 1) < RANK, sums[0], sums[1])
+    full[...] = s + pltpu.roll(s, RANK, 1)
 
     first = iota((RHS, 128), 1) < RANK
 

time: 27.2 us -> 27.1 us (level)
  no operation moved by 1% of the time
where the time goes in v6:
time: 27.1 us; the launch traced here: 26.9 us
  starting transfers between devices  11.9 us (44%)
  Pallas kernels  7.64 us (28%)
  waiting for transfers between devices  7.26 us (27%)
    ppermute x7, starting transfers between devices, moved(): return lax.ppermute(x, axis, [(i, to(i)) for i in range(n)])  11.9 us
    ppermute x7, waiting for transfers between devices, moved(): return lax.ppermute(x, axis, [(i, to(i)) for i in range(n)])  7.26 us
    pallas_call x1, Pallas kernels, on_device(): pl.pallas_call(prepare, out_shape=(ct, tr), in_specs=[ANY, ANY], out_spec...  3.47 us
    pallas_call x1, Pallas kernels, on_device(): pl.pallas_call(functools.partial(downward, len(arrived), sets), out_shape...  1.84 us
    pallas_call x1, Pallas kernels, on_device(): pl.pallas_call(functools.partial(pick, two_step), out_shape=(shape((nbloc...  1.1 us
    pallas_call x1, Pallas kernels, on_device(): pl.pallas_call(functools.partial(couple, two_step, len(picked)), out_shap...  0.72 us
  transfers between devices with their start and end apart: 7, of which 7 were waited for; matrix products, arithmetic and copies ran while one was open for 0% of the time, Pallas kernels for 18%

profile of v6, /device:TPU:0, one launch (start us, length us, event | category | flops | bytes accessed | tf_op | source)
XLA Modules:
  0.0 26.9 jit_solution(4395130784802406200)
XLA Ops:
  0.0 5.0 %collective-permute-start = (f32[73,512]{1,0:T(8,128)}, f32[73,512]{1,0:T(8,128)S(1)}, u32[]{:S(2)}, u32[]{:S(2)}) collective-permute-start(f32[73,512]{1,0:T(8,128)} %own.1), channel_id=1, source_target_pairs={{0,24},{8,16},{16,8},{24,0},{1,25},{9,17},{17,9},{25,1},{2,26},{10... | collective-permute-start | bytes 448520 | tf_op jit(solution)/shard_map/ppermute | solution.py:255
  5.0 0.0 collective-permute-start.1
  5.1 0.0 copy-start.1
  5.1 0.0 copy-start.2
  5.1 0.0 copy-start.3
  5.1 0.0 copy-start.4
  5.1 3.5 %prepare.1 = (bf16[8,256,256]{2,1,0:T(8,128)(2,1)S(1)}, bf16[576,1024]{1,0:T(8,128)(2,1)S(1)}) custom-call(f32[64,64,64]{2,1,0:T(8,128)} %coupling_in.1, f32[64,64,72]{2,1,0:T(8,128)} %bitcast.13), custom_call_target="tpu_custom_call" | custom-call | bytes 10485760 | tf_op jit(solution)/shard_map/prepare/pallas_call | solution.py:238
  8.6 0.3 %collective-permute-done.1 = s32[64]{0:T(128)S(1)} collective-permute-done((s32[64]{0:T(128)}, s32[64]{0:T(128)S(1)}, u32[]{:S(2)}, u32[]{:S(2)}) %collective-permute-start.1) | collective-permute-done | bytes 288 | tf_op jit(solution)/shard_map/ppermute | solution.py:255
  8.9 0.7 %collective-permute-done.refs_1_.far = f32[73,512]{1,0:T(8,128)S(1)} collective-permute-done((f32[73,512]{1,0:T(8,128)}, f32[73,512]{1,0:T(8,128)S(1)}, u32[]{:S(2)}, u32[]{:S(2)}) %collective-permute-start) | collective-permute-done | bytes 149536 | tf_op jit(solution)/shard_map/ppermute | solution.py:255
  9.6 0.0 copy-done.1
  9.6 0.2 relay.1
  9.8 0.0 copy-start
  9.8 3.2 %collective-permute-start.2 = (f32[64,512]{1,0:T(8,128)S(1)}, f32[64,512]{1,0:T(8,128)S(1)}, u32[]{:S(2)}, u32[]{:S(2)}) collective-permute-start(f32[64,512]{1,0:T(8,128)S(1)} %relay.1), channel_id=1, source_target_pairs={{0,8},{8,0},{16,24},{24,16},{1,9},{9,1},{17,25},{25,17},{2,10},{10... | collective-permute-start | bytes 393224 | tf_op jit(solution)/shard_map/ppermute | solution.py:255
  13.0 0.0 copy-done.2
  13.0 0.0 copy-done.3
  13.0 0.0 copy-done.4
  13.0 1.1 %pick.1 = (f32[64,512]{1,0:T(8,128)S(1)}, f32[8,8,128]{2,1,0:T(8,128)S(1)}) custom-call(s32[64]{0:T(128)S(1)} %copy-done.2, s32[64]{0:T(128)S(1)} %copy-done.3, s32[8]{0:T(128)S(1)} %copy-done.4, f32[73,512]{1,0:T(8,128)S(1)} %copy-done.1, f32[73,512]{1,0:T(8,128)S(1)} %collective-permute-done.refs_1_.far), custom_call_target="tpu_custom_call" | custom-call | tf_op jit(solution)/shard_map/pick/pallas_call | solution.py:278
  14.1 1.8 %collective-permute-done.2.refs_1_ = f32[64,512]{1,0:T(8,128)S(1)} collective-permute-done((f32[64,512]{1,0:T(8,128)S(1)}, f32[64,512]{1,0:T(8,128)S(1)}, u32[]{:S(2)}, u32[]{:S(2)}) %collective-permute-start.2) | collective-permute-done | bytes 131104 | tf_op jit(solution)/shard_map/ppermute | solution.py:255
  16.0 0.7 %couple.1 = (f32[4,40,128]{2,1,0:T(8,128)S(1)}, f32[512,128]{1,0:T(8,128)S(1)}, f32[512,128]{1,0:T(8,128)S(1)}) custom-call(f32[64,512]{1,0:T(8,128)S(1)} %get-tuple-element.19.refs_0_, f32[64,512]{1,0:T(8,128)S(1)} %collective-permute-done.2.refs_1_, bf16[8,256,256]{2,1,0:T(8,128)(2,1)S(1)} %get-tuple-element.21.refs_2_.ct, ...), custom_call_target="tpu_custom_call" | custom-call | tf_op jit(solution)/shard_map/couple/pallas_call | solution.py:291
  16.7 0.1 collective-permute-start.3
  16.8 0.2 couple_more.1
  17.1 1.0 %collective-permute-done.3 = f32[4,40,128]{2,1,0:T(8,128)S(1)} collective-permute-done((f32[4,40,128]{2,1,0:T(8,128)S(1)}, f32[4,40,128]{2,1,0:T(8,128)S(1)}, u32[]{:S(2)}, u32[]{:S(2)}) %collective-permute-start.3) | collective-permute-done | bytes 81952 | tf_op jit(solution)/shard_map/ppermute | solution.py:255
  18.1 2.5 %collective-permute-start.6 = (f32[72,128]{1,0:T(8,128)S(1)}, f32[72,128]{1,0:T(8,128)S(1)}, u32[]{:S(2)}, u32[]{:S(2)}) collective-permute-start(f32[72,128]{1,0:T(8,128)S(1)} %get-tuple-element.27), channel_id=1, source_target_pairs={{0,6},{1,7},{2,4},{3,5},{4,2},{5,3},{6,0},{7,1},{8,14},{9,15},{10,... | collective-permute-start | bytes 110600 | tf_op jit(solution)/shard_map/ppermute | solution.py:255
  20.6 0.5 %collective-permute-start.5 = (f32[72,128]{1,0:T(8,128)S(1)}, f32[72,128]{1,0:T(8,128)S(1)}, u32[]{:S(2)}, u32[]{:S(2)}) collective-permute-start(f32[72,128]{1,0:T(8,128)S(1)} %get-tuple-element.28), channel_id=1, source_target_pairs={{0,4},{1,5},{2,6},{3,7},{4,0},{5,1},{6,2},{7,3},{8,12},{9,13},{10,... | collective-permute-start | bytes 110600 | tf_op jit(solution)/shard_map/ppermute | solution.py:255
  21.1 0.5 %collective-permute-start.4 = (f32[72,128]{1,0:T(8,128)S(1)}, f32[72,128]{1,0:T(8,128)S(1)}, u32[]{:S(2)}, u32[]{:S(2)}) collective-permute-start(f32[72,128]{1,0:T(8,128)S(1)} %get-tuple-element.29), channel_id=1, source_target_pairs={{0,2},{1,3},{2,0},{3,1},{4,6},{5,7},{6,4},{7,5},{8,10},{9,11},{10,... | collective-permute-start | bytes 110600 | tf_op jit(solution)/shard_map/ppermute | solution.py:255
  21.7 1.4 %collective-permute-done.6.refs_3_ = f32[72,128]{1,0:T(8,128)S(1)} collective-permute-done((f32[72,128]{1,0:T(8,128)S(1)}, f32[72,128]{1,0:T(8,128)S(1)}, u32[]{:S(2)}, u32[]{:S(2)}) %collective-permute-start.6) | collective-permute-done | bytes 36896 | tf_op jit(solution)/shard_map/ppermute | solution.py:255
  23.0 1.5 %collective-permute-done.5.refs_2_ = f32[72,128]{1,0:T(8,128)S(1)} collective-permute-done((f32[72,128]{1,0:T(8,128)S(1)}, f32[72,128]{1,0:T(8,128)S(1)}, u32[]{:S(2)}, u32[]{:S(2)}) %collective-permute-start.5) | collective-permute-done | bytes 36896 | tf_op jit(solution)/shard_map/ppermute | solution.py:255
  24.6 0.5 %collective-permute-done.4.refs_1_ = f32[72,128]{1,0:T(8,128)S(1)} collective-permute-done((f32[72,128]{1,0:T(8,128)S(1)}, f32[72,128]{1,0:T(8,128)S(1)}, u32[]{:S(2)}, u32[]{:S(2)}) %collective-permute-start.4) | collective-permute-done | bytes 36896 | tf_op jit(solution)/shard_map/ppermute | solution.py:255
  25.1 0.0 copy-done
  25.1 1.8 %downward.1 = f32[8,8192]{1,0:T(8,128)} custom-call(f32[72,128]{1,0:T(8,128)S(1)} %get-tuple-element.30.refs_0_, f32[72,128]{1,0:T(8,128)S(1)} %collective-permute-done.4.refs_1_, f32[72,128]{1,0:T(8,128)S(1)} %collective-permute-done.5.refs_2_, f32[72,128]{1,0:T(8,128)S(1)} %collective-permute-done.6.refs_3_, ...), custom_call_target="tpu_custom_call" | custom-call | tf_op jit(solution)/shard_map/downward/pallas_call | solution.py:322
  (5 shorter events, 0.0 us)
Async XLA Ops:
  0.0 9.6 %collective-permute-start = (f32[73,512]{1,0:T(8,128)}, f32[73,512]{1,0:T(8,128)S(1)}, u32[]{:S(2)}, u32[]{:S(2)}) collective-permute-start(f32[73,512]{1,0:T(8,128)} %own.1), channel_id=1, source_target_pairs={{0,24},{8,16},{16,8},{24,0},{1,25},{9,17},{17,9},{25,1},{2,26},{10... | collective-permute-start | bytes 448520 | tf_op jit(solution)/shard_map/ppermute | solution.py:255
  5.0 3.8 %collective-permute-start.1 = (s32[64]{0:T(128)}, s32[64]{0:T(128)S(1)}, u32[]{:S(2)}, u32[]{:S(2)}) collective-permute-start(s32[64]{0:T(128)} %source.1), channel_id=1, source_target_pairs={{0,8},{8,0},{16,24},{24,16},{1,9},{9,1},{17,25},{25,17},{2,10},{10... | collective-permute-start | bytes 776 | tf_op jit(solution)/shard_map/ppermute | solution.py:255
  5.1 4.5 %copy-start.1 = (f32[73,512]{1,0:T(8,128)S(1)}, f32[73,512]{1,0:T(8,128)}, u32[]{:S(2)}) copy-start(f32[73,512]{1,0:T(8,128)} %own.1) | copy-start | bytes 448516
  5.1 8.0 %copy-start.2 = (s32[64]{0:T(128)S(1)}, s32[64]{0:T(128)}, u32[]{:S(2)}) copy-start(s32[64]{0:T(128)} %source.1) | copy-start | bytes 772
  5.1 8.0 %copy-start.3 = (s32[64]{0:T(128)S(1)}, s32[64]{0:T(128)}, u32[]{:S(2)}) copy-start(s32[64]{0:T(128)} %target.1) | copy-start | bytes 772
  5.1 8.0 %copy-start.4 = (s32[8]{0:T(128)S(1)}, s32[8]{0:T(128)}, u32[]{:S(2)}) copy-start(s32[8]{0:T(128)} %counts.1) | copy-start | bytes 100
  9.8 15.2 %copy-start = (f32[64,64,128]{2,1,0:T(8,128)S(1)}, f32[64,64,128]{2,1,0:T(8,128)}, u32[]{:S(2)}) copy-start(f32[64,64,128]{2,1,0:T(8,128)} %param.13) | copy-start | bytes 6291460
  9.8 6.1 %collective-permute-start.2 = (f32[64,512]{1,0:T(8,128)S(1)}, f32[64,512]{1,0:T(8,128)S(1)}, u32[]{:S(2)}, u32[]{:S(2)}) collective-permute-start(f32[64,512]{1,0:T(8,128)S(1)} %relay.1), channel_id=1, source_target_pairs={{0,8},{8,0},{16,24},{24,16},{1,9},{9,1},{17,25},{25,17},{2,10},{10... | collective-permute-start | bytes 393224 | tf_op jit(solution)/shard_map/ppermute | solution.py:255
  16.7 1.3 %collective-permute-start.3 = (f32[4,40,128]{2,1,0:T(8,128)S(1)}, f32[4,40,128]{2,1,0:T(8,128)S(1)}, u32[]{:S(2)}, u32[]{:S(2)}) collective-permute-start(f32[4,40,128]{2,1,0:T(8,128)S(1)} %get-tuple-element.25), channel_id=1, source_target_pairs={{0,1},{1,0},{2,3},{3,2},{4,5},{5,4},{6,7},{7,6},{8,9},{9,8},{10,11... | collective-permute-start | bytes 245768 | tf_op jit(solution)/shard_map/ppermute | solution.py:255
  18.1 4.9 %collective-permute-start.6 = (f32[72,128]{1,0:T(8,128)S(1)}, f32[72,128]{1,0:T(8,128)S(1)}, u32[]{:S(2)}, u32[]{:S(2)}) collective-permute-start(f32[72,128]{1,0:T(8,128)S(1)} %get-tuple-element.27), channel_id=1, source_target_pairs={{0,6},{1,7},{2,4},{3,5},{4,2},{5,3},{6,0},{7,1},{8,14},{9,15},{10,... | collective-permute-start | bytes 110600 | tf_op jit(solution)/shard_map/ppermute | solution.py:255
  20.6 4.0 %collective-permute-start.5 = (f32[72,128]{1,0:T(8,128)S(1)}, f32[72,128]{1,0:T(8,128)S(1)}, u32[]{:S(2)}, u32[]{:S(2)}) collective-permute-start(f32[72,128]{1,0:T(8,128)S(1)} %get-tuple-element.28), channel_id=1, source_target_pairs={{0,4},{1,5},{2,6},{3,7},{4,0},{5,1},{6,2},{7,3},{8,12},{9,13},{10,... | collective-permute-start | bytes 110600 | tf_op jit(solution)/shard_map/ppermute | solution.py:255
  21.1 4.0 %collective-permute-start.4 = (f32[72,128]{1,0:T(8,128)S(1)}, f32[72,128]{1,0:T(8,128)S(1)}, u32[]{:S(2)}, u32[]{:S(2)}) collective-permute-start(f32[72,128]{1,0:T(8,128)S(1)} %get-tuple-element.29), channel_id=1, source_target_pairs={{0,2},{1,3},{2,0},{3,1},{4,6},{5,7},{6,4},{7,5},{8,10},{9,11},{10,... | collective-permute-start | bytes 110600 | tf_op jit(solution)/shard_map/ppermute | solution.py:255

commit v7 on v6

--- a/solution.py
+++ b/solution.py
@@ -11,6 +11,7 @@
 RANK = 64
 RHS = 8
 SLOTS = 8
+CROSS = (3,)
 HALF = 4
 BF = jnp.bfloat16
 F32 = jnp.float32
@@ -117,7 +118,7 @@
 
 
 def couple(two_step, parts, *refs):
-    early, (ct, code, other, held_a, held_b) = refs[:parts], refs[parts:]
+    early, (ct, code, out, held_a, held_b) = refs[:parts], refs[parts:]
     nblocks, width = early[0].shape
     wide = lax.axis_index("wide") if two_step else 0
     picked = sum(part[...] for part in early)
@@ -138,27 +139,25 @@
             rows = pl.ds(2 * s + i, nblocks, stride=RHS)
             held_a[rows, :] = jnp.where(own == 0, x, 0.0)
             held_b[rows, :] = jnp.where(own == 2, x, 0.0)
-    towards(1, wide, 2 if two_step else 0, held_a, held_b, ct, code, other)
-
-
-def couple_more(two_step, held_a, held_b, ct, code, same):
-    towards(0, lax.axis_index("wide") if two_step else 0, 0, held_a, held_b, ct, code, same)
-
-
-def towards(parity, wide, shift, held_a, held_b, ct, code, out):
+    messages(range(out.shape[0]), wide, CROSS if two_step else (), held_a, held_b, ct, code, [out.at[c] for c in range(out.shape[0])])
+
+
+def messages(chips, wide, cross, held_a, held_b, ct, code, outs):
     left = iota((32, 128), 1) < RANK
-    for p in range(out.shape[0]):
-        peer = (2 * p + parity) ^ wide
-        at = pl.ds(pl.multiple_of(peer * 64, 64), 64)
-        z = product3(jnp.concatenate([held_a[at, :], held_b[at, :]], axis=1), ct[peer])
-        out[p, :32, :] = jnp.where(left, z[:32], z[32:])
-        out[p, 32:, :] = pltpu.roll(code[peer], shift, 0) if shift else code[peer]
-
-
-def downward(messages, sets, *refs):
-    arrived, (tr, basis, out, full, held, sems) = refs[:messages], refs[messages:]
-    nwide = messages * sets
-    value = jnp.concatenate([message[: 32 * sets, :] for message in arrived], axis=0)
+    for chip, out in zip(chips, outs):
+        for i in range(2):
+            peer = (2 * chip + (1 - i if chip in cross else i)) ^ wide
+            at = pl.ds(pl.multiple_of(peer * 64, 64), 64)
+            z = product3(jnp.concatenate([held_a[at, :], held_b[at, :]], axis=1), ct[peer])
+            out[32 * i : 32 * (i + 1), :] = jnp.where(left, z[:32], z[32:])
+        peer = (2 * chip + (chip in cross)) ^ wide
+        out[64:, :] = code[peer] + pltpu.roll(code[peer ^ 1], 2, 0)
+
+
+def downward(kinds, *refs):
+    nwide = len(kinds)
+    arrived, (tr, basis, out, full, held, sems) = refs[:nwide], refs[nwide:]
+    value = jnp.concatenate([message[at : at + 32, :] for message, (at, _) in zip(arrived, kinds)], axis=0)
     high, low = split(value)
     weights = jnp.concatenate([high, low], axis=1)
     lane = iota((1, 128), 1)
@@ -168,8 +167,8 @@
         for q in range(nwide // 4):
             part = None
             for e in range(4):
-                at = 32 * sets + 2 * (e % sets) + h
-                row = arrived[(4 * q + e) // sets][at : at + 1, :]
+                at = kinds[4 * q + e][1] + h
+                row = arrived[4 * q + e][at : at + 1, :]
                 part = row if part is None else jnp.where(lane // 32 == e, row, part)
             parts.append(part)
         codes.append(jnp.concatenate(parts, axis=1).astype(jnp.int32))
@@ -286,41 +285,36 @@
     )(source, target, counts, *tables)
     picked = [early, across] if two_step else [early]
 
-    half = shape((nwide // 2, 40, 128), F32)
-    spread = shape((nblocks * RHS, 128), F32)
-    other, held_a, held_b = pl.pallas_call(
+    chips = range(nwide // 2)
+    out = pl.pallas_call(
         functools.partial(couple, two_step, len(picked)),
-        out_shape=(half, spread, spread),
+        out_shape=shape((nwide // 2, 72, 128), F32),
         in_specs=[VMEM] * (len(picked) + 2),
-        out_specs=(VMEM,) * 3,
+        out_specs=VMEM,
+        scratch_shapes=[pltpu.VMEM((nblocks * RHS, 128), F32)] * 2,
         compiler_params=pltpu.CompilerParams(vmem_limit_bytes=32 << 20),
         name="couple",
     )(*picked, ct, code)
-    same = pl.pallas_call(
-        functools.partial(couple_more, two_step),
-        out_shape=half,
-        in_specs=[VMEM] * 4,
-        out_specs=VMEM,
-        compiler_params=pltpu.CompilerParams(vmem_limit_bytes=16 << 20),
-        cost_estimate=pl.CostEstimate(flops=0, bytes_accessed=4 << 20, transcendentals=0),
-        name="couple_more",
-    )(held_a, held_b, ct, code)
 
     if two_step:
-        mate = moved(other, "wide", nwide, lambda i: i ^ 1)
-        both = jnp.concatenate([same[:, :32], mate[:, :32], same[:, 32:] + mate[:, 32:]], axis=1)
-        arrived = [both[0]]
+        arrived = [out[0]]
         for k in (1, 2, 3):
-            arrived.append(moved(both[k], "wide", nwide, lambda i: i ^ (2 * k)))
-        sets = 2
+            arrived.append(moved(out[k], "wide", nwide, lambda i: i ^ (2 * k + (k in CROSS))))
+        mate = jnp.stack([x[32:] for x in arrived])
+        mate = moved(mate, "wide", nwide, lambda i: i ^ 1)
+        arrived = arrived + [mate[k] for k in range(4)]
+        kinds = [(0, 64)] * 4 + [(0, 34)] * 4
     else:
-        payload = jnp.stack([same, other], axis=1).reshape(nwide, 40, 128)
+        pairs = jnp.stack([out[c] for c in chips])
+        single = jnp.stack([pairs[:, :32], pairs[:, 32:64]], axis=1)
+        codes = jnp.stack([pairs[:, 64:], jnp.roll(pairs[:, 64:], -2, axis=1)], axis=1)
+        payload = jnp.concatenate([single, codes], axis=2).reshape(nwide, 40, 128)
         payload = lax.all_to_all(payload, "wide", split_axis=0, concat_axis=0, tiled=True)
         arrived = [payload[p] for p in range(nwide)]
-        sets = 1
+        kinds = [(0, 32)] * nwide
 
     return pl.pallas_call(
-        functools.partial(downward, len(arrived), sets),
+        functools.partial(downward, kinds),
         out_shape=shape((RHS, nleaf * points), F32),
         in_specs=[VMEM] * (len(arrived) + 2),
         out_specs=ANY,

time: 27.1 us -> 26 us (0.959)
  waiting for transfers between devices: 7.26 us -> 6.64 us
  starting transfers between devices: 11.9 us -> 11.6 us
    ppermute x7, waiting for transfers between devices: 7.26 us -> 6.64 us  [moved(): return lax.ppermute(x, axis, [(i, to(i)) for i in range(n)])]
    ppermute x7, starting transfers between devices: 11.9 us -> 11.6 us  [moved(): return lax.ppermute(x, axis, [(i, to(i)) for i in range(n)])]
    pallas_call x2 -> x1, Pallas kernels: 2.09 us -> 1.85 us  [on_device(): pl.pallas_call(functools.partial(downward, kinds), out_shape=shape((RHS,...]
where the time goes in v7:
time: 26 us; the launch traced here: 25.8 us
  starting transfers between devices  11.6 us (45%)
  Pallas kernels  7.49 us (29%)
  waiting for transfers between devices  6.64 us (26%)
    ppermute x7, starting transfers between devices, moved(): return lax.ppermute(x, axis, [(i, to(i)) for i in range(n)])  11.6 us
    ppermute x7, waiting for transfers between devices, moved(): return lax.ppermute(x, axis, [(i, to(i)) for i in range(n)])  6.64 us
    pallas_call x1, Pallas kernels, on_device(): pl.pallas_call(prepare, out_shape=(ct, tr), in_specs=[ANY, ANY], out_spec...  3.47 us
    pallas_call x1, Pallas kernels, on_device(): pl.pallas_call(functools.partial(downward, kinds), out_shape=shape((RHS,...  1.85 us
    pallas_call x1, Pallas kernels, on_device(): pl.pallas_call(functools.partial(pick, two_step), out_shape=(shape((nbloc...  1.1 us
    pallas_call x1, Pallas kernels, on_device(): pl.pallas_call(functools.partial(couple, two_step, len(picked)), out_shap...  0.82 us
  transfers between devices with their start and end apart: 7, of which 7 were waited for; matrix products, arithmetic and copies ran while one was open for 0% of the time, Pallas kernels for 18%

profile of v7, /device:TPU:0, one launch (start us, length us, event | category | flops | bytes accessed | tf_op | source)
XLA Modules:
  0.0 25.8 jit_solution(11907603996671330163)
XLA Ops:
  0.0 5.0 %collective-permute-start = (f32[73,512]{1,0:T(8,128)}, f32[73,512]{1,0:T(8,128)S(1)}, u32[]{:S(2)}, u32[]{:S(2)}) collective-permute-start(f32[73,512]{1,0:T(8,128)} %own.1), channel_id=1, source_target_pairs={{0,24},{8,16},{16,8},{24,0},{1,25},{9,17},{17,9},{25,1},{2,26},{10... | collective-permute-start | bytes 448520 | tf_op jit(solution)/shard_map/ppermute | solution.py:254
  5.0 0.0 collective-permute-start.1
  5.1 0.0 copy-start.1
  5.1 0.0 copy-start.2
  5.1 0.0 copy-start.3
  5.1 0.0 copy-start.4
  5.1 3.5 %prepare.1 = (bf16[8,256,256]{2,1,0:T(8,128)(2,1)S(1)}, bf16[576,1024]{1,0:T(8,128)(2,1)S(1)}) custom-call(f32[64,64,64]{2,1,0:T(8,128)} %coupling_in.1, f32[64,64,72]{2,1,0:T(8,128)} %bitcast.27), custom_call_target="tpu_custom_call" | custom-call | bytes 10485760 | tf_op jit(solution)/shard_map/prepare/pallas_call | solution.py:237
  8.6 0.0 copy-start
  8.6 0.3 %collective-permute-done.1 = s32[64]{0:T(128)S(1)} collective-permute-done((s32[64]{0:T(128)}, s32[64]{0:T(128)S(1)}, u32[]{:S(2)}, u32[]{:S(2)}) %collective-permute-start.1) | collective-permute-done | bytes 288 | tf_op jit(solution)/shard_map/ppermute | solution.py:254
  8.9 0.7 %collective-permute-done.refs_1_.far = f32[73,512]{1,0:T(8,128)S(1)} collective-permute-done((f32[73,512]{1,0:T(8,128)}, f32[73,512]{1,0:T(8,128)S(1)}, u32[]{:S(2)}, u32[]{:S(2)}) %collective-permute-start) | collective-permute-done | bytes 149536 | tf_op jit(solution)/shard_map/ppermute | solution.py:254
  9.6 0.0 copy-done.1
  9.6 0.2 relay.1
  9.8 3.2 %collective-permute-start.2 = (f32[64,512]{1,0:T(8,128)S(1)}, f32[64,512]{1,0:T(8,128)S(1)}, u32[]{:S(2)}, u32[]{:S(2)}) collective-permute-start(f32[64,512]{1,0:T(8,128)S(1)} %relay.1), channel_id=1, source_target_pairs={{0,8},{8,0},{16,24},{24,16},{1,9},{9,1},{17,25},{25,17},{2,10},{10... | collective-permute-start | bytes 393224 | tf_op jit(solution)/shard_map/ppermute | solution.py:254
  13.0 0.0 copy-done.2
  13.0 0.0 copy-done.3
  13.0 0.0 copy-done.4
  13.0 1.1 %pick.1 = (f32[64,512]{1,0:T(8,128)S(1)}, f32[8,8,128]{2,1,0:T(8,128)S(1)}) custom-call(s32[64]{0:T(128)S(1)} %copy-done.2, s32[64]{0:T(128)S(1)} %copy-done.3, s32[8]{0:T(128)S(1)} %copy-done.4, f32[73,512]{1,0:T(8,128)S(1)} %copy-done.1, f32[73,512]{1,0:T(8,128)S(1)} %collective-permute-done.refs_1_.far), custom_call_target="tpu_custom_call" | custom-call | tf_op jit(solution)/shard_map/pick/pallas_call | solution.py:277
  14.1 1.8 %collective-permute-done.2.refs_1_ = f32[64,512]{1,0:T(8,128)S(1)} collective-permute-done((f32[64,512]{1,0:T(8,128)S(1)}, f32[64,512]{1,0:T(8,128)S(1)}, u32[]{:S(2)}, u32[]{:S(2)}) %collective-permute-start.2) | collective-permute-done | bytes 131104 | tf_op jit(solution)/shard_map/ppermute | solution.py:254
  16.0 0.8 %couple.1 = f32[4,72,128]{2,1,0:T(8,128)S(1)} custom-call(f32[64,512]{1,0:T(8,128)S(1)} %get-tuple-element.16.refs_0_, f32[64,512]{1,0:T(8,128)S(1)} %collective-permute-done.2.refs_1_, bf16[8,256,256]{2,1,0:T(8,128)(2,1)S(1)} %get-tuple-element.18.refs_2_, f32[8,8,128]{2,1,0:T(8,128)S(1)} %get-tuple-element.19.refs_3_), custom_call_target="tpu_custom_call" | custom-call | tf_op jit(solution)/shard_map/couple/pallas_call | solution.py:289
  16.8 0.4 %collective-permute-start.5 = (f32[72,128]{1,0:T(8,128)S(1)}, f32[72,128]{1,0:T(8,128)S(1)}, u32[]{:S(2)}, u32[]{:S(2)}) collective-permute-start(f32[72,128]{1,0:T(8,128)S(1)} %get-tuple-element.21), channel_id=1, source_target_pairs={{0,7},{1,6},{2,5},{3,4},{4,3},{5,2},{6,1},{7,0},{8,15},{9,14},{10,... | collective-permute-start | bytes 110600 | tf_op jit(solution)/shard_map/ppermute | solution.py:254
  17.2 1.3 %collective-permute-start.4 = (f32[72,128]{1,0:T(8,128)S(1)}, f32[72,128]{1,0:T(8,128)S(1)}, u32[]{:S(2)}, u32[]{:S(2)}) collective-permute-start(f32[72,128]{1,0:T(8,128)S(1)} %get-tuple-element.22), channel_id=1, source_target_pairs={{0,4},{1,5},{2,6},{3,7},{4,0},{5,1},{6,2},{7,3},{8,12},{9,13},{10,... | collective-permute-start | bytes 110600 | tf_op jit(solution)/shard_map/ppermute | solution.py:254
  18.5 1.5 %collective-permute-start.3 = (f32[72,128]{1,0:T(8,128)S(1)}, f32[72,128]{1,0:T(8,128)S(1)}, u32[]{:S(2)}, u32[]{:S(2)}) collective-permute-start(f32[72,128]{1,0:T(8,128)S(1)} %get-tuple-element.23), channel_id=1, source_target_pairs={{0,2},{1,3},{2,0},{3,1},{4,6},{5,7},{6,4},{7,5},{8,10},{9,11},{10,... | collective-permute-start | bytes 110600 | tf_op jit(solution)/shard_map/ppermute | solution.py:254
  20.0 1.5 %collective-permute-done.5.refs_3_ = f32[72,128]{1,0:T(8,128)S(1)} collective-permute-done((f32[72,128]{1,0:T(8,128)S(1)}, f32[72,128]{1,0:T(8,128)S(1)}, u32[]{:S(2)}, u32[]{:S(2)}) %collective-permute-start.5) | collective-permute-done | bytes 36896 | tf_op jit(solution)/shard_map/ppermute | solution.py:254
  21.5 0.4 %collective-permute-done.4.refs_2_ = f32[72,128]{1,0:T(8,128)S(1)} collective-permute-done((f32[72,128]{1,0:T(8,128)S(1)}, f32[72,128]{1,0:T(8,128)S(1)}, u32[]{:S(2)}, u32[]{:S(2)}) %collective-permute-start.4) | collective-permute-done | bytes 36896 | tf_op jit(solution)/shard_map/ppermute | solution.py:254
  21.9 0.7 %collective-permute-done.3.refs_1_ = f32[72,128]{1,0:T(8,128)S(1)} collective-permute-done((f32[72,128]{1,0:T(8,128)S(1)}, f32[72,128]{1,0:T(8,128)S(1)}, u32[]{:S(2)}, u32[]{:S(2)}) %collective-permute-start.3) | collective-permute-done | bytes 36896 | tf_op jit(solution)/shard_map/ppermute | solution.py:254
  22.6 0.2 collective-permute-start.6
  22.8 1.2 %collective-permute-done.6 = f32[4,40,128]{2,1,0:T(8,128)S(1)} collective-permute-done((f32[4,40,128]{2,1,0:T(8,128)S(1)}, f32[4,40,128]{2,1,0:T(8,128)S(1)}, u32[]{:S(2)}, u32[]{:S(2)}) %collective-permute-start.6) | collective-permute-done | bytes 81952 | tf_op jit(solution)/shard_map/ppermute | solution.py:254
  24.0 0.0 copy-done
  24.0 1.8 %downward.1 = f32[8,8192]{1,0:T(8,128)} custom-call(f32[72,128]{1,0:T(8,128)S(1)} %get-tuple-element.24.refs_0_, f32[72,128]{1,0:T(8,128)S(1)} %collective-permute-done.3.refs_1_, f32[72,128]{1,0:T(8,128)S(1)} %collective-permute-done.4.refs_2_, f32[72,128]{1,0:T(8,128)S(1)} %collective-permute-done.5.refs_3_, f32[40,128]{1,0:T(8,128)S(1)} %get-tuple-element.28.refs_4_, ...), custom_call_target="tpu_custom_call" | custom-call | tf_op jit(solution)/shard_map/downward/pallas_call | solution.py:316
  (7 shorter events, 0.0 us)
Async XLA Ops:
  0.0 9.6 %collective-permute-start = (f32[73,512]{1,0:T(8,128)}, f32[73,512]{1,0:T(8,128)S(1)}, u32[]{:S(2)}, u32[]{:S(2)}) collective-permute-start(f32[73,512]{1,0:T(8,128)} %own.1), channel_id=1, source_target_pairs={{0,24},{8,16},{16,8},{24,0},{1,25},{9,17},{17,9},{25,1},{2,26},{10... | collective-permute-start | bytes 448520 | tf_op jit(solution)/shard_map/ppermute | solution.py:254
  5.0 3.8 %collective-permute-start.1 = (s32[64]{0:T(128)}, s32[64]{0:T(128)S(1)}, u32[]{:S(2)}, u32[]{:S(2)}) collective-permute-start(s32[64]{0:T(128)} %source.1), channel_id=1, source_target_pairs={{0,8},{8,0},{16,24},{24,16},{1,9},{9,1},{17,25},{25,17},{2,10},{10... | collective-permute-start | bytes 776 | tf_op jit(solution)/shard_map/ppermute | solution.py:254
  5.1 4.5 %copy-start.1 = (f32[73,512]{1,0:T(8,128)S(1)}, f32[73,512]{1,0:T(8,128)}, u32[]{:S(2)}) copy-start(f32[73,512]{1,0:T(8,128)} %own.1) | copy-start | bytes 448516
  5.1 8.0 %copy-start.2 = (s32[64]{0:T(128)S(1)}, s32[64]{0:T(128)}, u32[]{:S(2)}) copy-start(s32[64]{0:T(128)} %source.1) | copy-start | bytes 772
  5.1 8.0 %copy-start.3 = (s32[64]{0:T(128)S(1)}, s32[64]{0:T(128)}, u32[]{:S(2)}) copy-start(s32[64]{0:T(128)} %target.1) | copy-start | bytes 772
  5.1 8.0 %copy-start.4 = (s32[8]{0:T(128)S(1)}, s32[8]{0:T(128)}, u32[]{:S(2)}) copy-start(s32[8]{0:T(128)} %counts.1) | copy-start | bytes 100
  8.6 15.4 %copy-start = (f32[64,64,128]{2,1,0:T(8,128)S(1)}, f32[64,64,128]{2,1,0:T(8,128)}, u32[]{:S(2)}) copy-start(f32[64,64,128]{2,1,0:T(8,128)} %param.13) | copy-start | bytes 6291460
  9.8 6.1 %collective-permute-start.2 = (f32[64,512]{1,0:T(8,128)S(1)}, f32[64,512]{1,0:T(8,128)S(1)}, u32[]{:S(2)}, u32[]{:S(2)}) collective-permute-start(f32[64,512]{1,0:T(8,128)S(1)} %relay.1), channel_id=1, source_target_pairs={{0,8},{8,0},{16,24},{24,16},{1,9},{9,1},{17,25},{25,17},{2,10},{10... | collective-permute-start | bytes 393224 | tf_op jit(solution)/shard_map/ppermute | solution.py:254
  16.8 4.7 %collective-permute-start.5 = (f32[72,128]{1,0:T(8,128)S(1)}, f32[72,128]{1,0:T(8,128)S(1)}, u32[]{:S(2)}, u32[]{:S(2)}) collective-permute-start(f32[72,128]{1,0:T(8,128)S(1)} %get-tuple-element.21), channel_id=1, source_target_pairs={{0,7},{1,6},{2,5},{3,4},{4,3},{5,2},{6,1},{7,0},{8,15},{9,14},{10,... | collective-permute-start | bytes 110600 | tf_op jit(solution)/shard_map/ppermute | solution.py:254
  17.2 4.7 %collective-permute-start.4 = (f32[72,128]{1,0:T(8,128)S(1)}, f32[72,128]{1,0:T(8,128)S(1)}, u32[]{:S(2)}, u32[]{:S(2)}) collective-permute-start(f32[72,128]{1,0:T(8,128)S(1)} %get-tuple-element.22), channel_id=1, source_target_pairs={{0,4},{1,5},{2,6},{3,7},{4,0},{5,1},{6,2},{7,3},{8,12},{9,13},{10,... | collective-permute-start | bytes 110600 | tf_op jit(solution)/shard_map/ppermute | solution.py:254
  18.5 4.1 %collective-permute-start.3 = (f32[72,128]{1,0:T(8,128)S(1)}, f32[72,128]{1,0:T(8,128)S(1)}, u32[]{:S(2)}, u32[]{:S(2)}) collective-permute-start(f32[72,128]{1,0:T(8,128)S(1)} %get-tuple-element.23), channel_id=1, source_target_pairs={{0,2},{1,3},{2,0},{3,1},{4,6},{5,7},{6,4},{7,5},{8,10},{9,11},{10,... | collective-permute-start | bytes 110600 | tf_op jit(solution)/shard_map/ppermute | solution.py:254
  22.6 1.3 %collective-permute-start.6 = (f32[4,40,128]{2,1,0:T(8,128)S(1)}, f32[4,40,128]{2,1,0:T(8,128)S(1)}, u32[]{:S(2)}, u32[]{:S(2)}) collective-permute-start(f32[4,40,128]{2,1,0:T(8,128)S(1)} %pad_maximum_fusion), channel_id=1, source_target_pairs={{0,1},{1,0},{2,3},{3,2},{4,5},{5,4},{6,7},{7,6},{8,9},{9,8},{10,11... | collective-permute-start | bytes 245768 | tf_op jit(solution)/shard_map/ppermute | solution.py:254

commit v8 on v7

--- a/solution.py
+++ b/solution.py
@@ -106,15 +106,20 @@
         code[p] = value.astype(F32)
 
 
-def relay(theirs, own, far, out):
+def relay_own(theirs, own, part, hot):
     ncl, width = own.shape
     grp = lax.axis_index("grp")
     row = iota((128, theirs.shape[1]), 0)
-    hot = jnp.concatenate([theirs[...] - ncl * grp == row, theirs[...] - ncl * (grp ^ 3) == row], axis=0)
-    hot = jnp.where(hot, 1.0, 0.0).T.astype(BF)
-    none = jnp.zeros((128 - ncl, width), F32)
-    high, low = split(jnp.concatenate([own[...], none, far[...], none], axis=0))
-    out[...] = mm(hot, high) + mm(hot, low)
+    mine = jnp.where(theirs[...] - ncl * grp == row, 1.0, 0.0).T.astype(BF)
+    hot[...] = jnp.where(theirs[...] - ncl * (grp ^ 3) == row, 1.0, 0.0).T.astype(BF)
+    high, low = split(jnp.concatenate([own[...], jnp.zeros((128 - ncl, width), F32)], axis=0))
+    part[...] = mm(mine, high) + mm(mine, low)
+
+
+def relay(part, hot, far, out):
+    ncl, width = far.shape
+    high, low = split(jnp.concatenate([far[...], jnp.zeros((128 - ncl, width), F32)], axis=0))
+    out[...] = part[...] + (mm(hot[...], high) + mm(hot[...], low))
 
 
 def couple(two_step, parts, *refs):
@@ -256,7 +261,14 @@
     if two_step:
         far = moved(coeff_in, "grp", ngrp, lambda i: i ^ 3)
         theirs = moved(source, "grp", ngrp, lambda i: i ^ 1)
-        far, theirs = lax.optimization_barrier((far, theirs))
+        part, hot = pl.pallas_call(
+            relay_own,
+            out_shape=(shape((nblocks, width), F32), shape((nblocks, 128), BF)),
+            in_specs=[VMEM] * 2,
+            out_specs=(VMEM,) * 2,
+            compiler_params=pltpu.CompilerParams(vmem_limit_bytes=16 << 20),
+            name="relay_own",
+        )(theirs.reshape(1, nblocks), coeff_in)
         far, ct = lax.optimization_barrier((far, ct))
         across = pl.pallas_call(
             relay,
@@ -265,7 +277,7 @@
             out_specs=VMEM,
             compiler_params=pltpu.CompilerParams(vmem_limit_bytes=16 << 20),
             name="relay",
-        )(theirs.reshape(1, nblocks), coeff_in, far)
+        )(part, hot, far)
         across = moved(across, "grp", ngrp, lambda i: i ^ 1)
         tables = [coeff_in, far]
     else:

time: 26 us -> 25.9 us (level)
  transfers between devices with their start and end apart: 7 -> 7, of which waited for: 7 -> 7; matrix products, arithmetic and copies ran while one was open for 0% -> 0% of each run, Pallas kernels for 18% -> 19%
where the time goes in v8:
time: 25.9 us; the launch traced here: 25.8 us
  starting transfers between devices  11.6 us (45%)
  Pallas kernels  7.65 us (30%)
  waiting for transfers between devices  6.38 us (25%)
    ppermute x7, starting transfers between devices, moved(): return lax.ppermute(x, axis, [(i, to(i)) for i in range(n)])  11.6 us
    ppermute x7, waiting for transfers between devices, moved(): return lax.ppermute(x, axis, [(i, to(i)) for i in range(n)])  6.38 us
    pallas_call x1, Pallas kernels, on_device(): pl.pallas_call(prepare, out_shape=(ct, tr), in_specs=[ANY, ANY], out_spec...  3.47 us
    pallas_call x1, Pallas kernels, on_device(): pl.pallas_call(functools.partial(downward, kinds), out_shape=shape((RHS,...  1.84 us
    pallas_call x1, Pallas kernels, on_device(): pl.pallas_call(functools.partial(pick, two_step), out_shape=(shape((nbloc...  1.1 us
    pallas_call x1, Pallas kernels, on_device(): pl.pallas_call(functools.partial(couple, two_step, len(picked)), out_shap...  0.82 us
  transfers between devices with their start and end apart: 7, of which 7 were waited for; matrix products, arithmetic and copies ran while one was open for 0% of the time, Pallas kernels for 19%

profile of v8, /device:TPU:0, one launch (start us, length us, event | category | flops | bytes accessed | tf_op | source)
XLA Modules:
  0.0 25.8 jit_solution(86988221332802682)
XLA Ops:
  0.0 5.0 %collective-permute-start = (f32[73,512]{1,0:T(8,128)}, f32[73,512]{1,0:T(8,128)S(1)}, u32[]{:S(2)}, u32[]{:S(2)}) collective-permute-start(f32[73,512]{1,0:T(8,128)} %own.1), channel_id=1, source_target_pairs={{0,24},{8,16},{16,8},{24,0},{1,25},{9,17},{17,9},{25,1},{2,26},{10... | collective-permute-start | bytes 448520 | tf_op jit(solution)/shard_map/ppermute | solution.py:259
  5.0 0.0 collective-permute-start.1
  5.1 0.0 copy-start.1
  5.1 0.0 copy-start.2
  5.1 0.0 copy-start.3
  5.1 0.0 copy-start.4
  5.1 3.5 %prepare.1 = (bf16[8,256,256]{2,1,0:T(8,128)(2,1)S(1)}, bf16[576,1024]{1,0:T(8,128)(2,1)S(1)}) custom-call(f32[64,64,64]{2,1,0:T(8,128)} %coupling_in.1, f32[64,64,72]{2,1,0:T(8,128)} %bitcast.27), custom_call_target="tpu_custom_call" | custom-call | bytes 10485760 | tf_op jit(solution)/shard_map/prepare/pallas_call | solution.py:242
  8.6 0.0 copy-start
  8.6 0.3 %collective-permute-done.1 = s32[64]{0:T(128)S(1)} collective-permute-done((s32[64]{0:T(128)}, s32[64]{0:T(128)S(1)}, u32[]{:S(2)}, u32[]{:S(2)}) %collective-permute-start.1) | collective-permute-done | bytes 288 | tf_op jit(solution)/shard_map/ppermute | solution.py:259
  8.9 0.0 copy-done.1
  8.9 0.2 relay_own.1
  9.1 0.5 %collective-permute-done.refs_1_.far = f32[73,512]{1,0:T(8,128)S(1)} collective-permute-done((f32[73,512]{1,0:T(8,128)}, f32[73,512]{1,0:T(8,128)S(1)}, u32[]{:S(2)}, u32[]{:S(2)}) %collective-permute-start) | collective-permute-done | bytes 149536 | tf_op jit(solution)/shard_map/ppermute | solution.py:259
  9.6 0.2 relay.1
  9.8 3.2 %collective-permute-start.2 = (f32[64,512]{1,0:T(8,128)S(1)}, f32[64,512]{1,0:T(8,128)S(1)}, u32[]{:S(2)}, u32[]{:S(2)}) collective-permute-start(f32[64,512]{1,0:T(8,128)S(1)} %relay.1), channel_id=1, source_target_pairs={{0,8},{8,0},{16,24},{24,16},{1,9},{9,1},{17,25},{25,17},{2,10},{10... | collective-permute-start | bytes 393224 | tf_op jit(solution)/shard_map/ppermute | solution.py:259
  12.9 0.0 copy-done.2
  12.9 0.0 copy-done.3
  12.9 0.0 copy-done.4
  12.9 1.1 %pick.1 = (f32[64,512]{1,0:T(8,128)S(1)}, f32[8,8,128]{2,1,0:T(8,128)S(1)}) custom-call(s32[64]{0:T(128)S(1)} %copy-done.2, s32[64]{0:T(128)S(1)} %copy-done.3, s32[8]{0:T(128)S(1)} %copy-done.4, f32[73,512]{1,0:T(8,128)S(1)} %copy-done.1, f32[73,512]{1,0:T(8,128)S(1)} %collective-permute-done.refs_1_.far), custom_call_target="tpu_custom_call" | custom-call | tf_op jit(solution)/shard_map/pick/pallas_call | solution.py:289
  14.1 1.8 %collective-permute-done.2.refs_1_ = f32[64,512]{1,0:T(8,128)S(1)} collective-permute-done((f32[64,512]{1,0:T(8,128)S(1)}, f32[64,512]{1,0:T(8,128)S(1)}, u32[]{:S(2)}, u32[]{:S(2)}) %collective-permute-start.2) | collective-permute-done | bytes 131104 | tf_op jit(solution)/shard_map/ppermute | solution.py:259
  15.9 0.8 %couple.1 = f32[4,72,128]{2,1,0:T(8,128)S(1)} custom-call(f32[64,512]{1,0:T(8,128)S(1)} %get-tuple-element.15.refs_0_, f32[64,512]{1,0:T(8,128)S(1)} %collective-permute-done.2.refs_1_, bf16[8,256,256]{2,1,0:T(8,128)(2,1)S(1)} %get-tuple-element.18.refs_2_, f32[8,8,128]{2,1,0:T(8,128)S(1)} %get-tuple-element.19.refs_3_), custom_call_target="tpu_custom_call" | custom-call | tf_op jit(solution)/shard_map/couple/pallas_call | solution.py:301
  16.7 0.4 %collective-permute-start.5 = (f32[72,128]{1,0:T(8,128)S(1)}, f32[72,128]{1,0:T(8,128)S(1)}, u32[]{:S(2)}, u32[]{:S(2)}) collective-permute-start(f32[72,128]{1,0:T(8,128)S(1)} %get-tuple-element.21), channel_id=1, source_target_pairs={{0,7},{1,6},{2,5},{3,4},{4,3},{5,2},{6,1},{7,0},{8,15},{9,14},{10,... | collective-permute-start | bytes 110600 | tf_op jit(solution)/shard_map/ppermute | solution.py:259
  17.1 1.3 %collective-permute-start.4 = (f32[72,128]{1,0:T(8,128)S(1)}, f32[72,128]{1,0:T(8,128)S(1)}, u32[]{:S(2)}, u32[]{:S(2)}) collective-permute-start(f32[72,128]{1,0:T(8,128)S(1)} %get-tuple-element.22), channel_id=1, source_target_pairs={{0,4},{1,5},{2,6},{3,7},{4,0},{5,1},{6,2},{7,3},{8,12},{9,13},{10,... | collective-permute-start | bytes 110600 | tf_op jit(solution)/shard_map/ppermute | solution.py:259
  18.4 1.5 %collective-permute-start.3 = (f32[72,128]{1,0:T(8,128)S(1)}, f32[72,128]{1,0:T(8,128)S(1)}, u32[]{:S(2)}, u32[]{:S(2)}) collective-permute-start(f32[72,128]{1,0:T(8,128)S(1)} %get-tuple-element.23), channel_id=1, source_target_pairs={{0,2},{1,3},{2,0},{3,1},{4,6},{5,7},{6,4},{7,5},{8,10},{9,11},{10,... | collective-permute-start | bytes 110600 | tf_op jit(solution)/shard_map/ppermute | solution.py:259
  19.9 1.5 %collective-permute-done.5.refs_3_ = f32[72,128]{1,0:T(8,128)S(1)} collective-permute-done((f32[72,128]{1,0:T(8,128)S(1)}, f32[72,128]{1,0:T(8,128)S(1)}, u32[]{:S(2)}, u32[]{:S(2)}) %collective-permute-start.5) | collective-permute-done | bytes 36896 | tf_op jit(solution)/shard_map/ppermute | solution.py:259
  21.4 0.4 %collective-permute-done.4.refs_2_ = f32[72,128]{1,0:T(8,128)S(1)} collective-permute-done((f32[72,128]{1,0:T(8,128)S(1)}, f32[72,128]{1,0:T(8,128)S(1)}, u32[]{:S(2)}, u32[]{:S(2)}) %collective-permute-start.4) | collective-permute-done | bytes 36896 | tf_op jit(solution)/shard_map/ppermute | solution.py:259
  21.9 0.7 %collective-permute-done.3.refs_1_ = f32[72,128]{1,0:T(8,128)S(1)} collective-permute-done((f32[72,128]{1,0:T(8,128)S(1)}, f32[72,128]{1,0:T(8,128)S(1)}, u32[]{:S(2)}, u32[]{:S(2)}) %collective-permute-start.3) | collective-permute-done | bytes 36896 | tf_op jit(solution)/shard_map/ppermute | solution.py:259
  22.6 0.2 collective-permute-start.6
  22.7 1.2 %collective-permute-done.6 = f32[4,40,128]{2,1,0:T(8,128)S(1)} collective-permute-done((f32[4,40,128]{2,1,0:T(8,128)S(1)}, f32[4,40,128]{2,1,0:T(8,128)S(1)}, u32[]{:S(2)}, u32[]{:S(2)}) %collective-permute-start.6) | collective-permute-done | bytes 81952 | tf_op jit(solution)/shard_map/ppermute | solution.py:259
  23.9 0.0 copy-done
  23.9 1.8 %downward.1 = f32[8,8192]{1,0:T(8,128)} custom-call(f32[72,128]{1,0:T(8,128)S(1)} %get-tuple-element.24.refs_0_, f32[72,128]{1,0:T(8,128)S(1)} %collective-permute-done.3.refs_1_, f32[72,128]{1,0:T(8,128)S(1)} %collective-permute-done.4.refs_2_, f32[72,128]{1,0:T(8,128)S(1)} %collective-permute-done.5.refs_3_, f32[40,128]{1,0:T(8,128)S(1)} %get-tuple-element.28.refs_4_, ...), custom_call_target="tpu_custom_call" | custom-call | tf_op jit(solution)/shard_map/downward/pallas_call | solution.py:328
  (7 shorter events, 0.0 us)
Async XLA Ops:
  0.0 9.6 %collective-permute-start = (f32[73,512]{1,0:T(8,128)}, f32[73,512]{1,0:T(8,128)S(1)}, u32[]{:S(2)}, u32[]{:S(2)}) collective-permute-start(f32[73,512]{1,0:T(8,128)} %own.1), channel_id=1, source_target_pairs={{0,24},{8,16},{16,8},{24,0},{1,25},{9,17},{17,9},{25,1},{2,26},{10... | collective-permute-start | bytes 448520 | tf_op jit(solution)/shard_map/ppermute | solution.py:259
  5.0 3.8 %collective-permute-start.1 = (s32[64]{0:T(128)}, s32[64]{0:T(128)S(1)}, u32[]{:S(2)}, u32[]{:S(2)}) collective-permute-start(s32[64]{0:T(128)} %source.1), channel_id=1, source_target_pairs={{0,8},{8,0},{16,24},{24,16},{1,9},{9,1},{17,25},{25,17},{2,10},{10... | collective-permute-start | bytes 776 | tf_op jit(solution)/shard_map/ppermute | solution.py:259
  5.1 3.8 %copy-start.1 = (f32[73,512]{1,0:T(8,128)S(1)}, f32[73,512]{1,0:T(8,128)}, u32[]{:S(2)}) copy-start(f32[73,512]{1,0:T(8,128)} %own.1) | copy-start | bytes 448516
  5.1 7.9 %copy-start.2 = (s32[64]{0:T(128)S(1)}, s32[64]{0:T(128)}, u32[]{:S(2)}) copy-start(s32[64]{0:T(128)} %source.1) | copy-start | bytes 772
  5.1 7.9 %copy-start.3 = (s32[64]{0:T(128)S(1)}, s32[64]{0:T(128)}, u32[]{:S(2)}) copy-start(s32[64]{0:T(128)} %target.1) | copy-start | bytes 772
  5.1 7.9 %copy-start.4 = (s32[8]{0:T(128)S(1)}, s32[8]{0:T(128)}, u32[]{:S(2)}) copy-start(s32[8]{0:T(128)} %counts.1) | copy-start | bytes 100
  8.6 15.4 %copy-start = (f32[64,64,128]{2,1,0:T(8,128)S(1)}, f32[64,64,128]{2,1,0:T(8,128)}, u32[]{:S(2)}) copy-start(f32[64,64,128]{2,1,0:T(8,128)} %param.13) | copy-start | bytes 6291460
  9.8 6.1 %collective-permute-start.2 = (f32[64,512]{1,0:T(8,128)S(1)}, f32[64,512]{1,0:T(8,128)S(1)}, u32[]{:S(2)}, u32[]{:S(2)}) collective-permute-start(f32[64,512]{1,0:T(8,128)S(1)} %relay.1), channel_id=1, source_target_pairs={{0,8},{8,0},{16,24},{24,16},{1,9},{9,1},{17,25},{25,17},{2,10},{10... | collective-permute-start | bytes 393224 | tf_op jit(solution)/shard_map/ppermute | solution.py:259
  16.7 4.7 %collective-permute-start.5 = (f32[72,128]{1,0:T(8,128)S(1)}, f32[72,128]{1,0:T(8,128)S(1)}, u32[]{:S(2)}, u32[]{:S(2)}) collective-permute-start(f32[72,128]{1,0:T(8,128)S(1)} %get-tuple-element.21), channel_id=1, source_target_pairs={{0,7},{1,6},{2,5},{3,4},{4,3},{5,2},{6,1},{7,0},{8,15},{9,14},{10,... | collective-permute-start | bytes 110600 | tf_op jit(solution)/shard_map/ppermute | solution.py:259
  17.1 4.7 %collective-permute-start.4 = (f32[72,128]{1,0:T(8,128)S(1)}, f32[72,128]{1,0:T(8,128)S(1)}, u32[]{:S(2)}, u32[]{:S(2)}) collective-permute-start(f32[72,128]{1,0:T(8,128)S(1)} %get-tuple-element.22), channel_id=1, source_target_pairs={{0,4},{1,5},{2,6},{3,7},{4,0},{5,1},{6,2},{7,3},{8,12},{9,13},{10,... | collective-permute-start | bytes 110600 | tf_op jit(solution)/shard_map/ppermute | solution.py:259
  18.4 4.1 %collective-permute-start.3 = (f32[72,128]{1,0:T(8,128)S(1)}, f32[72,128]{1,0:T(8,128)S(1)}, u32[]{:S(2)}, u32[]{:S(2)}) collective-permute-start(f32[72,128]{1,0:T(8,128)S(1)} %get-tuple-element.23), channel_id=1, source_target_pairs={{0,2},{1,3},{2,0},{3,1},{4,6},{5,7},{6,4},{7,5},{8,10},{9,11},{10,... | collective-permute-start | bytes 110600 | tf_op jit(solution)/shard_map/ppermute | solution.py:259
  22.6 1.3 %collective-permute-start.6 = (f32[4,40,128]{2,1,0:T(8,128)S(1)}, f32[4,40,128]{2,1,0:T(8,128)S(1)}, u32[]{:S(2)}, u32[]{:S(2)}) collective-permute-start(f32[4,40,128]{2,1,0:T(8,128)S(1)} %pad_maximum_fusion), channel_id=1, source_target_pairs={{0,1},{1,0},{2,3},{3,2},{4,5},{5,4},{6,7},{7,6},{8,9},{9,8},{10,11... | collective-permute-start | bytes 245768 | tf_op jit(solution)/shard_map/ppermute | solution.py:259

commit v9 on v8

--- a/solution.py
+++ b/solution.py
@@ -79,7 +79,7 @@
 
 
 def pick(two_step, source, target, counts, *refs):
-    tables, (early, code, rows) = refs[:-3], refs[-3:]
+    tables, (early, code, turn, rows) = refs[:-4], refs[-4:]
     nmember, ncl = rows.shape[:2]
     nmember = nmember + 1 if two_step else nmember
     grp = lax.axis_index("grp")
@@ -104,6 +104,9 @@
             at = jnp.where(slot < counts[p], target[SLOTS * p + slot] * RHS, -RHS)
             value = jnp.where(here, at + lane % RHS, value)
         code[p] = value.astype(F32)
+    place, to = iota(turn.shape, 0), iota(turn.shape, 1)
+    same = (place // RHS == to % RANK) & (place % RHS // 2 == to // RANK)
+    turn[...] = jnp.where(same, 1.0, 0.0).astype(BF)
 
 
 def relay_own(theirs, own, part, hot):
@@ -123,16 +126,13 @@
 
 
 def couple(two_step, parts, *refs):
-    early, (ct, code, out, held_a, held_b) = refs[:parts], refs[parts:]
+    early, (turn, ct, code, out, held_a, held_b) = refs[:parts], refs[parts:]
     nblocks, width = early[0].shape
     wide = lax.axis_index("wide") if two_step else 0
     picked = sum(part[...] for part in early)
-    place, to = iota((width, 256), 0), iota((width, 256), 1)
-    turn = (place // RHS == to % RANK) & (place % RHS // 2 == to // RANK)
-    turn = jnp.where(turn, 1.0, 0.0).astype(BF)
     odd = iota((nblocks, width), 1) % 2
     high, low = split(jnp.concatenate([jnp.where(odd == i, picked, 0.0) for i in range(2)], axis=0))
-    turned = mm(jnp.concatenate([high, low], axis=0), turn)
+    turned = mm(jnp.concatenate([high, low], axis=0), turn[...])
     turned = turned[: 2 * nblocks] + turned[2 * nblocks :]
     first = iota((nblocks, 128), 1) < RANK
     own = iota((nblocks, 128), 0) % HALF - iota((nblocks, 128), 1) // RANK
@@ -286,11 +286,11 @@
             tables.append(moved(coeff_in, "grp", ngrp, lambda i: (i + k) % ngrp))
 
     held = (3 if two_step else ngrp, ncl, width)
-    early, code = pl.pallas_call(
+    early, code, turn = pl.pallas_call(
         functools.partial(pick, two_step),
-        out_shape=(shape((nblocks, width), F32), shape((nwide, 8, 128), F32)),
+        out_shape=(shape((nblocks, width), F32), shape((nwide, 8, 128), F32), shape((width, 256), BF)),
         in_specs=[SMEM] * 3 + [VMEM] * len(tables),
-        out_specs=(VMEM,) * 2,
+        out_specs=(VMEM,) * 3,
         scratch_shapes=[pltpu.VMEM(held, F32)],
         compiler_params=pltpu.CompilerParams(vmem_limit_bytes=16 << 20),
         name="pick",
@@ -301,12 +301,12 @@
     out = pl.pallas_call(
         functools.partial(couple, two_step, len(picked)),
         out_shape=shape((nwide // 2, 72, 128), F32),
-        in_specs=[VMEM] * (len(picked) + 2),
+        in_specs=[VMEM] * (len(picked) + 3),
         out_specs=VMEM,
         scratch_shapes=[pltpu.VMEM((nblocks * RHS, 128), F32)] * 2,
         compiler_params=pltpu.CompilerParams(vmem_limit_bytes=32 << 20),
         name="couple",
-    )(*picked, ct, code)
+    )(*picked, turn, ct, code)
 
     if two_step:
         arrived = [out[0]]

time: 25.9 us -> 25.8 us (level)
  transfers between devices with their start and end apart: 7 -> 7, of which waited for: 7 -> 7; matrix products, arithmetic and copies ran while one was open for 0% -> 0% of each run, Pallas kernels for 19% -> 20%
where the time goes in v9:
time: 25.8 us; the launch traced here: 25.7 us
  starting transfers between devices  11.6 us (45%)
  Pallas kernels  7.79 us (30%)
  waiting for transfers between devices  6.19 us (24%)
    ppermute x7, starting transfers between devices, moved(): return lax.ppermute(x, axis, [(i, to(i)) for i in range(n)])  11.6 us
    ppermute x7, waiting for transfers between devices, moved(): return lax.ppermute(x, axis, [(i, to(i)) for i in range(n)])  6.19 us
    pallas_call x1, Pallas kernels, on_device(): pl.pallas_call(prepare, out_shape=(ct, tr), in_specs=[ANY, ANY], out_spec...  3.47 us
    pallas_call x1, Pallas kernels, on_device(): pl.pallas_call(functools.partial(downward, kinds), out_shape=shape((RHS,...  1.85 us
    pallas_call x1, Pallas kernels, on_device(): pl.pallas_call(functools.partial(pick, two_step), out_shape=(shape((nbloc...  1.32 us
    pallas_call x1, Pallas kernels, on_device(): pl.pallas_call(functools.partial(couple, two_step, len(picked)), out_shap...  0.75 us
  transfers between devices with their start and end apart: 7, of which 7 were waited for; matrix products, arithmetic and copies ran while one was open for 0% of the time, Pallas kernels for 20%

profile of v9, /device:TPU:0, one launch (start us, length us, event | category | flops | bytes accessed | tf_op | source)
XLA Modules:
  0.0 25.7 jit_solution(6744565975139419966)
XLA Ops:
  0.0 5.0 %collective-permute-start = (f32[73,512]{1,0:T(8,128)}, f32[73,512]{1,0:T(8,128)S(1)}, u32[]{:S(2)}, u32[]{:S(2)}) collective-permute-start(f32[73,512]{1,0:T(8,128)} %own.1), channel_id=1, source_target_pairs={{0,24},{8,16},{16,8},{24,0},{1,25},{9,17},{17,9},{25,1},{2,26},{10... | collective-permute-start | bytes 448520 | tf_op jit(solution)/shard_map/ppermute | solution.py:259
  5.0 0.0 collective-permute-start.1
  5.1 0.0 copy-start.1
  5.1 0.0 copy-start.2
  5.1 0.0 copy-start.3
  5.1 0.0 copy-start.4
  5.1 3.5 %prepare.1 = (bf16[8,256,256]{2,1,0:T(8,128)(2,1)S(1)}, bf16[576,1024]{1,0:T(8,128)(2,1)S(1)}) custom-call(f32[64,64,64]{2,1,0:T(8,128)} %coupling_in.1, f32[64,64,72]{2,1,0:T(8,128)} %bitcast.27), custom_call_target="tpu_custom_call" | custom-call | bytes 10485760 | tf_op jit(solution)/shard_map/prepare/pallas_call | solution.py:242
  8.6 0.0 copy-start
  8.6 0.3 %collective-permute-done.1 = s32[64]{0:T(128)S(1)} collective-permute-done((s32[64]{0:T(128)}, s32[64]{0:T(128)S(1)}, u32[]{:S(2)}, u32[]{:S(2)}) %collective-permute-start.1) | collective-permute-done | bytes 288 | tf_op jit(solution)/shard_map/ppermute | solution.py:259
  8.9 0.0 copy-done.1
  8.9 0.2 relay_own.1
  9.1 0.5 %collective-permute-done.refs_1_.far = f32[73,512]{1,0:T(8,128)S(1)} collective-permute-done((f32[73,512]{1,0:T(8,128)}, f32[73,512]{1,0:T(8,128)S(1)}, u32[]{:S(2)}, u32[]{:S(2)}) %collective-permute-start) | collective-permute-done | bytes 149536 | tf_op jit(solution)/shard_map/ppermute | solution.py:259
  9.6 0.2 relay.1
  9.8 3.2 %collective-permute-start.2 = (f32[64,512]{1,0:T(8,128)S(1)}, f32[64,512]{1,0:T(8,128)S(1)}, u32[]{:S(2)}, u32[]{:S(2)}) collective-permute-start(f32[64,512]{1,0:T(8,128)S(1)} %relay.1), channel_id=1, source_target_pairs={{0,8},{8,0},{16,24},{24,16},{1,9},{9,1},{17,25},{25,17},{2,10},{10... | collective-permute-start | bytes 393224 | tf_op jit(solution)/shard_map/ppermute | solution.py:259
  12.9 0.0 copy-done.2
  12.9 0.0 copy-done.3
  12.9 0.0 copy-done.4
  12.9 1.3 %pick.1 = (f32[64,512]{1,0:T(8,128)S(1)}, f32[8,8,128]{2,1,0:T(8,128)S(1)}, bf16[512,256]{1,0:T(8,128)(2,1)S(1)}) custom-call(s32[64]{0:T(128)S(1)} %copy-done.2, s32[64]{0:T(128)S(1)} %copy-done.3, s32[8]{0:T(128)S(1)} %copy-done.4, f32[73,512]{1,0:T(8,128)S(1)} %copy-done.1, f32[73,512]{1,0:T(8,128)S(1)} %collective-permute-done.refs_1_.far), custom_call_target="tpu_custom_call" | custom-call | tf_op jit(solution)/shard_map/pick/pallas_call | solution.py:289
  14.3 1.6 %collective-permute-done.2.refs_1_ = f32[64,512]{1,0:T(8,128)S(1)} collective-permute-done((f32[64,512]{1,0:T(8,128)S(1)}, f32[64,512]{1,0:T(8,128)S(1)}, u32[]{:S(2)}, u32[]{:S(2)}) %collective-permute-start.2) | collective-permute-done | bytes 131104 | tf_op jit(solution)/shard_map/ppermute | solution.py:259
  15.9 0.7 %couple.1 = f32[4,72,128]{2,1,0:T(8,128)S(1)} custom-call(f32[64,512]{1,0:T(8,128)S(1)} %get-tuple-element.16.refs_0_, f32[64,512]{1,0:T(8,128)S(1)} %collective-permute-done.2.refs_1_, bf16[512,256]{1,0:T(8,128)(2,1)S(1)} %get-tuple-element.19.refs_2_, bf16[8,256,256]{2,1,0:T(8,128)(2,1)S(1)} %get-tuple-element.20.refs_3_, ...), custom_call_target="tpu_custom_call" | custom-call | tf_op jit(solution)/shard_map/couple/pallas_call | solution.py:301
  16.7 0.4 %collective-permute-start.5 = (f32[72,128]{1,0:T(8,128)S(1)}, f32[72,128]{1,0:T(8,128)S(1)}, u32[]{:S(2)}, u32[]{:S(2)}) collective-permute-start(f32[72,128]{1,0:T(8,128)S(1)} %get-tuple-element.23), channel_id=1, source_target_pairs={{0,7},{1,6},{2,5},{3,4},{4,3},{5,2},{6,1},{7,0},{8,15},{9,14},{10,... | collective-permute-start | bytes 110600 | tf_op jit(solution)/shard_map/ppermute | solution.py:259
  17.1 1.3 %collective-permute-start.4 = (f32[72,128]{1,0:T(8,128)S(1)}, f32[72,128]{1,0:T(8,128)S(1)}, u32[]{:S(2)}, u32[]{:S(2)}) collective-permute-start(f32[72,128]{1,0:T(8,128)S(1)} %get-tuple-element.24), channel_id=1, source_target_pairs={{0,4},{1,5},{2,6},{3,7},{4,0},{5,1},{6,2},{7,3},{8,12},{9,13},{10,... | collective-permute-start | bytes 110600 | tf_op jit(solution)/shard_map/ppermute | solution.py:259
  18.3 1.5 %collective-permute-start.3 = (f32[72,128]{1,0:T(8,128)S(1)}, f32[72,128]{1,0:T(8,128)S(1)}, u32[]{:S(2)}, u32[]{:S(2)}) collective-permute-start(f32[72,128]{1,0:T(8,128)S(1)} %get-tuple-element.25), channel_id=1, source_target_pairs={{0,2},{1,3},{2,0},{3,1},{4,6},{5,7},{6,4},{7,5},{8,10},{9,11},{10,... | collective-permute-start | bytes 110600 | tf_op jit(solution)/shard_map/ppermute | solution.py:259
  19.8 1.5 %collective-permute-done.5.refs_3_ = f32[72,128]{1,0:T(8,128)S(1)} collective-permute-done((f32[72,128]{1,0:T(8,128)S(1)}, f32[72,128]{1,0:T(8,128)S(1)}, u32[]{:S(2)}, u32[]{:S(2)}) %collective-permute-start.5) | collective-permute-done | bytes 36896 | tf_op jit(solution)/shard_map/ppermute | solution.py:259
  21.4 0.4 %collective-permute-done.4.refs_2_ = f32[72,128]{1,0:T(8,128)S(1)} collective-permute-done((f32[72,128]{1,0:T(8,128)S(1)}, f32[72,128]{1,0:T(8,128)S(1)}, u32[]{:S(2)}, u32[]{:S(2)}) %collective-permute-start.4) | collective-permute-done | bytes 36896 | tf_op jit(solution)/shard_map/ppermute | solution.py:259
  21.8 0.7 %collective-permute-done.3.refs_1_ = f32[72,128]{1,0:T(8,128)S(1)} collective-permute-done((f32[72,128]{1,0:T(8,128)S(1)}, f32[72,128]{1,0:T(8,128)S(1)}, u32[]{:S(2)}, u32[]{:S(2)}) %collective-permute-start.3) | collective-permute-done | bytes 36896 | tf_op jit(solution)/shard_map/ppermute | solution.py:259
  22.5 0.2 collective-permute-start.6
  22.7 1.2 %collective-permute-done.6 = f32[4,40,128]{2,1,0:T(8,128)S(1)} collective-permute-done((f32[4,40,128]{2,1,0:T(8,128)S(1)}, f32[4,40,128]{2,1,0:T(8,128)S(1)}, u32[]{:S(2)}, u32[]{:S(2)}) %collective-permute-start.6) | collective-permute-done | bytes 81952 | tf_op jit(solution)/shard_map/ppermute | solution.py:259
  23.8 0.0 copy-done
  23.8 1.8 %downward.1 = f32[8,8192]{1,0:T(8,128)} custom-call(f32[72,128]{1,0:T(8,128)S(1)} %get-tuple-element.26.refs_0_, f32[72,128]{1,0:T(8,128)S(1)} %collective-permute-done.3.refs_1_, f32[72,128]{1,0:T(8,128)S(1)} %collective-permute-done.4.refs_2_, f32[72,128]{1,0:T(8,128)S(1)} %collective-permute-done.5.refs_3_, f32[40,128]{1,0:T(8,128)S(1)} %get-tuple-element.30.refs_4_, ...), custom_call_target="tpu_custom_call" | custom-call | tf_op jit(solution)/shard_map/downward/pallas_call | solution.py:328
  (7 shorter events, 0.0 us)
Async XLA Ops:
  0.0 9.6 %collective-permute-start = (f32[73,512]{1,0:T(8,128)}, f32[73,512]{1,0:T(8,128)S(1)}, u32[]{:S(2)}, u32[]{:S(2)}) collective-permute-start(f32[73,512]{1,0:T(8,128)} %own.1), channel_id=1, source_target_pairs={{0,24},{8,16},{16,8},{24,0},{1,25},{9,17},{17,9},{25,1},{2,26},{10... | collective-permute-start | bytes 448520 | tf_op jit(solution)/shard_map/ppermute | solution.py:259
  5.0 3.8 %collective-permute-start.1 = (s32[64]{0:T(128)}, s32[64]{0:T(128)S(1)}, u32[]{:S(2)}, u32[]{:S(2)}) collective-permute-start(s32[64]{0:T(128)} %source.1), channel_id=1, source_target_pairs={{0,8},{8,0},{16,24},{24,16},{1,9},{9,1},{17,25},{25,17},{2,10},{10... | collective-permute-start | bytes 776 | tf_op jit(solution)/shard_map/ppermute | solution.py:259
  5.1 3.8 %copy-start.1 = (f32[73,512]{1,0:T(8,128)S(1)}, f32[73,512]{1,0:T(8,128)}, u32[]{:S(2)}) copy-start(f32[73,512]{1,0:T(8,128)} %own.1) | copy-start | bytes 448516
  5.1 7.9 %copy-start.2 = (s32[64]{0:T(128)S(1)}, s32[64]{0:T(128)}, u32[]{:S(2)}) copy-start(s32[64]{0:T(128)} %source.1) | copy-start | bytes 772
  5.1 7.9 %copy-start.3 = (s32[64]{0:T(128)S(1)}, s32[64]{0:T(128)}, u32[]{:S(2)}) copy-start(s32[64]{0:T(128)} %target.1) | copy-start | bytes 772
  5.1 7.9 %copy-start.4 = (s32[8]{0:T(128)S(1)}, s32[8]{0:T(128)}, u32[]{:S(2)}) copy-start(s32[8]{0:T(128)} %counts.1) | copy-start | bytes 100
  8.6 15.3 %copy-start = (f32[64,64,128]{2,1,0:T(8,128)S(1)}, f32[64,64,128]{2,1,0:T(8,128)}, u32[]{:S(2)}) copy-start(f32[64,64,128]{2,1,0:T(8,128)} %param.13) | copy-start | bytes 6291460
  9.8 6.1 %collective-permute-start.2 = (f32[64,512]{1,0:T(8,128)S(1)}, f32[64,512]{1,0:T(8,128)S(1)}, u32[]{:S(2)}, u32[]{:S(2)}) collective-permute-start(f32[64,512]{1,0:T(8,128)S(1)} %relay.1), channel_id=1, source_target_pairs={{0,8},{8,0},{16,24},{24,16},{1,9},{9,1},{17,25},{25,17},{2,10},{10... | collective-permute-start | bytes 393224 | tf_op jit(solution)/shard_map/ppermute | solution.py:259
  16.7 4.7 %collective-permute-start.5 = (f32[72,128]{1,0:T(8,128)S(1)}, f32[72,128]{1,0:T(8,128)S(1)}, u32[]{:S(2)}, u32[]{:S(2)}) collective-permute-start(f32[72,128]{1,0:T(8,128)S(1)} %get-tuple-element.23), channel_id=1, source_target_pairs={{0,7},{1,6},{2,5},{3,4},{4,3},{5,2},{6,1},{7,0},{8,15},{9,14},{10,... | collective-permute-start | bytes 110600 | tf_op jit(solution)/shard_map/ppermute | solution.py:259
  17.1 4.7 %collective-permute-start.4 = (f32[72,128]{1,0:T(8,128)S(1)}, f32[72,128]{1,0:T(8,128)S(1)}, u32[]{:S(2)}, u32[]{:S(2)}) collective-permute-start(f32[72,128]{1,0:T(8,128)S(1)} %get-tuple-element.24), channel_id=1, source_target_pairs={{0,4},{1,5},{2,6},{3,7},{4,0},{5,1},{6,2},{7,3},{8,12},{9,13},{10,... | collective-permute-start | bytes 110600 | tf_op jit(solution)/shard_map/ppermute | solution.py:259
  18.3 4.1 %collective-permute-start.3 = (f32[72,128]{1,0:T(8,128)S(1)}, f32[72,128]{1,0:T(8,128)S(1)}, u32[]{:S(2)}, u32[]{:S(2)}) collective-permute-start(f32[72,128]{1,0:T(8,128)S(1)} %get-tuple-element.25), channel_id=1, source_target_pairs={{0,2},{1,3},{2,0},{3,1},{4,6},{5,7},{6,4},{7,5},{8,10},{9,11},{10,... | collective-permute-start | bytes 110600 | tf_op jit(solution)/shard_map/ppermute | solution.py:259
  22.5 1.3 %collective-permute-start.6 = (f32[4,40,128]{2,1,0:T(8,128)S(1)}, f32[4,40,128]{2,1,0:T(8,128)S(1)}, u32[]{:S(2)}, u32[]{:S(2)}) collective-permute-start(f32[4,40,128]{2,1,0:T(8,128)S(1)} %pad_maximum_fusion), channel_id=1, source_target_pairs={{0,1},{1,0},{2,3},{3,2},{4,5},{5,4},{6,7},{7,6},{8,9},{9,8},{10,11... | collective-permute-start | bytes 245768 | tf_op jit(solution)/shard_map/ppermute | solution.py:259

commit v10 on v8

--- a/solution.py
+++ b/solution.py
@@ -310,7 +310,7 @@
 
     if two_step:
         arrived = [out[0]]
-        for k in (1, 2, 3):
+        for k in (2, 1, 3):
             arrived.append(moved(out[k], "wide", nwide, lambda i: i ^ (2 * k + (k in CROSS))))
         mate = jnp.stack([x[32:] for x in arrived])
         mate = moved(mate, "wide", nwide, lambda i: i ^ 1)

time: 25.9 us -> 25.8 us (level)
  no operation moved by 1% of the time
where the time goes in v10:
time: 25.8 us; the launch traced here: 25.7 us
  starting transfers between devices  11.6 us (45%)
  Pallas kernels  7.65 us (30%)
  waiting for transfers between devices  6.31 us (24%)
    ppermute x7, starting transfers between devices, moved(): return lax.ppermute(x, axis, [(i, to(i)) for i in range(n)])  11.6 us
    ppermute x7, waiting for transfers between devices, moved(): return lax.ppermute(x, axis, [(i, to(i)) for i in range(n)])  6.31 us
    pallas_call x1, Pallas kernels, on_device(): pl.pallas_call(prepare, out_shape=(ct, tr), in_specs=[ANY, ANY], out_spec...  3.47 us
    pallas_call x1, Pallas kernels, on_device(): pl.pallas_call(functools.partial(downward, kinds), out_shape=shape((RHS,...  1.85 us
    pallas_call x1, Pallas kernels, on_device(): pl.pallas_call(functools.partial(pick, two_step), out_shape=(shape((nbloc...  1.1 us
    pallas_call x1, Pallas kernels, on_device(): pl.pallas_call(functools.partial(couple, two_step, len(picked)), out_shap...  0.82 us
  transfers between devices with their start and end apart: 7, of which 7 were waited for; matrix products, arithmetic and copies ran while one was open for 0% of the time, Pallas kernels for 19%

profile of v10, /device:TPU:0, one launch (start us, length us, event | category | flops | bytes accessed | tf_op | source)
XLA Modules:
  0.0 25.7 jit_solution(17579417978978117154)
XLA Ops:
  0.0 5.0 %collective-permute-start = (f32[73,512]{1,0:T(8,128)}, f32[73,512]{1,0:T(8,128)S(1)}, u32[]{:S(2)}, u32[]{:S(2)}) collective-permute-start(f32[73,512]{1,0:T(8,128)} %own.1), channel_id=1, source_target_pairs={{0,24},{8,16},{16,8},{24,0},{1,25},{9,17},{17,9},{25,1},{2,26},{10... | collective-permute-start | bytes 448520 | tf_op jit(solution)/shard_map/ppermute | solution.py:259
  5.0 0.0 collective-permute-start.1
  5.1 0.0 copy-start.1
  5.1 0.0 copy-start.2
  5.1 0.0 copy-start.3
  5.1 0.0 copy-start.4
  5.1 3.5 %prepare.1 = (bf16[8,256,256]{2,1,0:T(8,128)(2,1)S(1)}, bf16[576,1024]{1,0:T(8,128)(2,1)S(1)}) custom-call(f32[64,64,64]{2,1,0:T(8,128)} %coupling_in.1, f32[64,64,72]{2,1,0:T(8,128)} %bitcast.27), custom_call_target="tpu_custom_call" | custom-call | bytes 10485760 | tf_op jit(solution)/shard_map/prepare/pallas_call | solution.py:242
  8.6 0.0 copy-start
  8.6 0.3 %collective-permute-done.1 = s32[64]{0:T(128)S(1)} collective-permute-done((s32[64]{0:T(128)}, s32[64]{0:T(128)S(1)}, u32[]{:S(2)}, u32[]{:S(2)}) %collective-permute-start.1) | collective-permute-done | bytes 288 | tf_op jit(solution)/shard_map/ppermute | solution.py:259
  8.9 0.0 copy-done.1
  8.9 0.2 relay_own.1
  9.1 0.5 %collective-permute-done.refs_1_.far = f32[73,512]{1,0:T(8,128)S(1)} collective-permute-done((f32[73,512]{1,0:T(8,128)}, f32[73,512]{1,0:T(8,128)S(1)}, u32[]{:S(2)}, u32[]{:S(2)}) %collective-permute-start) | collective-permute-done | bytes 149536 | tf_op jit(solution)/shard_map/ppermute | solution.py:259
  9.6 0.2 relay.1
  9.8 3.2 %collective-permute-start.2 = (f32[64,512]{1,0:T(8,128)S(1)}, f32[64,512]{1,0:T(8,128)S(1)}, u32[]{:S(2)}, u32[]{:S(2)}) collective-permute-start(f32[64,512]{1,0:T(8,128)S(1)} %relay.1), channel_id=1, source_target_pairs={{0,8},{8,0},{16,24},{24,16},{1,9},{9,1},{17,25},{25,17},{2,10},{10... | collective-permute-start | bytes 393224 | tf_op jit(solution)/shard_map/ppermute | solution.py:259
  12.9 0.0 copy-done.2
  12.9 0.0 copy-done.3
  12.9 0.0 copy-done.4
  12.9 1.1 %pick.1 = (f32[64,512]{1,0:T(8,128)S(1)}, f32[8,8,128]{2,1,0:T(8,128)S(1)}) custom-call(s32[64]{0:T(128)S(1)} %copy-done.2, s32[64]{0:T(128)S(1)} %copy-done.3, s32[8]{0:T(128)S(1)} %copy-done.4, f32[73,512]{1,0:T(8,128)S(1)} %copy-done.1, f32[73,512]{1,0:T(8,128)S(1)} %collective-permute-done.refs_1_.far), custom_call_target="tpu_custom_call" | custom-call | tf_op jit(solution)/shard_map/pick/pallas_call | solution.py:289
  14.1 1.8 %collective-permute-done.2.refs_1_ = f32[64,512]{1,0:T(8,128)S(1)} collective-permute-done((f32[64,512]{1,0:T(8,128)S(1)}, f32[64,512]{1,0:T(8,128)S(1)}, u32[]{:S(2)}, u32[]{:S(2)}) %collective-permute-start.2) | collective-permute-done | bytes 131104 | tf_op jit(solution)/shard_map/ppermute | solution.py:259
  15.9 0.8 %couple.1 = f32[4,72,128]{2,1,0:T(8,128)S(1)} custom-call(f32[64,512]{1,0:T(8,128)S(1)} %get-tuple-element.15.refs_0_, f32[64,512]{1,0:T(8,128)S(1)} %collective-permute-done.2.refs_1_, bf16[8,256,256]{2,1,0:T(8,128)(2,1)S(1)} %get-tuple-element.18.refs_2_, f32[8,8,128]{2,1,0:T(8,128)S(1)} %get-tuple-element.19.refs_3_), custom_call_target="tpu_custom_call" | custom-call | tf_op jit(solution)/shard_map/couple/pallas_call | solution.py:301
  16.7 0.4 %collective-permute-start.5 = (f32[72,128]{1,0:T(8,128)S(1)}, f32[72,128]{1,0:T(8,128)S(1)}, u32[]{:S(2)}, u32[]{:S(2)}) collective-permute-start(f32[72,128]{1,0:T(8,128)S(1)} %get-tuple-element.21), channel_id=1, source_target_pairs={{0,7},{1,6},{2,5},{3,4},{4,3},{5,2},{6,1},{7,0},{8,15},{9,14},{10,... | collective-permute-start | bytes 110600 | tf_op jit(solution)/shard_map/ppermute | solution.py:259
  17.1 1.2 %collective-permute-start.4 = (f32[72,128]{1,0:T(8,128)S(1)}, f32[72,128]{1,0:T(8,128)S(1)}, u32[]{:S(2)}, u32[]{:S(2)}) collective-permute-start(f32[72,128]{1,0:T(8,128)S(1)} %get-tuple-element.22), channel_id=1, source_target_pairs={{0,2},{1,3},{2,0},{3,1},{4,6},{5,7},{6,4},{7,5},{8,10},{9,11},{10,... | collective-permute-start | bytes 110600 | tf_op jit(solution)/shard_map/ppermute | solution.py:259
  18.4 1.5 %collective-permute-start.3 = (f32[72,128]{1,0:T(8,128)S(1)}, f32[72,128]{1,0:T(8,128)S(1)}, u32[]{:S(2)}, u32[]{:S(2)}) collective-permute-start(f32[72,128]{1,0:T(8,128)S(1)} %get-tuple-element.23), channel_id=1, source_target_pairs={{0,4},{1,5},{2,6},{3,7},{4,0},{5,1},{6,2},{7,3},{8,12},{9,13},{10,... | collective-permute-start | bytes 110600 | tf_op jit(solution)/shard_map/ppermute | solution.py:259
  19.9 1.5 %collective-permute-done.5.refs_3_ = f32[72,128]{1,0:T(8,128)S(1)} collective-permute-done((f32[72,128]{1,0:T(8,128)S(1)}, f32[72,128]{1,0:T(8,128)S(1)}, u32[]{:S(2)}, u32[]{:S(2)}) %collective-permute-start.5) | collective-permute-done | bytes 36896 | tf_op jit(solution)/shard_map/ppermute | solution.py:259
  21.4 0.1 collective-permute-done.4.refs_2_
  21.4 1.0 %collective-permute-done.3.refs_1_ = f32[72,128]{1,0:T(8,128)S(1)} collective-permute-done((f32[72,128]{1,0:T(8,128)S(1)}, f32[72,128]{1,0:T(8,128)S(1)}, u32[]{:S(2)}, u32[]{:S(2)}) %collective-permute-start.3) | collective-permute-done | bytes 36896 | tf_op jit(solution)/shard_map/ppermute | solution.py:259
  22.5 0.2 collective-permute-start.6
  22.7 1.2 %collective-permute-done.6 = f32[4,40,128]{2,1,0:T(8,128)S(1)} collective-permute-done((f32[4,40,128]{2,1,0:T(8,128)S(1)}, f32[4,40,128]{2,1,0:T(8,128)S(1)}, u32[]{:S(2)}, u32[]{:S(2)}) %collective-permute-start.6) | collective-permute-done | bytes 81952 | tf_op jit(solution)/shard_map/ppermute | solution.py:259
  23.8 0.0 copy-done
  23.8 1.8 %downward.1 = f32[8,8192]{1,0:T(8,128)} custom-call(f32[72,128]{1,0:T(8,128)S(1)} %get-tuple-element.24.refs_0_, f32[72,128]{1,0:T(8,128)S(1)} %collective-permute-done.3.refs_1_, f32[72,128]{1,0:T(8,128)S(1)} %collective-permute-done.4.refs_2_, f32[72,128]{1,0:T(8,128)S(1)} %collective-permute-done.5.refs_3_, f32[40,128]{1,0:T(8,128)S(1)} %get-tuple-element.28.refs_4_, ...), custom_call_target="tpu_custom_call" | custom-call | tf_op jit(solution)/shard_map/downward/pallas_call | solution.py:328
  (7 shorter events, 0.0 us)
Async XLA Ops:
  0.0 9.6 %collective-permute-start = (f32[73,512]{1,0:T(8,128)}, f32[73,512]{1,0:T(8,128)S(1)}, u32[]{:S(2)}, u32[]{:S(2)}) collective-permute-start(f32[73,512]{1,0:T(8,128)} %own.1), channel_id=1, source_target_pairs={{0,24},{8,16},{16,8},{24,0},{1,25},{9,17},{17,9},{25,1},{2,26},{10... | collective-permute-start | bytes 448520 | tf_op jit(solution)/shard_map/ppermute | solution.py:259
  5.0 3.8 %collective-permute-start.1 = (s32[64]{0:T(128)}, s32[64]{0:T(128)S(1)}, u32[]{:S(2)}, u32[]{:S(2)}) collective-permute-start(s32[64]{0:T(128)} %source.1), channel_id=1, source_target_pairs={{0,8},{8,0},{16,24},{24,16},{1,9},{9,1},{17,25},{25,17},{2,10},{10... | collective-permute-start | bytes 776 | tf_op jit(solution)/shard_map/ppermute | solution.py:259
  5.1 3.8 %copy-start.1 = (f32[73,512]{1,0:T(8,128)S(1)}, f32[73,512]{1,0:T(8,128)}, u32[]{:S(2)}) copy-start(f32[73,512]{1,0:T(8,128)} %own.1) | copy-start | bytes 448516
  5.1 7.9 %copy-start.2 = (s32[64]{0:T(128)S(1)}, s32[64]{0:T(128)}, u32[]{:S(2)}) copy-start(s32[64]{0:T(128)} %source.1) | copy-start | bytes 772
  5.1 7.9 %copy-start.3 = (s32[64]{0:T(128)S(1)}, s32[64]{0:T(128)}, u32[]{:S(2)}) copy-start(s32[64]{0:T(128)} %target.1) | copy-start | bytes 772
  5.1 7.9 %copy-start.4 = (s32[8]{0:T(128)S(1)}, s32[8]{0:T(128)}, u32[]{:S(2)}) copy-start(s32[8]{0:T(128)} %counts.1) | copy-start | bytes 100
  8.6 15.3 %copy-start = (f32[64,64,128]{2,1,0:T(8,128)S(1)}, f32[64,64,128]{2,1,0:T(8,128)}, u32[]{:S(2)}) copy-start(f32[64,64,128]{2,1,0:T(8,128)} %param.13) | copy-start | bytes 6291460
  9.8 6.1 %collective-permute-start.2 = (f32[64,512]{1,0:T(8,128)S(1)}, f32[64,512]{1,0:T(8,128)S(1)}, u32[]{:S(2)}, u32[]{:S(2)}) collective-permute-start(f32[64,512]{1,0:T(8,128)S(1)} %relay.1), channel_id=1, source_target_pairs={{0,8},{8,0},{16,24},{24,16},{1,9},{9,1},{17,25},{25,17},{2,10},{10... | collective-permute-start | bytes 393224 | tf_op jit(solution)/shard_map/ppermute | solution.py:259
  16.7 4.6 %collective-permute-start.5 = (f32[72,128]{1,0:T(8,128)S(1)}, f32[72,128]{1,0:T(8,128)S(1)}, u32[]{:S(2)}, u32[]{:S(2)}) collective-permute-start(f32[72,128]{1,0:T(8,128)S(1)} %get-tuple-element.21), channel_id=1, source_target_pairs={{0,7},{1,6},{2,5},{3,4},{4,3},{5,2},{6,1},{7,0},{8,15},{9,14},{10,... | collective-permute-start | bytes 110600 | tf_op jit(solution)/shard_map/ppermute | solution.py:259
  17.1 4.3 %collective-permute-start.4 = (f32[72,128]{1,0:T(8,128)S(1)}, f32[72,128]{1,0:T(8,128)S(1)}, u32[]{:S(2)}, u32[]{:S(2)}) collective-permute-start(f32[72,128]{1,0:T(8,128)S(1)} %get-tuple-element.22), channel_id=1, source_target_pairs={{0,2},{1,3},{2,0},{3,1},{4,6},{5,7},{6,4},{7,5},{8,10},{9,11},{10,... | collective-permute-start | bytes 110600 | tf_op jit(solution)/shard_map/ppermute | solution.py:259
  18.4 4.1 %collective-permute-start.3 = (f32[72,128]{1,0:T(8,128)S(1)}, f32[72,128]{1,0:T(8,128)S(1)}, u32[]{:S(2)}, u32[]{:S(2)}) collective-permute-start(f32[72,128]{1,0:T(8,128)S(1)} %get-tuple-element.23), channel_id=1, source_target_pairs={{0,4},{1,5},{2,6},{3,7},{4,0},{5,1},{6,2},{7,3},{8,12},{9,13},{10,... | collective-permute-start | bytes 110600 | tf_op jit(solution)/shard_map/ppermute | solution.py:259
  22.5 1.3 %collective-permute-start.6 = (f32[4,40,128]{2,1,0:T(8,128)S(1)}, f32[4,40,128]{2,1,0:T(8,128)S(1)}, u32[]{:S(2)}, u32[]{:S(2)}) collective-permute-start(f32[4,40,128]{2,1,0:T(8,128)S(1)} %pad_maximum_fusion), channel_id=1, source_target_pairs={{0,1},{1,0},{2,3},{3,2},{4,5},{5,4},{6,7},{7,6},{8,9},{9,8},{10,11... | collective-permute-start | bytes 245768 | tf_op jit(solution)/shard_map/ppermute | solution.py:259
